TPU v7x, 128 devices: a whole 4x4x4 slice. The times are simulated.
128 devices in a mesh: gx: 8 (over x, core), gy: 16 (over z, y).
Axes of the slice: x: 4, y: 4, z: 4, core: 2. Of those that a mesh axis runs over, the one named last changes fastest.
Arguments:
- estimate: float32 [2, 1024, 2048], P(None, 'gx', 'gy'), may hold values from 0.24 to 5.3
- views: bfloat16 [4, 2, 1024, 2048], P(None, None, 'gx', 'gy'), may hold values from 0.18 to 7
- psf_rows: float32 [4, 31], replicated, may hold values from 0.05 to 1
- psf_cols: float32 [4, 31], replicated, may hold values from 0.05 to 1
- shifts: int32 [4, 128], P(None, 'gx'), may hold values from 0 to 15, as said below
- codes: int32 [4, 128, 16], P(None, 'gx', 'gy'), may hold values from 0 to 15
Outputs:
- updated: float32 [2, 1024, 2048], P(None, 'gx', 'gy')
Inputs may be any that keep to these rules, and one draw needn't show every extreme that they name: `shifts`: within each view and each group of 16 consecutive block rows that starts at a multiple of 16, no displacement occurs more than 2 times, and one occurs exactly 2 times.
All inputs are finite; a program needn't handle non-finite values.
Results may differ from a plain program's by a relative error of at most 0.0003.
Values sent between devices are 32-bit elements; how exact they have to be, the bound alone decides.
No kernel may reach another device: no remote copies, remote signals or barrier semaphores. Data moves between devices by JAX's collectives and lax.ppermute only.
A program may use at most 64 MiB of HBM per device.

v0:
```python
import functools

import jax
import jax.numpy as jnp
import numpy as np
from jax import lax
from jax.experimental import pallas as pl
from jax.experimental.pallas import tpu as pltpu
from jax.sharding import PartitionSpec as P

ITERS = 2
V = 4
Z = 2
T = 128
ROWS = 16
GY = 16
GX = 8
CHUNKS = 64
META = 16
UNIT = ROWS * (1 + V) + 8
PERM = (0, 1, 2, 3, 7, 6, 5, 4)
SNAKE = PERM + tuple(8 + p for p in PERM)
AXES = ("gx", "gy")
F32 = jnp.float32
BF16 = jnp.bfloat16
VMEM = pl.BlockSpec(memory_space=pltpu.VMEM)
SMEM = pl.BlockSpec(memory_space=pltpu.SMEM)
PARAMS = pltpu.CompilerParams(vmem_limit_bytes=48 * 1024 * 1024)


def device_of(core, chunk):
    place = (chunk % 16 + 8 * core) % 16
    return (2 * (chunk // 16) + core) * GY + SNAKE.index(place)


FORWARD = [
    (device_of(c, q), device_of(c, (q + 1) % CHUNKS)) for c in range(2) for q in range(CHUNKS)
]
BACKWARD = [(b, a) for a, b in FORWARD]
SWAP = [((2 * x + c) * GY + g, (2 * x + 1 - c) * GY + g)
        for x in range(GX // 2) for c in range(2) for g in range(GY)]


def split(x):
    hi = x.astype(BF16)
    return hi, (x - hi.astype(F32)).astype(BF16)


def pack_kernel(core_ref, codes_ref, shifts_ref, est_ref, views_ref, keep_ref, send_ref):
    core = core_ref[0]
    lane = lax.broadcasted_iota(jnp.int32, (8, T), 1)
    for slot in range(8):
        chunk = PERM[slot]
        rows = pl.ds(chunk * ROWS, ROWS)
        meta = jnp.zeros((8, T), F32)
        for half in range(2):
            for v in range(V):
                code = codes_ref[v, 2 * chunk + half].astype(F32)
                shift = shifts_ref[v, 2 * chunk + half].astype(F32)
                meta = jnp.where(lane == half * V + v, code, meta)
                meta = jnp.where(lane == 8 + half * V + v, shift, meta)
        for ref, plane in ((keep_ref, core), (send_ref, 1 - core)):
            ref[slot, 0:ROWS, :] = est_ref[plane, rows, :]
            for v in range(V):
                ref[slot, pl.ds(ROWS * (1 + v), ROWS), :] = views_ref[v, plane, rows, :].astype(F32)
            ref[slot, pl.ds(ROWS * (1 + V), 8), :] = meta


def taps_kernel(cols_ref, rows_ref, band_ref, row_ref, back_ref):
    for v in range(V):
        for d in range(2):
            base = jnp.broadcast_to(cols_ref[2 * v + d : 2 * v + d + 1, :], (2 * T, 2 * T))
            turned = pltpu.roll(base, 0, 1, stride=1, stride_axis=0)[:, :T]
            hi, lo = split(turned)
            band_ref[v, d, 0 : 2 * T, :] = hi
            band_ref[v, d, 2 * T : 4 * T, :] = lo
            band_ref[v, d, 4 * T : 6 * T, :] = hi
        base = jnp.broadcast_to(rows_ref[2 * v : 2 * v + 1, :], (ROWS, T))
        hi, lo = split(pltpu.roll(base, 0, 1, stride=1, stride_axis=0)[:, : 3 * ROWS])
        row_ref[v] = jnp.concatenate([hi, hi, lo], axis=1)
        base = jnp.broadcast_to(rows_ref[2 * v + 1 : 2 * v + 2, :], (3 * ROWS, T))
        hi, lo = split(pltpu.roll(base, 0, 1, stride=1, stride_axis=0)[:, :ROWS])
        back_ref[v] = jnp.concatenate([hi, hi, lo], axis=1)


def column_pass(pieces, band):
    lane = lax.broadcasted_iota(jnp.int32, (ROWS, T), 1)
    turned = [pltpu.roll(p, T // 2, 1) for p in pieces]
    zero = jnp.zeros((ROWS, T), F32)
    turned = [zero] + turned + [zero]
    moved = [
        jnp.where(lane < T // 2, turned[j], turned[j + 1]) for j in range(len(pieces) + 1)
    ]
    his, los = zip(*[split(m) for m in moved])
    left = len(pieces)

    def windows(parts):
        return jnp.concatenate(
            [jnp.concatenate([parts[c], parts[c + 1]], axis=1) for c in range(left)], axis=0
        )

    hi, lo = windows(his), windows(los)
    return jnp.dot(
        jnp.concatenate([hi, hi, lo], axis=1), band, preferred_element_type=F32
    )


def step_kernel(
    meta_ref, flag_ref, before_ref, own_ref, after_ref, arrived_ref, band_ref, row_ref, back_ref,
    low_ref, mid_ref, high_ref, est2, slope2, view_u, total2,
):
    lane = lax.broadcasted_iota(jnp.int32, (GY, 8, T), 2)
    inner = jnp.where(lane < T - 1, 1.0 / 16.0, 0.0).astype(F32)
    for src, ref in enumerate((before_ref, own_ref, after_ref)):
        for half in range(2):
            b = 2 * src + half
            x = ref[0 : GY * ROWS, :].reshape(GY, ROWS, T)[:, 8 * half : 8 * half + 8, :]
            if src != 1:
                x = x * flag_ref[src // 2]
            d = (pltpu.roll(x, T - 1, 2) - x) * inner
            est2[b, 0:GY] = x
            est2[b, GY : 2 * GY] = x
            slope2[b, 0:GY] = d
            slope2[b, GY : 2 * GY] = d
    total2[...] = jnp.zeros(total2.shape, F32)
    inner8 = inner[0]
    for v in range(V):
        for src in range(3):
            parts = []
            for half in range(2):
                b = 2 * src + half
                shift = meta_ref[src * GY, 8 + half * V + v]
                x = est2[b, pl.ds(shift, GY)]
                d = slope2[b, pl.ds(shift, GY)]
                parts.append([
                    x[c] + meta_ref[src * GY + c, half * V + v].astype(F32) * d[c]
                    for c in range(GY)
                ])
            for c in range(GY):
                hi, lo = split(jnp.concatenate([parts[0][c], parts[1][c]], axis=0))
                cols = slice(T * c, T * c + T)
                view_u[v, ROWS * src : ROWS * src + ROWS, cols] = hi
                view_u[v, ROWS * (3 + src) : ROWS * (4 + src), cols] = lo
                view_u[v, ROWS * (6 + src) : ROWS * (7 + src), cols] = hi
        smooth = jnp.dot(row_ref[v], view_u[v], preferred_element_type=F32)
        blurred = column_pass([smooth[:, T * c : T * c + T] for c in range(GY)], band_ref[v, 0])
        ratio = [
            arrived_ref[c, ROWS * (1 + v) : ROWS * (2 + v), :]
            / blurred[ROWS * c : ROWS * c + ROWS, :]
            for c in range(GY)
        ]
        again = column_pass(ratio, band_ref[v, 1])
        his, los = zip(*[split(again[ROWS * c : ROWS * c + ROWS, :]) for c in range(GY)])
        hi, lo = jnp.concatenate(his, axis=1), jnp.concatenate(los, axis=1)
        spread = jnp.dot(
            back_ref[v], jnp.concatenate([hi, lo, hi], axis=0), preferred_element_type=F32
        )
        for b in range(6):
            src, half = b // 2, b % 2
            shift = meta_ref[src * GY, 8 + half * V + v]
            parts = []
            for c in range(GY):
                r = spread[8 * b : 8 * b + 8, T * c : T * c + T]
                g = r * inner8
                g = pltpu.roll(g, 1, 1) - g
                parts.append(r + meta_ref[src * GY + c, half * V + v].astype(F32) * g)
            total2[b, pl.ds(shift, GY)] += jnp.stack(parts)
    for src, ref in enumerate((low_ref, mid_ref, high_ref)):
        for half in range(2):
            b = 2 * src + half
            y = total2[b, 0:GY] + total2[b, GY : 2 * GY]
            for c in range(GY):
                ref[ROWS * c + 8 * half : ROWS * c + 8 * half + 8, :] = y[c]


def place(base, width, taps, at):
    left = at
    return jnp.pad(taps, ((0, 0), (left, width - left - taps.shape[1])))


def body(estimate, views, psf_rows, psf_cols, shifts, codes):
    core = lax.axis_index("gx") % 2
    group = lax.axis_index("gx") // 2
    gy = lax.axis_index("gy")
    within = gy % 4 + 4 * (gy // 4)
    within = jnp.where((gy // 4) % 2 == 0, within, 4 * (gy // 4) + 3 - gy % 4)
    chunk = group * 16 + (within + 8 * core) % 16
    flags = jnp.stack([chunk > 0, chunk < CHUNKS - 1]).astype(F32)

    unit = jax.ShapeDtypeStruct((8, UNIT, T), F32)
    keep, send = pl.pallas_call(
        pack_kernel,
        out_shape=(unit, unit),
        in_specs=[SMEM, SMEM, SMEM, VMEM, VMEM],
        out_specs=(VMEM, VMEM),
        compiler_params=PARAMS,
        name="pack",
    )(core.reshape(1), codes[:, :, 0], shifts, estimate, views)
    other = lax.ppermute(send, AXES, SWAP)

    rows_n = psf_rows / jnp.sum(psf_rows, axis=1, keepdims=True)
    cols_n = psf_cols / jnp.sum(psf_cols, axis=1, keepdims=True)
    col_base = jnp.stack(
        [place(None, 2 * T, cols_n[:, ::-1], 177), place(None, 2 * T, cols_n, 177)], axis=1
    ).reshape(2 * V, 2 * T)
    row_base = jnp.stack(
        [place(None, T, rows_n, 1), place(None, T, rows_n[:, ::-1], T - 31)], axis=1
    ).reshape(2 * V, T)
    band, row_mat, back_mat = pl.pallas_call(
        taps_kernel,
        out_shape=(
            jax.ShapeDtypeStruct((V, 2, 6 * T, T), BF16),
            jax.ShapeDtypeStruct((V, ROWS, 9 * ROWS), BF16),
            jax.ShapeDtypeStruct((V, 3 * ROWS, 3 * ROWS), BF16),
        ),
        in_specs=[VMEM, VMEM],
        out_specs=(VMEM, VMEM, VMEM),
        compiler_params=PARAMS,
        name="taps",
    )(col_base, row_base)

    arrived = lax.all_to_all(
        jnp.concatenate([keep, other], axis=0), "gy", split_axis=0, concat_axis=0, tiled=True
    )
    own = arrived[:, :ROWS, :].reshape(GY * ROWS, T)
    own_meta = arrived[:, ROWS * (1 + V), :]
    meta = None
    step = pl.pallas_call(
        step_kernel,
        out_shape=(jax.ShapeDtypeStruct((GY * ROWS, T), F32),) * 3,
        in_specs=[SMEM, SMEM] + [VMEM] * 7,
        out_specs=(VMEM,) * 3,
        scratch_shapes=[
            pltpu.VMEM((6, 2 * GY, 8, T), F32),
            pltpu.VMEM((6, 2 * GY, 8, T), F32),
            pltpu.VMEM((V, 9 * ROWS, GY * T), BF16),
            pltpu.VMEM((6, 2 * GY, 8, T), F32),
        ],
        compiler_params=PARAMS,
        name="step",
    )
    for sweep in range(ITERS):
        out = jnp.concatenate([own, own_meta], axis=0) if sweep == 0 else own
        before = lax.ppermute(out, AXES, FORWARD)
        after = lax.ppermute(out, AXES, BACKWARD)
        if sweep == 0:
            meta = jnp.concatenate(
                [before[GY * ROWS :, :META], own_meta[:, :META], after[GY * ROWS :, :META]], axis=0
            ).astype(jnp.int32)
        low, mid, high = step(meta, flags, before, own, after, arrived, band, row_mat, back_mat)
        from_after = lax.ppermute(low, AXES, BACKWARD)
        from_before = lax.ppermute(high, AXES, FORWARD)
        own = own * ((mid + from_before * flags[0] + from_after * flags[1]) * 0.25)
    home = lax.all_to_all(
        own.reshape(GY, ROWS, T), "gy", split_axis=0, concat_axis=0, tiled=True
    )
    mine, theirs = home[:8], home[8:]
    got = lax.ppermute(theirs, AXES, SWAP)

    def ordered(part):
        return jnp.concatenate([part[PERM.index(q)] for q in range(8)], axis=0)

    mine, got = ordered(mine), ordered(got)
    return jnp.where(core == 0, jnp.stack([mine, got]), jnp.stack([got, mine]))


def solution(mesh):
    placed = (
        P(None, "gx", "gy"),
        P(None, None, "gx", "gy"),
        P(),
        P(),
        P(None, "gx"),
        P(None, "gx", "gy"),
    )
    return jax.shard_map(
        body, mesh=mesh, in_specs=placed, out_specs=P(None, "gx", "gy"), check_vma=False
    )
```

profile of v0, /device:TPU:1, one launch (start us, length us, event | category | flops | bytes accessed | tf_op | source)
XLA Modules:
  0.0 90.2 jit_solution(16052468731118955417)
XLA Ops:
  0.0 0.0 copy-start
  0.0 0.9 %copy-done = bf16[4,2,128,128]{3,2,1,0:T(8,128)(2,1)S(1)} copy-done((bf16[4,2,128,128]{3,2,1,0:T(8,128)(2,1)S(1)}, bf16[4,2,128,128]{3,2,1,0:T(8,128)(2,1)}, u32[]{:S(2)}) %copy-start) | copy-done | bytes 262168
  1.0 0.0 copy-start.1
  1.0 0.9 copy-done.1
  1.9 0.0 copy-start.2
  1.9 0.7 copy-done.2
  2.5 0.0 copy-start.3
  2.5 0.7 copy-done.3
  3.2 0.0 copy-start.4
  3.2 0.0 copy-start.5
  3.2 0.7 pack.1
  3.9 1.5 %collective-permute-start = (f32[8,88,128]{2,1,0:T(8,128)S(1)}, f32[8,88,128]{2,1,0:T(8,128)S(1)}, u32[]{:S(2)}, u32[]{:S(2)}) collective-permute-start(f32[8,88,128]{2,1,0:T(8,128)S(1)} %get-tuple-element.17), channel_id=1, source_target_pairs={{0,16},{1,17},{2,18},{3,19},{4,20},{5,21},{6,22},{7,23},{8,24},{9,... | collective-permute-start | bytes 1081352 | tf_op jit(solution)/shard_map/ppermute | solution.py:199
  5.4 0.8 reduce_sum.18
  6.2 0.5 collective-permute-done
  6.7 0.9 %pad_maximum_fusion = f32[16,88,128]{2,1,0:T(8,128)} fusion(f32[8,88,128]{2,1,0:T(8,128)S(1)} %collective-permute-done, f32[8,88,128]{2,1,0:T(8,128)S(1)} %get-tuple-element.16), kind=kLoop, calls=%fused_computation | loop fusion | flops 180224 | bytes 1441792 | tf_op jit(solution)/shard_map/concatenate | solution.py:223
  7.6 7.9 %all-to-all-start = ((f32[16,88,128]{2,1,0:T(8,128)}), f32[16,88,128]{2,1,0:T(8,128)S(1)}, u32[]{:S(2)}, u32[]{:S(2)}) async-start(f32[16,88,128]{2,1,0:T(8,128)} %pad_maximum_fusion), calls=%async_computation | async-start | bytes 1441792 | tf_op jit(solution)/shard_map/all_to_all | solution.py:222
  15.5 0.0 copy-done.4
  15.5 0.1 broadcast_divide_fusion.1
  15.6 0.1 rev.6
  15.7 0.0 copy-done.5
  15.7 0.1 reduce_sum.19
  15.8 0.1 broadcast_divide_fusion
  15.9 0.1 rev.7
  16.0 0.1 pad_bitcast_fusion.2
  16.0 0.1 pad_bitcast_fusion
  16.1 12.2 %all-to-all-done.arrived_ref = f32[16,88,128]{2,1,0:T(8,128)S(1)} async-done(((f32[16,88,128]{2,1,0:T(8,128)}), f32[16,88,128]{2,1,0:T(8,128)S(1)}, u32[]{:S(2)}, u32[]{:S(2)}) %all-to-all-start) | async-done | bytes 720928 | tf_op jit(solution)/shard_map/all_to_all | solution.py:222
  28.4 0.4 collective-permute-start.1
  28.7 2.4 %collective-permute-start.2 = (f32[272,128]{1,0:T(8,128)S(1)}, f32[272,128]{1,0:T(8,128)S(1)}, u32[]{:S(2)}, u32[]{:S(2)}) collective-permute-start(f32[272,128]{1,0:T(8,128)S(1)} %pad_maximum_fusion.1), channel_id=1, source_target_pairs={{1,0},{2,1},{3,2},{7,3},{6,7},{5,6},{4,5},{8,4},{9,8},{10,9},{11,1... | collective-permute-start | bytes 417800 | tf_op jit(solution)/shard_map/ppermute | solution.py:245
  31.1 0.8 taps.1
  32.0 0.1 add_convert_fusion.flag_ref
  32.0 1.5 %collective-permute-done.1.before_ref = f32[272,128]{1,0:T(8,128)S(1)} collective-permute-done((f32[272,128]{1,0:T(8,128)S(1)}, f32[272,128]{1,0:T(8,128)S(1)}, u32[]{:S(2)}, u32[]{:S(2)}) %collective-permute-start.1) | collective-permute-done | bytes 139296 | tf_op jit(solution)/shard_map/ppermute | solution.py:244
  33.5 0.0 collective-permute-done.2.after_ref
  33.6 4.8 %step.2 = (f32[256,128]{1,0:T(8,128)S(1)}, f32[256,128]{1,0:T(8,128)S(1)}, f32[256,128]{1,0:T(8,128)S(1)}) custom-call(s32[48,16]{1,0:T(8,128)S(1)} %maximum_convert_fusion.meta_ref, f32[2]{0:T(128)S(1)} %add_convert_fusion.flag_ref, f32[272,128]{1,0:T(8,128)S(1)} %collective-permute-done.1.before_ref, f32[256,128]{1,0:T(8,128)S(1)} %bitcast.87, ...), custom_call_target="tpu_custom_call" | custom-call | tf_op jit(solution)/shard_map/step/pallas_call | solution.py:250
  38.4 0.7 collective-permute-start.3
  39.1 2.1 %collective-permute-start.4 = (f32[256,128]{1,0:T(8,128)S(1)}, f32[256,128]{1,0:T(8,128)S(1)}, u32[]{:S(2)}, u32[]{:S(2)}) collective-permute-start(f32[256,128]{1,0:T(8,128)S(1)} %get-tuple-element.23), channel_id=1, source_target_pairs={{1,0},{2,1},{3,2},{7,3},{6,7},{5,6},{4,5},{8,4},{9,8},{10,9},{11,1... | collective-permute-start | bytes 393224 | tf_op jit(solution)/shard_map/ppermute | solution.py:251
  41.2 0.6 fusion
  41.8 1.7 %collective-permute-done.3 = f32[256,128]{1,0:T(8,128)S(1)} collective-permute-done((f32[256,128]{1,0:T(8,128)S(1)}, f32[256,128]{1,0:T(8,128)S(1)}, u32[]{:S(2)}, u32[]{:S(2)}) %collective-permute-start.3) | collective-permute-done | bytes 131104 | tf_op jit(solution)/shard_map/ppermute | solution.py:252
  43.5 0.0 collective-permute-done.4
  43.5 1.3 %multiply_multiply_fusion.1.own_ref = f32[256,128]{1,0:T(8,128)S(1)} fusion(f32[256,128]{1,0:T(8,128)S(1)} %collective-permute-done.4, f32[256,128]{1,0:T(8,128)S(1)} %get-tuple-element.21, f32[256,128]{1,0:T(8,128)S(1)} %collective-permute-done.3, f32[]{:T(128)} %bitcast.12, f32[]{:T(128)} %bitcast.11, f32[16,16,128]{2,1,0:T(8,128)S(1)} %slice.107), kind=kLoop, calls=%fused_computation.4 | loop fusion | flops 196608 | bytes 655368 | tf_op jit(solution)/shard_map/mul | solution.py:253
  44.8 0.1 collective-permute-start.5
  44.8 2.8 %collective-permute-start.6 = (f32[256,128]{1,0:T(8,128)S(1)}, f32[256,128]{1,0:T(8,128)S(1)}, u32[]{:S(2)}, u32[]{:S(2)}) collective-permute-start(f32[256,128]{1,0:T(8,128)S(1)} %multiply_multiply_fusion.1.own_ref), channel_id=1, source_target_pairs={{1,0},{2,1},{3,2},{7,3},{6,7},{5,6},{4,5},{8,4},{9,8},{10,9},{11,1... | collective-permute-start | bytes 393224 | tf_op jit(solution)/shard_map/ppermute | solution.py:245
  47.7 3.7 %collective-permute-done.5.before_ref = f32[256,128]{1,0:T(8,128)S(1)} collective-permute-done((f32[256,128]{1,0:T(8,128)S(1)}, f32[256,128]{1,0:T(8,128)S(1)}, u32[]{:S(2)}, u32[]{:S(2)}) %collective-permute-start.5) | collective-permute-done | bytes 131104 | tf_op jit(solution)/shard_map/ppermute | solution.py:244
  51.3 0.0 collective-permute-done.6.after_ref
  51.4 4.8 %step.3 = (f32[256,128]{1,0:T(8,128)S(1)}, f32[256,128]{1,0:T(8,128)S(1)}, f32[256,128]{1,0:T(8,128)S(1)}) custom-call(s32[48,16]{1,0:T(8,128)S(1)} %maximum_convert_fusion.meta_ref, f32[2]{0:T(128)S(1)} %add_convert_fusion.flag_ref, f32[256,128]{1,0:T(8,128)S(1)} %collective-permute-done.5.before_ref, f32[256,128]{1,0:T(8,128)S(1)} %multiply_multiply_fusion.1.own_ref, ...), custom_call_target="tpu_custom_call" | custom-call | tf_op jit(solution)/shard_map/step/pallas_call | solution.py:250
  56.1 0.1 collective-permute-start.7
  56.2 2.7 %collective-permute-start.8 = (f32[256,128]{1,0:T(8,128)S(1)}, f32[256,128]{1,0:T(8,128)S(1)}, u32[]{:S(2)}, u32[]{:S(2)}) collective-permute-start(f32[256,128]{1,0:T(8,128)S(1)} %get-tuple-element.26), channel_id=1, source_target_pairs={{1,0},{2,1},{3,2},{7,3},{6,7},{5,6},{4,5},{8,4},{9,8},{10,9},{11,1... | collective-permute-start | bytes 393224 | tf_op jit(solution)/shard_map/ppermute | solution.py:251
  58.9 3.3 %collective-permute-done.7 = f32[256,128]{1,0:T(8,128)S(1)} collective-permute-done((f32[256,128]{1,0:T(8,128)S(1)}, f32[256,128]{1,0:T(8,128)S(1)}, u32[]{:S(2)}, u32[]{:S(2)}) %collective-permute-start.7) | collective-permute-done | bytes 131104 | tf_op jit(solution)/shard_map/ppermute | solution.py:252
  62.3 0.0 collective-permute-done.8
  62.3 1.9 %multiply_multiply_fusion = f32[256,128]{1,0:T(8,128)} fusion(f32[256,128]{1,0:T(8,128)S(1)} %multiply_multiply_fusion.1.own_ref, f32[256,128]{1,0:T(8,128)S(1)} %collective-permute-done.8, f32[256,128]{1,0:T(8,128)S(1)} %get-tuple-element.24, f32[256,128]{1,0:T(8,128)S(1)} %collective-permute-done.7, f32[]{:T(128)} %bitcast.12, f32[]{:T(128)} %bitcast.11), kind=kLoop, calls=%fused_computation.3 | loop fusion | flops 196608 | bytes 655368 | tf_op jit(solution)/shard_map/mul | solution.py:253
  64.2 3.6 %all-to-all-start.1 = ((f32[16,16,128]{2,1,0:T(8,128)}), f32[16,16,128]{2,1,0:T(8,128)S(1)}, u32[]{:S(2)}, u32[]{:S(2)}) async-start(f32[16,16,128]{2,1,0:T(8,128)} %bitcast.13), calls=%async_computation.1 | async-start | bytes 262144 | tf_op jit(solution)/shard_map/all_to_all | solution.py:254
  67.8 6.8 %all-to-all-done.1 = f32[16,16,128]{2,1,0:T(8,128)S(1)} async-done(((f32[16,16,128]{2,1,0:T(8,128)}), f32[16,16,128]{2,1,0:T(8,128)S(1)}, u32[]{:S(2)}, u32[]{:S(2)}) %all-to-all-start.1) | async-done | bytes 131104 | tf_op jit(solution)/shard_map/all_to_all | solution.py:254
  74.7 13.9 %collective-permute-start.9 = (f32[8,16,128]{2,1,0:T(8,128)S(1)}, f32[8,16,128]{2,1,0:T(8,128)S(1)}, u32[]{:S(2)}, u32[]{:S(2)}) collective-permute-start(f32[8,16,128]{2,1,0:T(8,128)S(1)} %slice.120), channel_id=1, source_target_pairs={{0,16},{1,17},{2,18},{3,19},{4,20},{5,21},{6,22},{7,23},{8,24},{9,... | collective-permute-start | bytes 196616 | tf_op jit(solution)/shard_map/ppermute | solution.py:258
  88.7 0.8 collective-permute-done.9
  89.6 0.7 maximum_select_fusion
  (28 shorter events, 0.1 us)
Async XLA Ops:
  0.0 0.9 %copy-start = (bf16[4,2,128,128]{3,2,1,0:T(8,128)(2,1)S(1)}, bf16[4,2,128,128]{3,2,1,0:T(8,128)(2,1)}, u32[]{:S(2)}) copy-start(bf16[4,2,128,128]{3,2,1,0:T(8,128)(2,1)} %views_ref.1) | copy-start | bytes 786436
  1.0 0.9 %copy-start.1 = (f32[2,128,128]{2,1,0:T(8,128)S(1)}, f32[2,128,128]{2,1,0:T(8,128)}, u32[]{:S(2)}) copy-start(f32[2,128,128]{2,1,0:T(8,128)} %est_ref.1) | copy-start | bytes 393220
  1.9 0.7 copy-start.2
  2.5 0.7 copy-start.3
  3.2 12.3 %copy-start.4 = (f32[4,31]{1,0:T(4,128)S(1)}, f32[4,31]{1,0:T(4,128)}, u32[]{:S(2)}) copy-start(f32[4,31]{1,0:T(4,128)} %param.9) | copy-start | bytes 1492
  3.2 12.4 %copy-start.5 = (f32[4,31]{1,0:T(4,128)S(1)}, f32[4,31]{1,0:T(4,128)}, u32[]{:S(2)}) copy-start(f32[4,31]{1,0:T(4,128)} %param.8) | copy-start | bytes 1492
  3.9 2.8 %collective-permute-start = (f32[8,88,128]{2,1,0:T(8,128)S(1)}, f32[8,88,128]{2,1,0:T(8,128)S(1)}, u32[]{:S(2)}, u32[]{:S(2)}) collective-permute-start(f32[8,88,128]{2,1,0:T(8,128)S(1)} %get-tuple-element.17), channel_id=1, source_target_pairs={{0,16},{1,17},{2,18},{3,19},{4,20},{5,21},{6,22},{7,23},{8,24},{9,... | collective-permute-start | bytes 1081352 | tf_op jit(solution)/shard_map/ppermute | solution.py:199
  7.6 20.7 %all-to-all-start = ((f32[16,88,128]{2,1,0:T(8,128)}), f32[16,88,128]{2,1,0:T(8,128)S(1)}, u32[]{:S(2)}, u32[]{:S(2)}) async-start(f32[16,88,128]{2,1,0:T(8,128)} %pad_maximum_fusion), calls=%async_computation | async-start | bytes 1441792 | tf_op jit(solution)/shard_map/all_to_all | solution.py:222
  28.4 5.2 %collective-permute-start.1 = (f32[272,128]{1,0:T(8,128)S(1)}, f32[272,128]{1,0:T(8,128)S(1)}, u32[]{:S(2)}, u32[]{:S(2)}) collective-permute-start(f32[272,128]{1,0:T(8,128)S(1)} %pad_maximum_fusion.1), channel_id=1, source_target_pairs={{0,1},{1,2},{2,3},{3,7},{7,6},{6,5},{5,4},{4,8},{8,9},{9,10},{10,1... | collective-permute-start | bytes 417800 | tf_op jit(solution)/shard_map/ppermute | solution.py:244
  28.7 4.8 %collective-permute-start.2 = (f32[272,128]{1,0:T(8,128)S(1)}, f32[272,128]{1,0:T(8,128)S(1)}, u32[]{:S(2)}, u32[]{:S(2)}) collective-permute-start(f32[272,128]{1,0:T(8,128)S(1)} %pad_maximum_fusion.1), channel_id=1, source_target_pairs={{1,0},{2,1},{3,2},{7,3},{6,7},{5,6},{4,5},{8,4},{9,8},{10,9},{11,1... | collective-permute-start | bytes 417800 | tf_op jit(solution)/shard_map/ppermute | solution.py:245
  38.4 5.1 %collective-permute-start.3 = (f32[256,128]{1,0:T(8,128)S(1)}, f32[256,128]{1,0:T(8,128)S(1)}, u32[]{:S(2)}, u32[]{:S(2)}) collective-permute-start(f32[256,128]{1,0:T(8,128)S(1)} %get-tuple-element.22), channel_id=1, source_target_pairs={{0,1},{1,2},{2,3},{3,7},{7,6},{6,5},{5,4},{4,8},{8,9},{9,10},{10,1... | collective-permute-start | bytes 393224 | tf_op jit(solution)/shard_map/ppermute | solution.py:252
  39.1 4.4 %collective-permute-start.4 = (f32[256,128]{1,0:T(8,128)S(1)}, f32[256,128]{1,0:T(8,128)S(1)}, u32[]{:S(2)}, u32[]{:S(2)}) collective-permute-start(f32[256,128]{1,0:T(8,128)S(1)} %get-tuple-element.23), channel_id=1, source_target_pairs={{1,0},{2,1},{3,2},{7,3},{6,7},{5,6},{4,5},{8,4},{9,8},{10,9},{11,1... | collective-permute-start | bytes 393224 | tf_op jit(solution)/shard_map/ppermute | solution.py:251
  44.8 6.6 %collective-permute-start.5 = (f32[256,128]{1,0:T(8,128)S(1)}, f32[256,128]{1,0:T(8,128)S(1)}, u32[]{:S(2)}, u32[]{:S(2)}) collective-permute-start(f32[256,128]{1,0:T(8,128)S(1)} %multiply_multiply_fusion.1.own_ref), channel_id=1, source_target_pairs={{0,1},{1,2},{2,3},{3,7},{7,6},{6,5},{5,4},{4,8},{8,9},{9,10},{10,1... | collective-permute-start | bytes 393224 | tf_op jit(solution)/shard_map/ppermute | solution.py:244
  44.8 6.5 %collective-permute-start.6 = (f32[256,128]{1,0:T(8,128)S(1)}, f32[256,128]{1,0:T(8,128)S(1)}, u32[]{:S(2)}, u32[]{:S(2)}) collective-permute-start(f32[256,128]{1,0:T(8,128)S(1)} %multiply_multiply_fusion.1.own_ref), channel_id=1, source_target_pairs={{1,0},{2,1},{3,2},{7,3},{6,7},{5,6},{4,5},{8,4},{9,8},{10,9},{11,1... | collective-permute-start | bytes 393224 | tf_op jit(solution)/shard_map/ppermute | solution.py:245
  56.1 6.1 %collective-permute-start.7 = (f32[256,128]{1,0:T(8,128)S(1)}, f32[256,128]{1,0:T(8,128)S(1)}, u32[]{:S(2)}, u32[]{:S(2)}) collective-permute-start(f32[256,128]{1,0:T(8,128)S(1)} %get-tuple-element.25), channel_id=1, source_target_pairs={{0,1},{1,2},{2,3},{3,7},{7,6},{6,5},{5,4},{4,8},{8,9},{9,10},{10,1... | collective-permute-start | bytes 393224 | tf_op jit(solution)/shard_map/ppermute | solution.py:252
  56.2 6.0 %collective-permute-start.8 = (f32[256,128]{1,0:T(8,128)S(1)}, f32[256,128]{1,0:T(8,128)S(1)}, u32[]{:S(2)}, u32[]{:S(2)}) collective-permute-start(f32[256,128]{1,0:T(8,128)S(1)} %get-tuple-element.26), channel_id=1, source_target_pairs={{1,0},{2,1},{3,2},{7,3},{6,7},{5,6},{4,5},{8,4},{9,8},{10,9},{11,1... | collective-permute-start | bytes 393224 | tf_op jit(solution)/shard_map/ppermute | solution.py:251
  64.2 10.5 %all-to-all-start.1 = ((f32[16,16,128]{2,1,0:T(8,128)}), f32[16,16,128]{2,1,0:T(8,128)S(1)}, u32[]{:S(2)}, u32[]{:S(2)}) async-start(f32[16,16,128]{2,1,0:T(8,128)} %bitcast.13), calls=%async_computation.1 | async-start | bytes 262144 | tf_op jit(solution)/shard_map/all_to_all | solution.py:254
  74.7 14.8 %collective-permute-start.9 = (f32[8,16,128]{2,1,0:T(8,128)S(1)}, f32[8,16,128]{2,1,0:T(8,128)S(1)}, u32[]{:S(2)}, u32[]{:S(2)}) collective-permute-start(f32[8,16,128]{2,1,0:T(8,128)S(1)} %slice.120), channel_id=1, source_target_pairs={{0,16},{1,17},{2,18},{3,19},{4,20},{5,21},{6,22},{7,23},{8,24},{9,... | collective-permute-start | bytes 196616 | tf_op jit(solution)/shard_map/ppermute | solution.py:258
where the time goes:
time: 90.7 us; the launch traced here: 90.2 us
  starting transfers between devices  38.1 us (42%)
  waiting for transfers between devices  30.6 us (34%)
  Pallas kernels  11.1 us (12%)
  other arithmetic  6 us (7%)
  local copies, waits for them, and re-layouts  4.26 us (5%)
    ppermute x1, starting transfers between devices, body(): got = lax.ppermute(theirs, AXES, SWAP)  13.9 us
    all_to_all x1, waiting for transfers between devices, body(): lax.all_to_all(jnp.concatenate([keep, other], axis=0), 'gy', split_axis=0...  12.2 us
    pallas_call x2, Pallas kernels, body(): step(meta, flags, before, own, after, arrived, band, row_mat, back_mat)  9.57 us
    all_to_all x1, starting transfers between devices, body(): lax.all_to_all(jnp.concatenate([keep, other], axis=0), 'gy', split_axis=0...  7.85 us
    all_to_all x1, waiting for transfers between devices, body(): lax.all_to_all(own.reshape(GY, ROWS, T), 'gy', split_axis=0, concat_axis=...  6.83 us
    ppermute x2, starting transfers between devices, body(): after = lax.ppermute(out, AXES, BACKWARD)  5.2 us
    ppermute x2, waiting for transfers between devices, body(): before = lax.ppermute(out, AXES, FORWARD)  5.2 us
    ppermute x2, waiting for transfers between devices, body(): from_before = lax.ppermute(high, AXES, FORWARD)  5 us
  transfers between devices with their start and end apart: 12, of which 8 were waited for; matrix products, arithmetic and copies ran while one was open for 2% of the time, Pallas kernels for 1%

commit v1 on v0

--- a/solution.py
+++ b/solution.py
@@ -1,8 +1,5 @@
-import functools
-
 import jax
 import jax.numpy as jnp
-import numpy as np
 from jax import lax
 from jax.experimental import pallas as pl
 from jax.experimental.pallas import tpu as pltpu
@@ -24,13 +21,28 @@
 F32 = jnp.float32
 BF16 = jnp.bfloat16
 VMEM = pl.BlockSpec(memory_space=pltpu.VMEM)
+HBM = pl.BlockSpec(memory_space=pltpu.HBM)
 SMEM = pl.BlockSpec(memory_space=pltpu.SMEM)
 PARAMS = pltpu.CompilerParams(vmem_limit_bytes=48 * 1024 * 1024)
 
 
 def device_of(core, chunk):
-    place = (chunk % 16 + 8 * core) % 16
-    return (2 * (chunk // 16) + core) * GY + SNAKE.index(place)
+    group = chunk // 16
+    within = chunk % 16 if group % 2 == 0 else 15 - chunk % 16
+    return (2 * group + core) * GY + SNAKE.index((within + 8 * core) % 16)
+
+
+def here():
+    core, group = lax.axis_index("gx") % 2, lax.axis_index("gx") // 2
+    row, col = lax.axis_index("gy") // 4, lax.axis_index("gy") % 4
+    place = 4 * row + jnp.where(row % 2 == 0, col, 3 - col)
+    within = (place + 8 * core) % 16
+    odd = group % 2
+    return core, odd, 16 * group + jnp.where(odd == 0, within, 15 - within)
+
+
+def slot_chunk(slot, odd):
+    return jnp.where(odd == 0, PERM[slot], 7 - PERM[slot])
 
 
 FORWARD = [
@@ -46,12 +58,24 @@
     return hi, (x - hi.astype(F32)).astype(BF16)
 
 
-def pack_kernel(core_ref, codes_ref, shifts_ref, est_ref, views_ref, keep_ref, send_ref):
-    core = core_ref[0]
+def pack_kernel(
+    codes_hbm, shifts_hbm, est_hbm, views_hbm, keep_ref, send_ref, codes_ref, shifts_ref, est, views, sems
+):
+    core, odd, _ = here()
+    copies = [
+        pltpu.make_async_copy(codes_hbm, codes_ref, sems.at[0]),
+        pltpu.make_async_copy(shifts_hbm, shifts_ref, sems.at[1]),
+        pltpu.make_async_copy(est_hbm, est, sems.at[2]),
+        pltpu.make_async_copy(views_hbm, views, sems.at[3]),
+    ]
+    for copy in copies:
+        copy.start()
+    for copy in copies:
+        copy.wait()
     lane = lax.broadcasted_iota(jnp.int32, (8, T), 1)
     for slot in range(8):
-        chunk = PERM[slot]
-        rows = pl.ds(chunk * ROWS, ROWS)
+        chunk = slot_chunk(slot, odd)
+        rows = pl.ds(pl.multiple_of(chunk * ROWS, ROWS), ROWS)
         meta = jnp.zeros((8, T), F32)
         for half in range(2):
             for v in range(V):
@@ -60,10 +84,38 @@
                 meta = jnp.where(lane == half * V + v, code, meta)
                 meta = jnp.where(lane == 8 + half * V + v, shift, meta)
         for ref, plane in ((keep_ref, core), (send_ref, 1 - core)):
-            ref[slot, 0:ROWS, :] = est_ref[plane, rows, :]
+            ref[slot, 0:ROWS, :] = est[plane, rows, :]
             for v in range(V):
-                ref[slot, pl.ds(ROWS * (1 + v), ROWS), :] = views_ref[v, plane, rows, :].astype(F32)
+                ref[slot, pl.ds(ROWS * (1 + v), ROWS), :] = views[v, plane, rows, :].astype(F32)
             ref[slot, pl.ds(ROWS * (1 + V), 8), :] = meta
+
+
+def join_kernel(keep_ref, other_ref, out_hbm, sems):
+    _, odd, _ = here()
+    copies = [
+        pltpu.make_async_copy(keep_ref, out_hbm.at[pl.ds(8 * odd, 8)], sems.at[0]),
+        pltpu.make_async_copy(other_ref, out_hbm.at[pl.ds(8 - 8 * odd, 8)], sems.at[1]),
+    ]
+    for copy in copies:
+        copy.start()
+    for copy in copies:
+        copy.wait()
+
+
+def update_kernel(own_ref, mid_ref, low_ref, high_ref, out_ref):
+    _, _, chunk = here()
+    has_before = jnp.where(chunk > 0, 1.0, 0.0).astype(F32)
+    has_after = jnp.where(chunk < CHUNKS - 1, 1.0, 0.0).astype(F32)
+    total = mid_ref[...] + high_ref[...] * has_before + low_ref[...] * has_after
+    out_ref[...] = own_ref[0 : GY * ROWS, :] * (total * 0.25)
+
+
+def unpack_kernel(home_ref, got_ref, out_ref):
+    core, odd, _ = here()
+    for slot in range(8):
+        rows = pl.ds(pl.multiple_of(slot_chunk(slot, odd) * ROWS, ROWS), ROWS)
+        out_ref[core, rows, :] = home_ref[8 * odd + slot]
+        out_ref[1 - core, rows, :] = got_ref[slot]
 
 
 def taps_kernel(cols_ref, rows_ref, band_ref, row_ref, back_ref):
@@ -106,9 +158,11 @@
 
 
 def step_kernel(
-    meta_ref, flag_ref, before_ref, own_ref, after_ref, arrived_ref, band_ref, row_ref, back_ref,
+    meta_ref, before_ref, own_ref, after_ref, arrived_ref, band_ref, row_ref, back_ref,
     low_ref, mid_ref, high_ref, est2, slope2, view_u, total2,
 ):
+    _, _, here_chunk = here()
+    inside = {0: here_chunk > 0, 2: here_chunk < CHUNKS - 1}
     lane = lax.broadcasted_iota(jnp.int32, (GY, 8, T), 2)
     inner = jnp.where(lane < T - 1, 1.0 / 16.0, 0.0).astype(F32)
     for src, ref in enumerate((before_ref, own_ref, after_ref)):
@@ -116,7 +170,7 @@
             b = 2 * src + half
             x = ref[0 : GY * ROWS, :].reshape(GY, ROWS, T)[:, 8 * half : 8 * half + 8, :]
             if src != 1:
-                x = x * flag_ref[src // 2]
+                x = x * jnp.where(inside[src], 1.0, 0.0).astype(F32)
             d = (pltpu.roll(x, T - 1, 2) - x) * inner
             est2[b, 0:GY] = x
             est2[b, GY : 2 * GY] = x
@@ -179,23 +233,23 @@
 
 
 def body(estimate, views, psf_rows, psf_cols, shifts, codes):
-    core = lax.axis_index("gx") % 2
-    group = lax.axis_index("gx") // 2
-    gy = lax.axis_index("gy")
-    within = gy % 4 + 4 * (gy // 4)
-    within = jnp.where((gy // 4) % 2 == 0, within, 4 * (gy // 4) + 3 - gy % 4)
-    chunk = group * 16 + (within + 8 * core) % 16
-    flags = jnp.stack([chunk > 0, chunk < CHUNKS - 1]).astype(F32)
-
+    _, odd, _ = here()
     unit = jax.ShapeDtypeStruct((8, UNIT, T), F32)
     keep, send = pl.pallas_call(
         pack_kernel,
         out_shape=(unit, unit),
-        in_specs=[SMEM, SMEM, SMEM, VMEM, VMEM],
+        in_specs=[HBM] * 4,
         out_specs=(VMEM, VMEM),
+        scratch_shapes=[
+            pltpu.SMEM((V, 2 * 8), jnp.int32),
+            pltpu.SMEM((V, 2 * 8), jnp.int32),
+            pltpu.VMEM((Z, T, T), F32),
+            pltpu.VMEM((V, Z, T, T), BF16),
+            pltpu.SemaphoreType.DMA((4,)),
+        ],
         compiler_params=PARAMS,
         name="pack",
-    )(core.reshape(1), codes[:, :, 0], shifts, estimate, views)
+    )(codes[:, :, 0], shifts, estimate, views)
     other = lax.ppermute(send, AXES, SWAP)
 
     rows_n = psf_rows / jnp.sum(psf_rows, axis=1, keepdims=True)
@@ -219,16 +273,30 @@
         name="taps",
     )(col_base, row_base)
 
-    arrived = lax.all_to_all(
-        jnp.concatenate([keep, other], axis=0), "gy", split_axis=0, concat_axis=0, tiled=True
-    )
+    joined = pl.pallas_call(
+        join_kernel,
+        out_shape=jax.ShapeDtypeStruct((GY, UNIT, T), F32),
+        in_specs=[VMEM, VMEM],
+        out_specs=HBM,
+        scratch_shapes=[pltpu.SemaphoreType.DMA((2,))],
+        compiler_params=PARAMS,
+        name="join",
+    )(keep, other)
+    arrived = lax.all_to_all(joined, "gy", split_axis=0, concat_axis=0, tiled=True)
     own = arrived[:, :ROWS, :].reshape(GY * ROWS, T)
     own_meta = arrived[:, ROWS * (1 + V), :]
-    meta = None
+    update = pl.pallas_call(
+        update_kernel,
+        out_shape=jax.ShapeDtypeStruct((GY * ROWS, T), F32),
+        in_specs=[VMEM] * 4,
+        out_specs=VMEM,
+        compiler_params=PARAMS,
+        name="update",
+    )
     step = pl.pallas_call(
         step_kernel,
         out_shape=(jax.ShapeDtypeStruct((GY * ROWS, T), F32),) * 3,
-        in_specs=[SMEM, SMEM] + [VMEM] * 7,
+        in_specs=[SMEM] + [VMEM] * 7,
         out_specs=(VMEM,) * 3,
         scratch_shapes=[
             pltpu.VMEM((6, 2 * GY, 8, T), F32),
@@ -247,21 +315,22 @@
             meta = jnp.concatenate(
                 [before[GY * ROWS :, :META], own_meta[:, :META], after[GY * ROWS :, :META]], axis=0
             ).astype(jnp.int32)
-        low, mid, high = step(meta, flags, before, own, after, arrived, band, row_mat, back_mat)
+        low, mid, high = step(meta, before, own, after, arrived, band, row_mat, back_mat)
         from_after = lax.ppermute(low, AXES, BACKWARD)
         from_before = lax.ppermute(high, AXES, FORWARD)
-        own = own * ((mid + from_before * flags[0] + from_after * flags[1]) * 0.25)
+        own = update(own, mid, from_after, from_before)
     home = lax.all_to_all(
         own.reshape(GY, ROWS, T), "gy", split_axis=0, concat_axis=0, tiled=True
     )
-    mine, theirs = home[:8], home[8:]
-    got = lax.ppermute(theirs, AXES, SWAP)
-
-    def ordered(part):
-        return jnp.concatenate([part[PERM.index(q)] for q in range(8)], axis=0)
-
-    mine, got = ordered(mine), ordered(got)
-    return jnp.where(core == 0, jnp.stack([mine, got]), jnp.stack([got, mine]))
+    got = lax.ppermute(lax.dynamic_slice_in_dim(home, 8 - 8 * odd, 8, 0), AXES, SWAP)
+    return pl.pallas_call(
+        unpack_kernel,
+        out_shape=jax.ShapeDtypeStruct((Z, T, T), F32),
+        in_specs=[VMEM, VMEM],
+        out_specs=VMEM,
+        compiler_params=PARAMS,
+        name="unpack",
+    )(home, got)
 
 
 def solution(mesh):

time: 90.7 us -> 85.5 us (0.943)
  starting transfers between devices: 38.1 us -> 32.5 us
  other arithmetic: 6 us -> 0.42 us
  waiting for transfers between devices: 30.6 us -> 35 us
  Pallas kernels: 11.1 us -> 13.4 us
    ppermute x1, starting transfers between devices: 13.9 us -> 8.66 us  [body(): lax.ppermute(lax.dynamic_slice_in_dim(home, 8 - 8 * odd, 8, 0), AXES, SWAP)]
    ppermute x2, waiting for transfers between devices: 0.01 us -> 3.89 us  [body(): from_after = lax.ppermute(low, AXES, BACKWARD)]
    mul x2 -> x0, other arithmetic: 3.23 us -> none  [body(): own = own * ((mid + from_before * flags[0] + from_after * flags[1]) * 0.25)]
    pallas_call x3 -> x7, Pallas kernels: 10.2 us -> 12.6 us  [the longest x2 9.54 us: body(): step(meta, before, own, after, arrived, band, row_mat, back_mat)]
    ppermute x2, waiting for transfers between devices: 5.2 us -> 3.86 us  [body(): before = lax.ppermute(out, AXES, FORWARD)]
    ppermute x2, waiting for transfers between devices: 5 us -> 6.16 us  [body(): from_before = lax.ppermute(high, AXES, FORWARD)]
    concatenate x1 -> x0, other arithmetic: 0.92 us -> none  [body(): jnp.concatenate([keep, other], axis=0)]
    unnamed x26 -> x12, local copies, waits for them, and re-layouts: 3.25 us -> 3.22 us
  transfers between devices with their start and end apart: 12 -> 12, of which waited for: 8 -> 10; matrix products, arithmetic and copies ran while one was open for 2% -> 1% of each run, Pallas kernels for 1% -> 1%
where the time goes in v1:
time: 85.5 us; the launch traced here: 85.2 us
  waiting for transfers between devices  35 us (41%)
  starting transfers between devices  32.5 us (38%)
  Pallas kernels  13.4 us (16%)
  local copies, waits for them, and re-layouts  3.61 us (4%)
    all_to_all x1, waiting for transfers between devices, body(): lax.all_to_all(joined, 'gy', split_axis=0, concat_axis=0, tiled=True)  12.1 us
    pallas_call x2, Pallas kernels, body(): step(meta, before, own, after, arrived, band, row_mat, back_mat)  9.54 us
    ppermute x1, starting transfers between devices, body(): lax.ppermute(lax.dynamic_slice_in_dim(home, 8 - 8 * odd, 8, 0), AXES, SWAP)  8.66 us
    all_to_all x1, starting transfers between devices, body(): lax.all_to_all(joined, 'gy', split_axis=0, concat_axis=0, tiled=True)  7.86 us
    all_to_all x1, waiting for transfers between devices, body(): lax.all_to_all(own.reshape(GY, ROWS, T), 'gy', split_axis=0, concat_axis=...  6.77 us
    ppermute x2, waiting for transfers between devices, body(): from_before = lax.ppermute(high, AXES, FORWARD)  6.16 us
    ppermute x2, starting transfers between devices, body(): from_after = lax.ppermute(low, AXES, BACKWARD)  5.49 us
    ppermute x2, starting transfers between devices, body(): after = lax.ppermute(out, AXES, BACKWARD)  5.05 us
  transfers between devices with their start and end apart: 12, of which 10 were waited for; matrix products, arithmetic and copies ran while one was open for 1% of the time, Pallas kernels for 1%

profile of v1, /device:TPU:1, one launch (start us, length us, event | category | flops | bytes accessed | tf_op | source)
XLA Modules:
  0.0 85.2 jit_solution(5504275617548307515)
XLA Ops:
  0.0 0.0 copy-start
  0.0 0.9 %copy-done = bf16[4,2,128,128]{3,2,1,0:T(8,128)(2,1)S(1)} copy-done((bf16[4,2,128,128]{3,2,1,0:T(8,128)(2,1)S(1)}, bf16[4,2,128,128]{3,2,1,0:T(8,128)(2,1)}, u32[]{:S(2)}) %copy-start) | copy-done | bytes 262168
  1.0 0.0 copy-start.1
  1.0 0.9 %copy-done.1 = f32[2,128,128]{2,1,0:T(8,128)S(1)} copy-done((f32[2,128,128]{2,1,0:T(8,128)S(1)}, f32[2,128,128]{2,1,0:T(8,128)}, u32[]{:S(2)}) %copy-start.1) | copy-done | bytes 131096
  1.9 0.0 copy-start.2
  1.9 0.7 copy-done.2
  2.5 0.0 copy-start.3
  2.5 0.7 copy-done.3
  3.2 0.0 copy-start.4
  3.2 0.0 copy-start.5
  3.2 0.8 pack.1
  4.0 1.5 %collective-permute-start = (f32[8,88,128]{2,1,0:T(8,128)S(1)}, f32[8,88,128]{2,1,0:T(8,128)S(1)}, u32[]{:S(2)}, u32[]{:S(2)}) collective-permute-start(f32[8,88,128]{2,1,0:T(8,128)S(1)} %get-tuple-element.17), channel_id=1, source_target_pairs={{0,16},{1,17},{2,18},{3,19},{4,20},{5,21},{6,22},{7,23},{8,24},{9,... | collective-permute-start | bytes 1081352 | tf_op jit(solution)/shard_map/ppermute | solution.py:253
  5.5 1.3 %collective-permute-done.other_ref = f32[8,88,128]{2,1,0:T(8,128)S(1)} collective-permute-done((f32[8,88,128]{2,1,0:T(8,128)S(1)}, f32[8,88,128]{2,1,0:T(8,128)S(1)}, u32[]{:S(2)}, u32[]{:S(2)}) %collective-permute-start) | collective-permute-done | bytes 360480 | tf_op jit(solution)/shard_map/ppermute | solution.py:253
  6.8 0.9 %join.1 = f32[16,88,128]{2,1,0:T(8,128)} custom-call(f32[8,88,128]{2,1,0:T(8,128)S(1)} %get-tuple-element.16.keep_ref, f32[8,88,128]{2,1,0:T(8,128)S(1)} %collective-permute-done.other_ref), custom_call_target="tpu_custom_call" | custom-call | tf_op jit(solution)/shard_map/join/pallas_call | solution.py:276
  7.7 7.9 %all-to-all-start = ((f32[16,88,128]{2,1,0:T(8,128)}), f32[16,88,128]{2,1,0:T(8,128)S(1)}, u32[]{:S(2)}, u32[]{:S(2)}) async-start(f32[16,88,128]{2,1,0:T(8,128)} %join.1), calls=%async_computation | async-start | bytes 1441792 | tf_op jit(solution)/shard_map/all_to_all | solution.py:285
  15.6 0.0 copy-done.4
  15.6 0.1 reduce_sum.18
  15.7 0.1 broadcast_divide_fusion.1
  15.8 0.1 rev.6
  15.9 0.0 copy-done.5
  15.9 0.1 reduce_sum.19
  16.0 0.1 broadcast_divide_fusion
  16.1 0.1 rev.7
  16.2 0.1 pad_bitcast_fusion
  16.3 12.1 %all-to-all-done.arrived_ref = f32[16,88,128]{2,1,0:T(8,128)S(1)} async-done(((f32[16,88,128]{2,1,0:T(8,128)}), f32[16,88,128]{2,1,0:T(8,128)S(1)}, u32[]{:S(2)}, u32[]{:S(2)}) %all-to-all-start) | async-done | bytes 720928 | tf_op jit(solution)/shard_map/all_to_all | solution.py:285
  28.5 0.4 collective-permute-start.1
  28.8 2.4 %collective-permute-start.2 = (f32[272,128]{1,0:T(8,128)S(1)}, f32[272,128]{1,0:T(8,128)S(1)}, u32[]{:S(2)}, u32[]{:S(2)}) collective-permute-start(f32[272,128]{1,0:T(8,128)S(1)} %pad_maximum_fusion), channel_id=1, source_target_pairs={{1,0},{2,1},{3,2},{7,3},{6,7},{5,6},{4,5},{8,4},{9,8},{10,9},{11,1... | collective-permute-start | bytes 417800 | tf_op jit(solution)/shard_map/ppermute | solution.py:313
  31.2 0.1 pad_bitcast_fusion.2
  31.3 0.8 taps.1
  32.1 1.5 %collective-permute-done.1.before_ref = f32[272,128]{1,0:T(8,128)S(1)} collective-permute-done((f32[272,128]{1,0:T(8,128)S(1)}, f32[272,128]{1,0:T(8,128)S(1)}, u32[]{:S(2)}, u32[]{:S(2)}) %collective-permute-start.1) | collective-permute-done | bytes 139296 | tf_op jit(solution)/shard_map/ppermute | solution.py:312
  33.6 0.0 collective-permute-done.2.after_ref
  33.7 4.8 %step.2 = (f32[256,128]{1,0:T(8,128)S(1)}, f32[256,128]{1,0:T(8,128)S(1)}, f32[256,128]{1,0:T(8,128)S(1)}) custom-call(s32[48,16]{1,0:T(8,128)S(1)} %maximum_convert_fusion.meta_ref, f32[272,128]{1,0:T(8,128)S(1)} %collective-permute-done.1.before_ref, f32[256,128]{1,0:T(8,128)S(1)} %bitcast.15, f32[272,128]{1,0:T(8,128)S(1)} %collective-permute-done.2.after_ref, ...), custom_call_target="tpu_custom_call" | custom-call | tf_op jit(solution)/shard_map/step/pallas_call | solution.py:318
  38.4 2.7 %collective-permute-start.3 = (f32[256,128]{1,0:T(8,128)S(1)}, f32[256,128]{1,0:T(8,128)S(1)}, u32[]{:S(2)}, u32[]{:S(2)}) collective-permute-start(f32[256,128]{1,0:T(8,128)S(1)} %get-tuple-element.22), channel_id=1, source_target_pairs={{1,0},{2,1},{3,2},{7,3},{6,7},{5,6},{4,5},{8,4},{9,8},{10,9},{11,1... | collective-permute-start | bytes 393224 | tf_op jit(solution)/shard_map/ppermute | solution.py:319
  41.2 0.0 collective-permute-start.4
  41.2 1.9 %collective-permute-done.3.low_ref = f32[256,128]{1,0:T(8,128)S(1)} collective-permute-done((f32[256,128]{1,0:T(8,128)S(1)}, f32[256,128]{1,0:T(8,128)S(1)}, u32[]{:S(2)}, u32[]{:S(2)}) %collective-permute-start.3) | collective-permute-done | bytes 131104 | tf_op jit(solution)/shard_map/ppermute | solution.py:319
  43.1 3.1 %collective-permute-done.4.high_ref = f32[256,128]{1,0:T(8,128)S(1)} collective-permute-done((f32[256,128]{1,0:T(8,128)S(1)}, f32[256,128]{1,0:T(8,128)S(1)}, u32[]{:S(2)}, u32[]{:S(2)}) %collective-permute-start.4) | collective-permute-done | bytes 131104 | tf_op jit(solution)/shard_map/ppermute | solution.py:320
  46.3 0.1 collective-permute-start.5
  46.3 2.7 %collective-permute-start.6 = (f32[256,128]{1,0:T(8,128)S(1)}, f32[256,128]{1,0:T(8,128)S(1)}, u32[]{:S(2)}, u32[]{:S(2)}) collective-permute-start(f32[256,128]{1,0:T(8,128)S(1)} %update.2.own_ref), channel_id=1, source_target_pairs={{1,0},{2,1},{3,2},{7,3},{6,7},{5,6},{4,5},{8,4},{9,8},{10,9},{11,1... | collective-permute-start | bytes 393224 | tf_op jit(solution)/shard_map/ppermute | solution.py:313
  49.0 2.4 %collective-permute-done.5.before_ref = f32[256,128]{1,0:T(8,128)S(1)} collective-permute-done((f32[256,128]{1,0:T(8,128)S(1)}, f32[256,128]{1,0:T(8,128)S(1)}, u32[]{:S(2)}, u32[]{:S(2)}) %collective-permute-start.5) | collective-permute-done | bytes 131104 | tf_op jit(solution)/shard_map/ppermute | solution.py:312
  51.4 0.0 collective-permute-done.6.after_ref
  51.4 4.8 %step.3 = (f32[256,128]{1,0:T(8,128)S(1)}, f32[256,128]{1,0:T(8,128)S(1)}, f32[256,128]{1,0:T(8,128)S(1)}) custom-call(s32[48,16]{1,0:T(8,128)S(1)} %maximum_convert_fusion.meta_ref, f32[256,128]{1,0:T(8,128)S(1)} %collective-permute-done.5.before_ref, f32[256,128]{1,0:T(8,128)S(1)} %update.2.own_ref, f32[256,128]{1,0:T(8,128)S(1)} %collective-permute-done.6.after_ref, ...), custom_call_target="tpu_custom_call" | custom-call | tf_op jit(solution)/shard_map/step/pallas_call | solution.py:318
  56.1 2.7 %collective-permute-start.7 = (f32[256,128]{1,0:T(8,128)S(1)}, f32[256,128]{1,0:T(8,128)S(1)}, u32[]{:S(2)}, u32[]{:S(2)}) collective-permute-start(f32[256,128]{1,0:T(8,128)S(1)} %get-tuple-element.25), channel_id=1, source_target_pairs={{1,0},{2,1},{3,2},{7,3},{6,7},{5,6},{4,5},{8,4},{9,8},{10,9},{11,1... | collective-permute-start | bytes 393224 | tf_op jit(solution)/shard_map/ppermute | solution.py:319
  58.9 0.0 collective-permute-start.8
  58.9 1.9 %collective-permute-done.7.low_ref = f32[256,128]{1,0:T(8,128)S(1)} collective-permute-done((f32[256,128]{1,0:T(8,128)S(1)}, f32[256,128]{1,0:T(8,128)S(1)}, u32[]{:S(2)}, u32[]{:S(2)}) %collective-permute-start.7) | collective-permute-done | bytes 131104 | tf_op jit(solution)/shard_map/ppermute | solution.py:319
  60.8 3.1 %collective-permute-done.8.high_ref = f32[256,128]{1,0:T(8,128)S(1)} collective-permute-done((f32[256,128]{1,0:T(8,128)S(1)}, f32[256,128]{1,0:T(8,128)S(1)}, u32[]{:S(2)}, u32[]{:S(2)}) %collective-permute-start.8) | collective-permute-done | bytes 131104 | tf_op jit(solution)/shard_map/ppermute | solution.py:320
  63.9 0.7 update.3
  64.6 3.5 %all-to-all-start.1 = ((f32[16,16,128]{2,1,0:T(8,128)}), f32[16,16,128]{2,1,0:T(8,128)S(1)}, u32[]{:S(2)}, u32[]{:S(2)}) async-start(f32[16,16,128]{2,1,0:T(8,128)} %bitcast.8), calls=%async_computation.1 | async-start | bytes 262144 | tf_op jit(solution)/shard_map/all_to_all | solution.py:322
  68.2 6.8 %all-to-all-done.1.home_ref = f32[16,16,128]{2,1,0:T(8,128)S(1)} async-done(((f32[16,16,128]{2,1,0:T(8,128)}), f32[16,16,128]{2,1,0:T(8,128)S(1)}, u32[]{:S(2)}, u32[]{:S(2)}) %all-to-all-start.1) | async-done | bytes 131104 | tf_op jit(solution)/shard_map/all_to_all | solution.py:322
  74.9 8.7 %collective-permute-start.9 = (f32[8,16,128]{2,1,0:T(8,128)S(1)}, f32[8,16,128]{2,1,0:T(8,128)S(1)}, u32[]{:S(2)}, u32[]{:S(2)}) collective-permute-start(f32[8,16,128]{2,1,0:T(8,128)S(1)} %constant_dynamic-slice_fusion), channel_id=1, source_target_pairs={{0,16},{1,17},{2,18},{3,19},{4,20},{5,21},{6,22},{7,23},{8,24},{9,... | collective-permute-start | bytes 196616 | tf_op jit(solution)/shard_map/ppermute | solution.py:325
  83.6 0.9 %collective-permute-done.9.got_ref = f32[8,16,128]{2,1,0:T(8,128)S(1)} collective-permute-done((f32[8,16,128]{2,1,0:T(8,128)S(1)}, f32[8,16,128]{2,1,0:T(8,128)S(1)}, u32[]{:S(2)}, u32[]{:S(2)}) %collective-permute-start.9) | collective-permute-done | bytes 65568 | tf_op jit(solution)/shard_map/ppermute | solution.py:325
  84.5 0.7 unpack.1
  (13 shorter events, 0.1 us)
Async XLA Ops:
  0.0 0.9 %copy-start = (bf16[4,2,128,128]{3,2,1,0:T(8,128)(2,1)S(1)}, bf16[4,2,128,128]{3,2,1,0:T(8,128)(2,1)}, u32[]{:S(2)}) copy-start(bf16[4,2,128,128]{3,2,1,0:T(8,128)(2,1)} %views_hbm.1) | copy-start | bytes 786436
  1.0 0.9 %copy-start.1 = (f32[2,128,128]{2,1,0:T(8,128)S(1)}, f32[2,128,128]{2,1,0:T(8,128)}, u32[]{:S(2)}) copy-start(f32[2,128,128]{2,1,0:T(8,128)} %est_hbm.1) | copy-start | bytes 393220
  1.9 0.7 copy-start.2
  2.5 0.7 copy-start.3
  3.2 12.4 %copy-start.4 = (f32[4,31]{1,0:T(4,128)S(1)}, f32[4,31]{1,0:T(4,128)}, u32[]{:S(2)}) copy-start(f32[4,31]{1,0:T(4,128)} %param.9) | copy-start | bytes 1492
  3.2 12.7 %copy-start.5 = (f32[4,31]{1,0:T(4,128)S(1)}, f32[4,31]{1,0:T(4,128)}, u32[]{:S(2)}) copy-start(f32[4,31]{1,0:T(4,128)} %param.8) | copy-start | bytes 1492
  4.0 2.8 %collective-permute-start = (f32[8,88,128]{2,1,0:T(8,128)S(1)}, f32[8,88,128]{2,1,0:T(8,128)S(1)}, u32[]{:S(2)}, u32[]{:S(2)}) collective-permute-start(f32[8,88,128]{2,1,0:T(8,128)S(1)} %get-tuple-element.17), channel_id=1, source_target_pairs={{0,16},{1,17},{2,18},{3,19},{4,20},{5,21},{6,22},{7,23},{8,24},{9,... | collective-permute-start | bytes 1081352 | tf_op jit(solution)/shard_map/ppermute | solution.py:253
  7.7 20.7 %all-to-all-start = ((f32[16,88,128]{2,1,0:T(8,128)}), f32[16,88,128]{2,1,0:T(8,128)S(1)}, u32[]{:S(2)}, u32[]{:S(2)}) async-start(f32[16,88,128]{2,1,0:T(8,128)} %join.1), calls=%async_computation | async-start | bytes 1441792 | tf_op jit(solution)/shard_map/all_to_all | solution.py:285
  28.5 5.2 %collective-permute-start.1 = (f32[272,128]{1,0:T(8,128)S(1)}, f32[272,128]{1,0:T(8,128)S(1)}, u32[]{:S(2)}, u32[]{:S(2)}) collective-permute-start(f32[272,128]{1,0:T(8,128)S(1)} %pad_maximum_fusion), channel_id=1, source_target_pairs={{0,1},{1,2},{2,3},{3,7},{7,6},{6,5},{5,4},{4,8},{8,9},{9,10},{10,1... | collective-permute-start | bytes 417800 | tf_op jit(solution)/shard_map/ppermute | solution.py:312
  28.8 4.8 %collective-permute-start.2 = (f32[272,128]{1,0:T(8,128)S(1)}, f32[272,128]{1,0:T(8,128)S(1)}, u32[]{:S(2)}, u32[]{:S(2)}) collective-permute-start(f32[272,128]{1,0:T(8,128)S(1)} %pad_maximum_fusion), channel_id=1, source_target_pairs={{1,0},{2,1},{3,2},{7,3},{6,7},{5,6},{4,5},{8,4},{9,8},{10,9},{11,1... | collective-permute-start | bytes 417800 | tf_op jit(solution)/shard_map/ppermute | solution.py:313
  38.4 4.7 %collective-permute-start.3 = (f32[256,128]{1,0:T(8,128)S(1)}, f32[256,128]{1,0:T(8,128)S(1)}, u32[]{:S(2)}, u32[]{:S(2)}) collective-permute-start(f32[256,128]{1,0:T(8,128)S(1)} %get-tuple-element.22), channel_id=1, source_target_pairs={{1,0},{2,1},{3,2},{7,3},{6,7},{5,6},{4,5},{8,4},{9,8},{10,9},{11,1... | collective-permute-start | bytes 393224 | tf_op jit(solution)/shard_map/ppermute | solution.py:319
  41.2 5.0 %collective-permute-start.4 = (f32[256,128]{1,0:T(8,128)S(1)}, f32[256,128]{1,0:T(8,128)S(1)}, u32[]{:S(2)}, u32[]{:S(2)}) collective-permute-start(f32[256,128]{1,0:T(8,128)S(1)} %get-tuple-element.23), channel_id=1, source_target_pairs={{0,1},{1,2},{2,3},{3,7},{7,6},{6,5},{5,4},{4,8},{8,9},{9,10},{10,1... | collective-permute-start | bytes 393224 | tf_op jit(solution)/shard_map/ppermute | solution.py:320
  46.3 5.1 %collective-permute-start.5 = (f32[256,128]{1,0:T(8,128)S(1)}, f32[256,128]{1,0:T(8,128)S(1)}, u32[]{:S(2)}, u32[]{:S(2)}) collective-permute-start(f32[256,128]{1,0:T(8,128)S(1)} %update.2.own_ref), channel_id=1, source_target_pairs={{0,1},{1,2},{2,3},{3,7},{7,6},{6,5},{5,4},{4,8},{8,9},{9,10},{10,1... | collective-permute-start | bytes 393224 | tf_op jit(solution)/shard_map/ppermute | solution.py:312
  46.3 5.0 %collective-permute-start.6 = (f32[256,128]{1,0:T(8,128)S(1)}, f32[256,128]{1,0:T(8,128)S(1)}, u32[]{:S(2)}, u32[]{:S(2)}) collective-permute-start(f32[256,128]{1,0:T(8,128)S(1)} %update.2.own_ref), channel_id=1, source_target_pairs={{1,0},{2,1},{3,2},{7,3},{6,7},{5,6},{4,5},{8,4},{9,8},{10,9},{11,1... | collective-permute-start | bytes 393224 | tf_op jit(solution)/shard_map/ppermute | solution.py:313
  56.1 4.7 %collective-permute-start.7 = (f32[256,128]{1,0:T(8,128)S(1)}, f32[256,128]{1,0:T(8,128)S(1)}, u32[]{:S(2)}, u32[]{:S(2)}) collective-permute-start(f32[256,128]{1,0:T(8,128)S(1)} %get-tuple-element.25), channel_id=1, source_target_pairs={{1,0},{2,1},{3,2},{7,3},{6,7},{5,6},{4,5},{8,4},{9,8},{10,9},{11,1... | collective-permute-start | bytes 393224 | tf_op jit(solution)/shard_map/ppermute | solution.py:319
  58.9 5.0 %collective-permute-start.8 = (f32[256,128]{1,0:T(8,128)S(1)}, f32[256,128]{1,0:T(8,128)S(1)}, u32[]{:S(2)}, u32[]{:S(2)}) collective-permute-start(f32[256,128]{1,0:T(8,128)S(1)} %get-tuple-element.26), channel_id=1, source_target_pairs={{0,1},{1,2},{2,3},{3,7},{7,6},{6,5},{5,4},{4,8},{8,9},{9,10},{10,1... | collective-permute-start | bytes 393224 | tf_op jit(solution)/shard_map/ppermute | solution.py:320
  64.6 10.3 %all-to-all-start.1 = ((f32[16,16,128]{2,1,0:T(8,128)}), f32[16,16,128]{2,1,0:T(8,128)S(1)}, u32[]{:S(2)}, u32[]{:S(2)}) async-start(f32[16,16,128]{2,1,0:T(8,128)} %bitcast.8), calls=%async_computation.1 | async-start | bytes 262144 | tf_op jit(solution)/shard_map/all_to_all | solution.py:322
  74.9 9.6 %collective-permute-start.9 = (f32[8,16,128]{2,1,0:T(8,128)S(1)}, f32[8,16,128]{2,1,0:T(8,128)S(1)}, u32[]{:S(2)}, u32[]{:S(2)}) collective-permute-start(f32[8,16,128]{2,1,0:T(8,128)S(1)} %constant_dynamic-slice_fusion), channel_id=1, source_target_pairs={{0,16},{1,17},{2,18},{3,19},{4,20},{5,21},{6,22},{7,23},{8,24},{9,... | collective-permute-start | bytes 196616 | tf_op jit(solution)/shard_map/ppermute | solution.py:325

commit v2 on v1

--- a/solution.py
+++ b/solution.py
@@ -15,8 +15,6 @@
 CHUNKS = 64
 META = 16
 UNIT = ROWS * (1 + V) + 8
-PERM = (0, 1, 2, 3, 7, 6, 5, 4)
-SNAKE = PERM + tuple(8 + p for p in PERM)
 AXES = ("gx", "gy")
 F32 = jnp.float32
 BF16 = jnp.bfloat16
@@ -26,31 +24,45 @@
 PARAMS = pltpu.CompilerParams(vmem_limit_bytes=48 * 1024 * 1024)
 
 
-def device_of(core, chunk):
-    group = chunk // 16
-    within = chunk % 16 if group % 2 == 0 else 15 - chunk % 16
-    return (2 * group + core) * GY + SNAKE.index((within + 8 * core) % 16)
+def device_of(plane, chunk):
+    core, block = chunk % 2, chunk // 2
+    group, tile, part = block // 8, block % 8 // 4, block % 4
+    inner = (tile == 0) == (group % 2 == 0)
+    row = (1 if inner else 0, 2 if inner else 3)[plane]
+    return (2 * group + core) * GY + 4 * row + (part if tile == 0 else 3 - part)
+
+
+def both_ways(pairs):
+    return [(a, b) for a, b in pairs] + [(b, a) for a, b in pairs]
+
+
+SWAP = both_ways([(2 * x * GY + g, (2 * x + 1) * GY + g) for x in range(GX // 2) for g in range(GY)])
+PAIR = both_ways(
+    [
+        (device_of(p, q), device_of(p, q + 1))
+        for p in range(Z) for q in range(1, CHUNKS - 1, 2)
+    ]
+    + [(device_of(0, q), device_of(1, q)) for q in (0, CHUNKS - 1)]
+)
+
+
+def own_tile_inner():
+    core, group = lax.axis_index("gx") % 2, lax.axis_index("gx") // 2
+    return core, (core + group) % 2 == 0
 
 
 def here():
     core, group = lax.axis_index("gx") % 2, lax.axis_index("gx") // 2
     row, col = lax.axis_index("gy") // 4, lax.axis_index("gy") % 4
-    place = 4 * row + jnp.where(row % 2 == 0, col, 3 - col)
-    within = (place + 8 * core) % 16
-    odd = group % 2
-    return core, odd, 16 * group + jnp.where(odd == 0, within, 15 - within)
-
-
-def slot_chunk(slot, odd):
-    return jnp.where(odd == 0, PERM[slot], 7 - PERM[slot])
-
-
-FORWARD = [
-    (device_of(c, q), device_of(c, (q + 1) % CHUNKS)) for c in range(2) for q in range(CHUNKS)
-]
-BACKWARD = [(b, a) for a, b in FORWARD]
-SWAP = [((2 * x + c) * GY + g, (2 * x + 1 - c) * GY + g)
-        for x in range(GX // 2) for c in range(2) for g in range(GY)]
+    inner = jnp.where((row == 1) | (row == 2), 1, 0)
+    first_tile = (inner + group) % 2 == 1
+    block = 8 * group + jnp.where(first_tile, col, 7 - col)
+    paired = jnp.where(core == 0, block > 0, block < CHUNKS // 2 - 1)
+    return core, jnp.where(paired, 1.0, 0.0).astype(F32)
+
+
+def part_of(col, core):
+    return jnp.where(core == 0, col, 3 - col)
 
 
 def split(x):
@@ -61,7 +73,7 @@
 def pack_kernel(
     codes_hbm, shifts_hbm, est_hbm, views_hbm, keep_ref, send_ref, codes_ref, shifts_ref, est, views, sems
 ):
-    core, odd, _ = here()
+    core, _ = own_tile_inner()
     copies = [
         pltpu.make_async_copy(codes_hbm, codes_ref, sems.at[0]),
         pltpu.make_async_copy(shifts_hbm, shifts_ref, sems.at[1]),
@@ -74,16 +86,17 @@
         copy.wait()
     lane = lax.broadcasted_iota(jnp.int32, (8, T), 1)
     for slot in range(8):
-        chunk = slot_chunk(slot, odd)
-        rows = pl.ds(pl.multiple_of(chunk * ROWS, ROWS), ROWS)
-        meta = jnp.zeros((8, T), F32)
-        for half in range(2):
-            for v in range(V):
-                code = codes_ref[v, 2 * chunk + half].astype(F32)
-                shift = shifts_ref[v, 2 * chunk + half].astype(F32)
-                meta = jnp.where(lane == half * V + v, code, meta)
-                meta = jnp.where(lane == 8 + half * V + v, shift, meta)
-        for ref, plane in ((keep_ref, core), (send_ref, 1 - core)):
+        plane, col = slot // 4, slot % 4
+        for ref, sub in ((keep_ref, core), (send_ref, 1 - core)):
+            chunk = 2 * part_of(col, core) + sub
+            rows = pl.ds(pl.multiple_of(chunk * ROWS, ROWS), ROWS)
+            meta = jnp.zeros((8, T), F32)
+            for half in range(2):
+                for v in range(V):
+                    code = codes_ref[v, 2 * chunk + half].astype(F32)
+                    shift = shifts_ref[v, 2 * chunk + half].astype(F32)
+                    meta = jnp.where(lane == half * V + v, code, meta)
+                    meta = jnp.where(lane == 8 + half * V + v, shift, meta)
             ref[slot, 0:ROWS, :] = est[plane, rows, :]
             for v in range(V):
                 ref[slot, pl.ds(ROWS * (1 + v), ROWS), :] = views[v, plane, rows, :].astype(F32)
@@ -91,31 +104,37 @@
 
 
 def join_kernel(keep_ref, other_ref, out_hbm, sems):
-    _, odd, _ = here()
-    copies = [
-        pltpu.make_async_copy(keep_ref, out_hbm.at[pl.ds(8 * odd, 8)], sems.at[0]),
-        pltpu.make_async_copy(other_ref, out_hbm.at[pl.ds(8 - 8 * odd, 8)], sems.at[1]),
-    ]
+    _, inner = own_tile_inner()
+    copies = []
+    for i, (ref, near) in enumerate(((keep_ref, inner), (other_ref, jnp.logical_not(inner)))):
+        first, second = jnp.where(near, 4, 0), jnp.where(near, 8, 12)
+        copies.append(
+            pltpu.make_async_copy(ref.at[0:4], out_hbm.at[pl.ds(first, 4)], sems.at[2 * i])
+        )
+        copies.append(
+            pltpu.make_async_copy(ref.at[4:8], out_hbm.at[pl.ds(second, 4)], sems.at[2 * i + 1])
+        )
     for copy in copies:
         copy.start()
     for copy in copies:
         copy.wait()
 
 
-def update_kernel(own_ref, mid_ref, low_ref, high_ref, out_ref):
-    _, _, chunk = here()
-    has_before = jnp.where(chunk > 0, 1.0, 0.0).astype(F32)
-    has_after = jnp.where(chunk < CHUNKS - 1, 1.0, 0.0).astype(F32)
-    total = mid_ref[...] + high_ref[...] * has_before + low_ref[...] * has_after
+def update_kernel(own_ref, mid_ref, paired_ref, swapped_ref, out_ref):
+    _, has_pair = here()
+    total = mid_ref[...] + paired_ref[...] * has_pair + swapped_ref[...]
     out_ref[...] = own_ref[0 : GY * ROWS, :] * (total * 0.25)
 
 
 def unpack_kernel(home_ref, got_ref, out_ref):
-    core, odd, _ = here()
+    core, inner = own_tile_inner()
     for slot in range(8):
-        rows = pl.ds(pl.multiple_of(slot_chunk(slot, odd) * ROWS, ROWS), ROWS)
-        out_ref[core, rows, :] = home_ref[8 * odd + slot]
-        out_ref[1 - core, rows, :] = got_ref[slot]
+        plane, col = slot // 4, slot % 4
+        start = 2 * part_of(col, core)
+        source = jnp.where(inner, 4 + slot, 12 * plane + col)
+        for sub, value in ((core, home_ref[source]), (1 - core, got_ref[slot])):
+            rows = pl.ds(pl.multiple_of((start + sub) * ROWS, ROWS), ROWS)
+            out_ref[plane, rows, :] = value
 
 
 def taps_kernel(cols_ref, rows_ref, band_ref, row_ref, back_ref):
@@ -158,19 +177,24 @@
 
 
 def step_kernel(
-    meta_ref, before_ref, own_ref, after_ref, arrived_ref, band_ref, row_ref, back_ref,
-    low_ref, mid_ref, high_ref, est2, slope2, view_u, total2,
+    meta_ref, paired_ref, own_ref, swapped_ref, arrived_ref, band_ref, row_ref, back_ref,
+    pair_ref, mid_ref, swap_ref, est2, slope2, view_u, total2,
 ):
-    _, _, here_chunk = here()
-    inside = {0: here_chunk > 0, 2: here_chunk < CHUNKS - 1}
+    core, has_pair = here()
+    first = core == 0
+    bases = (jnp.where(first, 0, 2 * GY), GY, jnp.where(first, 2 * GY, 0))
+
+    def own_block(ref, half):
+        return ref[0 : GY * ROWS, :].reshape(GY, ROWS, T)[:, 8 * half : 8 * half + 8, :]
+
     lane = lax.broadcasted_iota(jnp.int32, (GY, 8, T), 2)
     inner = jnp.where(lane < T - 1, 1.0 / 16.0, 0.0).astype(F32)
-    for src, ref in enumerate((before_ref, own_ref, after_ref)):
-        for half in range(2):
+    for half in range(2):
+        paired = own_block(paired_ref, half) * has_pair
+        swapped = own_block(swapped_ref, half)
+        before, after = jnp.where(first, paired, swapped), jnp.where(first, swapped, paired)
+        for src, x in enumerate((before, own_block(own_ref, half), after)):
             b = 2 * src + half
-            x = ref[0 : GY * ROWS, :].reshape(GY, ROWS, T)[:, 8 * half : 8 * half + 8, :]
-            if src != 1:
-                x = x * jnp.where(inside[src], 1.0, 0.0).astype(F32)
             d = (pltpu.roll(x, T - 1, 2) - x) * inner
             est2[b, 0:GY] = x
             est2[b, GY : 2 * GY] = x
@@ -183,11 +207,11 @@
             parts = []
             for half in range(2):
                 b = 2 * src + half
-                shift = meta_ref[src * GY, 8 + half * V + v]
+                shift = meta_ref[bases[src], 8 + half * V + v]
                 x = est2[b, pl.ds(shift, GY)]
                 d = slope2[b, pl.ds(shift, GY)]
                 parts.append([
-                    x[c] + meta_ref[src * GY + c, half * V + v].astype(F32) * d[c]
+                    x[c] + meta_ref[bases[src] + c, half * V + v].astype(F32) * d[c]
                     for c in range(GY)
                 ])
             for c in range(GY):
@@ -211,18 +235,20 @@
         )
         for b in range(6):
             src, half = b // 2, b % 2
-            shift = meta_ref[src * GY, 8 + half * V + v]
+            shift = meta_ref[bases[src], 8 + half * V + v]
             parts = []
             for c in range(GY):
                 r = spread[8 * b : 8 * b + 8, T * c : T * c + T]
                 g = r * inner8
                 g = pltpu.roll(g, 1, 1) - g
-                parts.append(r + meta_ref[src * GY + c, half * V + v].astype(F32) * g)
+                parts.append(r + meta_ref[bases[src] + c, half * V + v].astype(F32) * g)
             total2[b, pl.ds(shift, GY)] += jnp.stack(parts)
-    for src, ref in enumerate((low_ref, mid_ref, high_ref)):
-        for half in range(2):
-            b = 2 * src + half
-            y = total2[b, 0:GY] + total2[b, GY : 2 * GY]
+    for half in range(2):
+        low, mid, high = [
+            total2[2 * src + half, 0:GY] + total2[2 * src + half, GY : 2 * GY] for src in range(3)
+        ]
+        pair, swap = jnp.where(first, low, high), jnp.where(first, high, low)
+        for ref, y in ((pair_ref, pair), (mid_ref, mid), (swap_ref, swap)):
             for c in range(GY):
                 ref[ROWS * c + 8 * half : ROWS * c + 8 * half + 8, :] = y[c]
 
@@ -233,7 +259,7 @@
 
 
 def body(estimate, views, psf_rows, psf_cols, shifts, codes):
-    _, odd, _ = here()
+    _, inner = own_tile_inner()
     unit = jax.ShapeDtypeStruct((8, UNIT, T), F32)
     keep, send = pl.pallas_call(
         pack_kernel,
@@ -278,7 +304,7 @@
         out_shape=jax.ShapeDtypeStruct((GY, UNIT, T), F32),
         in_specs=[VMEM, VMEM],
         out_specs=HBM,
-        scratch_shapes=[pltpu.SemaphoreType.DMA((2,))],
+        scratch_shapes=[pltpu.SemaphoreType.DMA((4,))],
         compiler_params=PARAMS,
         name="join",
     )(keep, other)
@@ -309,20 +335,19 @@
     )
     for sweep in range(ITERS):
         out = jnp.concatenate([own, own_meta], axis=0) if sweep == 0 else own
-        before = lax.ppermute(out, AXES, FORWARD)
-        after = lax.ppermute(out, AXES, BACKWARD)
+        paired = lax.ppermute(out, AXES, PAIR)
+        swapped = lax.ppermute(out, AXES, SWAP)
         if sweep == 0:
             meta = jnp.concatenate(
-                [before[GY * ROWS :, :META], own_meta[:, :META], after[GY * ROWS :, :META]], axis=0
+                [paired[GY * ROWS :, :META], own_meta[:, :META], swapped[GY * ROWS :, :META]], axis=0
             ).astype(jnp.int32)
-        low, mid, high = step(meta, before, own, after, arrived, band, row_mat, back_mat)
-        from_after = lax.ppermute(low, AXES, BACKWARD)
-        from_before = lax.ppermute(high, AXES, FORWARD)
-        own = update(own, mid, from_after, from_before)
+        pair, mid, swap = step(meta, paired, own, swapped, arrived, band, row_mat, back_mat)
+        own = update(own, mid, lax.ppermute(pair, AXES, PAIR), lax.ppermute(swap, AXES, SWAP))
     home = lax.all_to_all(
         own.reshape(GY, ROWS, T), "gy", split_axis=0, concat_axis=0, tiled=True
     )
-    got = lax.ppermute(lax.dynamic_slice_in_dim(home, 8 - 8 * odd, 8, 0), AXES, SWAP)
+    theirs = jnp.where(inner, jnp.concatenate([home[0:4], home[12:16]], axis=0), home[4:12])
+    got = lax.ppermute(theirs, AXES, SWAP)
     return pl.pallas_call(
         unpack_kernel,
         out_shape=jax.ShapeDtypeStruct((Z, T, T), F32),

time: 85.5 us -> 73.3 us (0.86)
  starting transfers between devices: 32.5 us -> 23.1 us
  waiting for transfers between devices: 35 us -> 32 us
    ppermute x9, starting transfers between devices: 19.6 us -> 10.2 us  [the longest x2 4.46 us: body(): paired = lax.ppermute(out, AXES, PAIR)]
    ppermute x9, waiting for transfers between devices: 14.8 us -> 11.8 us  [the longest x2 5.85 us: body(): lax.ppermute(pair, AXES, PAIR)]
  transfers between devices with their start and end apart: 12 -> 12, of which waited for: 10 -> 8; matrix products, arithmetic and copies ran while one was open for 1% -> 1% of each run, Pallas kernels for 1% -> 1%
where the time goes in v2:
time: 73.3 us; the launch traced here: 72.9 us
  waiting for transfers between devices  32 us (44%)
  starting transfers between devices  23.1 us (32%)
  Pallas kernels  13.6 us (19%)
  local copies, waits for them, and re-layouts  3.61 us (5%)
    all_to_all x1, waiting for transfers between devices, body(): lax.all_to_all(joined, 'gy', split_axis=0, concat_axis=0, tiled=True)  12.2 us
    pallas_call x2, Pallas kernels, body(): step(meta, paired, own, swapped, arrived, band, row_mat, back_mat)  9.57 us
    all_to_all x1, starting transfers between devices, body(): lax.all_to_all(joined, 'gy', split_axis=0, concat_axis=0, tiled=True)  7.86 us
    all_to_all x1, waiting for transfers between devices, body(): lax.all_to_all(own.reshape(GY, ROWS, T), 'gy', split_axis=0, concat_axis=...  6.82 us
    ppermute x2, waiting for transfers between devices, body(): lax.ppermute(pair, AXES, PAIR)  5.85 us
    ppermute x2, waiting for transfers between devices, body(): paired = lax.ppermute(out, AXES, PAIR)  5 us
    ppermute x2, starting transfers between devices, body(): paired = lax.ppermute(out, AXES, PAIR)  4.46 us
    all_to_all x1, starting transfers between devices, body(): lax.all_to_all(own.reshape(GY, ROWS, T), 'gy', split_axis=0, concat_axis=...  3.51 us
  transfers between devices with their start and end apart: 12, of which 8 were waited for; matrix products, arithmetic and copies ran while one was open for 1% of the time, Pallas kernels for 1%

profile of v2, /device:TPU:1, one launch (start us, length us, event | category | flops | bytes accessed | tf_op | source)
XLA Modules:
  0.0 72.9 jit_solution(4070949495590841240)
XLA Ops:
  0.0 0.0 copy-start
  0.0 0.9 %copy-done = bf16[4,2,128,128]{3,2,1,0:T(8,128)(2,1)S(1)} copy-done((bf16[4,2,128,128]{3,2,1,0:T(8,128)(2,1)S(1)}, bf16[4,2,128,128]{3,2,1,0:T(8,128)(2,1)}, u32[]{:S(2)}) %copy-start) | copy-done | bytes 262168
  1.0 0.0 copy-start.1
  1.0 0.9 %copy-done.1 = f32[2,128,128]{2,1,0:T(8,128)S(1)} copy-done((f32[2,128,128]{2,1,0:T(8,128)S(1)}, f32[2,128,128]{2,1,0:T(8,128)}, u32[]{:S(2)}) %copy-start.1) | copy-done | bytes 131096
  1.9 0.0 copy-start.2
  1.9 0.7 copy-done.2
  2.5 0.0 copy-start.3
  2.5 0.7 copy-done.3
  3.2 0.0 copy-start.4
  3.2 0.0 copy-start.5
  3.2 0.9 %pack.1 = (f32[8,88,128]{2,1,0:T(8,128)S(1)}, f32[8,88,128]{2,1,0:T(8,128)S(1)}) custom-call(s32[4,16]{1,0:T(4,128)S(1)} %bitcast.18, s32[4,16]{1,0:T(4,128)S(1)} %copy-done.3, f32[2,128,128]{2,1,0:T(8,128)S(1)} %copy-done.1, bf16[4,2,128,128]{3,2,1,0:T(8,128)(2,1)S(1)} %copy-done), custom_call_target="tpu_custom_call" | custom-call | tf_op jit(solution)/shard_map/pack/pallas_call | solution.py:264
  4.1 1.5 %collective-permute-start = (f32[8,88,128]{2,1,0:T(8,128)S(1)}, f32[8,88,128]{2,1,0:T(8,128)S(1)}, u32[]{:S(2)}, u32[]{:S(2)}) collective-permute-start(f32[8,88,128]{2,1,0:T(8,128)S(1)} %get-tuple-element.17), channel_id=1, source_target_pairs={{0,16},{1,17},{2,18},{3,19},{4,20},{5,21},{6,22},{7,23},{8,24},{9,... | collective-permute-start | bytes 1081352 | tf_op jit(solution)/shard_map/ppermute | solution.py:279
  5.6 1.3 %collective-permute-done.other_ref = f32[8,88,128]{2,1,0:T(8,128)S(1)} collective-permute-done((f32[8,88,128]{2,1,0:T(8,128)S(1)}, f32[8,88,128]{2,1,0:T(8,128)S(1)}, u32[]{:S(2)}, u32[]{:S(2)}) %collective-permute-start) | collective-permute-done | bytes 360480 | tf_op jit(solution)/shard_map/ppermute | solution.py:279
  6.9 0.9 %join.1 = f32[16,88,128]{2,1,0:T(8,128)} custom-call(f32[8,88,128]{2,1,0:T(8,128)S(1)} %get-tuple-element.16.keep_ref, f32[8,88,128]{2,1,0:T(8,128)S(1)} %collective-permute-done.other_ref), custom_call_target="tpu_custom_call" | custom-call | tf_op jit(solution)/shard_map/join/pallas_call | solution.py:302
  7.8 7.9 %all-to-all-start = ((f32[16,88,128]{2,1,0:T(8,128)}), f32[16,88,128]{2,1,0:T(8,128)S(1)}, u32[]{:S(2)}, u32[]{:S(2)}) async-start(f32[16,88,128]{2,1,0:T(8,128)} %join.1), calls=%async_computation | async-start | bytes 1441792 | tf_op jit(solution)/shard_map/all_to_all | solution.py:311
  15.7 0.0 copy-done.4
  15.7 0.1 reduce_sum.18
  15.8 0.1 broadcast_divide_fusion.1
  15.9 0.1 rev.6
  16.0 0.0 copy-done.5
  16.0 0.1 reduce_sum.19
  16.1 0.1 broadcast_divide_fusion
  16.2 0.1 rev.7
  16.3 0.1 pad_bitcast_fusion
  16.4 12.2 %all-to-all-done.arrived_ref = f32[16,88,128]{2,1,0:T(8,128)S(1)} async-done(((f32[16,88,128]{2,1,0:T(8,128)}), f32[16,88,128]{2,1,0:T(8,128)S(1)}, u32[]{:S(2)}, u32[]{:S(2)}) %all-to-all-start) | async-done | bytes 720928 | tf_op jit(solution)/shard_map/all_to_all | solution.py:311
  28.6 2.9 %collective-permute-start.1 = (f32[272,128]{1,0:T(8,128)S(1)}, f32[272,128]{1,0:T(8,128)S(1)}, u32[]{:S(2)}, u32[]{:S(2)}) collective-permute-start(f32[272,128]{1,0:T(8,128)S(1)} %pad_maximum_fusion), channel_id=1, source_target_pairs={{20,5},{21,6},{22,7},{23,3},{19,2},{18,1},{17,0},{16,32},{48,33},{... | collective-permute-start | bytes 417800 | tf_op jit(solution)/shard_map/ppermute | solution.py:338
  31.5 0.0 collective-permute-start.2
  31.5 0.1 pad_bitcast_fusion.2
  31.6 0.8 %taps.1 = (bf16[4,2,768,128]{3,2,1,0:T(8,128)(2,1)S(1)}, bf16[4,16,144]{2,1,0:T(8,128)(2,1)S(1)}, bf16[4,48,48]{2,1,0:T(8,128)(2,1)S(1)}) custom-call(f32[8,256]{1,0:T(8,128)S(1)} %reshape.15.cols_ref, f32[8,128]{1,0:T(8,128)S(1)} %bitcast.17), custom_call_target="tpu_custom_call" | custom-call | tf_op jit(solution)/shard_map/taps/pallas_call | solution.py:289
  32.4 2.1 %collective-permute-done.1.paired_ref = f32[272,128]{1,0:T(8,128)S(1)} collective-permute-done((f32[272,128]{1,0:T(8,128)S(1)}, f32[272,128]{1,0:T(8,128)S(1)}, u32[]{:S(2)}, u32[]{:S(2)}) %collective-permute-start.1) | collective-permute-done | bytes 139296 | tf_op jit(solution)/shard_map/ppermute | solution.py:338
  34.5 0.0 collective-permute-done.2.swapped_ref
  34.5 4.8 %step.2 = (f32[256,128]{1,0:T(8,128)S(1)}, f32[256,128]{1,0:T(8,128)S(1)}, f32[256,128]{1,0:T(8,128)S(1)}) custom-call(s32[48,16]{1,0:T(8,128)S(1)} %maximum_convert_fusion.meta_ref, f32[272,128]{1,0:T(8,128)S(1)} %collective-permute-done.1.paired_ref, f32[256,128]{1,0:T(8,128)S(1)} %bitcast.15, f32[272,128]{1,0:T(8,128)S(1)} %collective-permute-done.2.swapped_ref, ...), custom_call_target="tpu_custom_call" | custom-call | tf_op jit(solution)/shard_map/step/pallas_call | solution.py:344
  39.3 1.6 %collective-permute-start.3 = (f32[256,128]{1,0:T(8,128)S(1)}, f32[256,128]{1,0:T(8,128)S(1)}, u32[]{:S(2)}, u32[]{:S(2)}) collective-permute-start(f32[256,128]{1,0:T(8,128)S(1)} %get-tuple-element.22), channel_id=1, source_target_pairs={{20,5},{21,6},{22,7},{23,3},{19,2},{18,1},{17,0},{16,32},{48,33},{... | collective-permute-start | bytes 393224 | tf_op jit(solution)/shard_map/ppermute | solution.py:345
  40.9 0.0 collective-permute-start.4
  40.9 2.9 %collective-permute-done.3.paired_ref = f32[256,128]{1,0:T(8,128)S(1)} collective-permute-done((f32[256,128]{1,0:T(8,128)S(1)}, f32[256,128]{1,0:T(8,128)S(1)}, u32[]{:S(2)}, u32[]{:S(2)}) %collective-permute-start.3) | collective-permute-done | bytes 131104 | tf_op jit(solution)/shard_map/ppermute | solution.py:345
  43.8 0.0 collective-permute-done.4.swapped_ref
  43.8 0.1 update.2.own_ref
  43.9 1.5 %collective-permute-start.5 = (f32[256,128]{1,0:T(8,128)S(1)}, f32[256,128]{1,0:T(8,128)S(1)}, u32[]{:S(2)}, u32[]{:S(2)}) collective-permute-start(f32[256,128]{1,0:T(8,128)S(1)} %update.2.own_ref), channel_id=1, source_target_pairs={{20,5},{21,6},{22,7},{23,3},{19,2},{18,1},{17,0},{16,32},{48,33},{... | collective-permute-start | bytes 393224 | tf_op jit(solution)/shard_map/ppermute | solution.py:338
  45.4 0.0 collective-permute-start.6
  45.4 2.9 %collective-permute-done.5.paired_ref = f32[256,128]{1,0:T(8,128)S(1)} collective-permute-done((f32[256,128]{1,0:T(8,128)S(1)}, f32[256,128]{1,0:T(8,128)S(1)}, u32[]{:S(2)}, u32[]{:S(2)}) %collective-permute-start.5) | collective-permute-done | bytes 131104 | tf_op jit(solution)/shard_map/ppermute | solution.py:338
  48.3 0.0 collective-permute-done.6.swapped_ref
  48.3 4.8 %step.3 = (f32[256,128]{1,0:T(8,128)S(1)}, f32[256,128]{1,0:T(8,128)S(1)}, f32[256,128]{1,0:T(8,128)S(1)}) custom-call(s32[48,16]{1,0:T(8,128)S(1)} %maximum_convert_fusion.meta_ref, f32[256,128]{1,0:T(8,128)S(1)} %collective-permute-done.5.paired_ref, f32[256,128]{1,0:T(8,128)S(1)} %update.2.own_ref, f32[256,128]{1,0:T(8,128)S(1)} %collective-permute-done.6.swapped_ref, ...), custom_call_target="tpu_custom_call" | custom-call | tf_op jit(solution)/shard_map/step/pallas_call | solution.py:344
  53.1 1.5 %collective-permute-start.7 = (f32[256,128]{1,0:T(8,128)S(1)}, f32[256,128]{1,0:T(8,128)S(1)}, u32[]{:S(2)}, u32[]{:S(2)}) collective-permute-start(f32[256,128]{1,0:T(8,128)S(1)} %get-tuple-element.25), channel_id=1, source_target_pairs={{20,5},{21,6},{22,7},{23,3},{19,2},{18,1},{17,0},{16,32},{48,33},{... | collective-permute-start | bytes 393224 | tf_op jit(solution)/shard_map/ppermute | solution.py:345
  54.7 0.0 collective-permute-start.8
  54.7 2.9 %collective-permute-done.7.paired_ref = f32[256,128]{1,0:T(8,128)S(1)} collective-permute-done((f32[256,128]{1,0:T(8,128)S(1)}, f32[256,128]{1,0:T(8,128)S(1)}, u32[]{:S(2)}, u32[]{:S(2)}) %collective-permute-start.7) | collective-permute-done | bytes 131104 | tf_op jit(solution)/shard_map/ppermute | solution.py:345
  57.6 0.0 collective-permute-done.8.swapped_ref
  57.6 0.7 update.3
  58.3 3.5 %all-to-all-start.1 = ((f32[16,16,128]{2,1,0:T(8,128)}), f32[16,16,128]{2,1,0:T(8,128)S(1)}, u32[]{:S(2)}, u32[]{:S(2)}) async-start(f32[16,16,128]{2,1,0:T(8,128)} %bitcast.8), calls=%async_computation.1 | async-start | bytes 262144 | tf_op jit(solution)/shard_map/all_to_all | solution.py:346
  61.9 6.8 %all-to-all-done.1.home_ref = f32[16,16,128]{2,1,0:T(8,128)S(1)} async-done(((f32[16,16,128]{2,1,0:T(8,128)}), f32[16,16,128]{2,1,0:T(8,128)S(1)}, u32[]{:S(2)}, u32[]{:S(2)}) %all-to-all-start.1) | async-done | bytes 131104 | tf_op jit(solution)/shard_map/all_to_all | solution.py:346
  68.7 2.6 %collective-permute-start.9 = (f32[8,16,128]{2,1,0:T(8,128)S(1)}, f32[8,16,128]{2,1,0:T(8,128)S(1)}, u32[]{:S(2)}, u32[]{:S(2)}) collective-permute-start(f32[8,16,128]{2,1,0:T(8,128)S(1)} %slice_select_fusion), channel_id=1, source_target_pairs={{0,16},{1,17},{2,18},{3,19},{4,20},{5,21},{6,22},{7,23},{8,24},{9,... | collective-permute-start | bytes 196616 | tf_op jit(solution)/shard_map/ppermute | solution.py:350
  71.3 0.9 %collective-permute-done.9.got_ref = f32[8,16,128]{2,1,0:T(8,128)S(1)} collective-permute-done((f32[8,16,128]{2,1,0:T(8,128)S(1)}, f32[8,16,128]{2,1,0:T(8,128)S(1)}, u32[]{:S(2)}, u32[]{:S(2)}) %collective-permute-start.9) | collective-permute-done | bytes 65568 | tf_op jit(solution)/shard_map/ppermute | solution.py:350
  72.2 0.7 unpack.1
  (13 shorter events, 0.1 us)
Async XLA Ops:
  0.0 0.9 %copy-start = (bf16[4,2,128,128]{3,2,1,0:T(8,128)(2,1)S(1)}, bf16[4,2,128,128]{3,2,1,0:T(8,128)(2,1)}, u32[]{:S(2)}) copy-start(bf16[4,2,128,128]{3,2,1,0:T(8,128)(2,1)} %views_hbm.1) | copy-start | bytes 786436
  1.0 0.9 %copy-start.1 = (f32[2,128,128]{2,1,0:T(8,128)S(1)}, f32[2,128,128]{2,1,0:T(8,128)}, u32[]{:S(2)}) copy-start(f32[2,128,128]{2,1,0:T(8,128)} %est_hbm.1) | copy-start | bytes 393220
  1.9 0.7 copy-start.2
  2.5 0.7 copy-start.3
  3.2 12.5 %copy-start.4 = (f32[4,31]{1,0:T(4,128)S(1)}, f32[4,31]{1,0:T(4,128)}, u32[]{:S(2)}) copy-start(f32[4,31]{1,0:T(4,128)} %param.9) | copy-start | bytes 1492
  3.2 12.8 %copy-start.5 = (f32[4,31]{1,0:T(4,128)S(1)}, f32[4,31]{1,0:T(4,128)}, u32[]{:S(2)}) copy-start(f32[4,31]{1,0:T(4,128)} %param.8) | copy-start | bytes 1492
  4.1 2.8 %collective-permute-start = (f32[8,88,128]{2,1,0:T(8,128)S(1)}, f32[8,88,128]{2,1,0:T(8,128)S(1)}, u32[]{:S(2)}, u32[]{:S(2)}) collective-permute-start(f32[8,88,128]{2,1,0:T(8,128)S(1)} %get-tuple-element.17), channel_id=1, source_target_pairs={{0,16},{1,17},{2,18},{3,19},{4,20},{5,21},{6,22},{7,23},{8,24},{9,... | collective-permute-start | bytes 1081352 | tf_op jit(solution)/shard_map/ppermute | solution.py:279
  7.8 20.7 %all-to-all-start = ((f32[16,88,128]{2,1,0:T(8,128)}), f32[16,88,128]{2,1,0:T(8,128)S(1)}, u32[]{:S(2)}, u32[]{:S(2)}) async-start(f32[16,88,128]{2,1,0:T(8,128)} %join.1), calls=%async_computation | async-start | bytes 1441792 | tf_op jit(solution)/shard_map/all_to_all | solution.py:311
  28.6 5.9 %collective-permute-start.1 = (f32[272,128]{1,0:T(8,128)S(1)}, f32[272,128]{1,0:T(8,128)S(1)}, u32[]{:S(2)}, u32[]{:S(2)}) collective-permute-start(f32[272,128]{1,0:T(8,128)S(1)} %pad_maximum_fusion), channel_id=1, source_target_pairs={{20,5},{21,6},{22,7},{23,3},{19,2},{18,1},{17,0},{16,32},{48,33},{... | collective-permute-start | bytes 417800 | tf_op jit(solution)/shard_map/ppermute | solution.py:338
  31.5 3.0 %collective-permute-start.2 = (f32[272,128]{1,0:T(8,128)S(1)}, f32[272,128]{1,0:T(8,128)S(1)}, u32[]{:S(2)}, u32[]{:S(2)}) collective-permute-start(f32[272,128]{1,0:T(8,128)S(1)} %pad_maximum_fusion), channel_id=1, source_target_pairs={{0,16},{1,17},{2,18},{3,19},{4,20},{5,21},{6,22},{7,23},{8,24},{9,... | collective-permute-start | bytes 417800 | tf_op jit(solution)/shard_map/ppermute | solution.py:339
  39.3 4.5 %collective-permute-start.3 = (f32[256,128]{1,0:T(8,128)S(1)}, f32[256,128]{1,0:T(8,128)S(1)}, u32[]{:S(2)}, u32[]{:S(2)}) collective-permute-start(f32[256,128]{1,0:T(8,128)S(1)} %get-tuple-element.22), channel_id=1, source_target_pairs={{20,5},{21,6},{22,7},{23,3},{19,2},{18,1},{17,0},{16,32},{48,33},{... | collective-permute-start | bytes 393224 | tf_op jit(solution)/shard_map/ppermute | solution.py:345
  40.9 2.9 %collective-permute-start.4 = (f32[256,128]{1,0:T(8,128)S(1)}, f32[256,128]{1,0:T(8,128)S(1)}, u32[]{:S(2)}, u32[]{:S(2)}) collective-permute-start(f32[256,128]{1,0:T(8,128)S(1)} %get-tuple-element.23), channel_id=1, source_target_pairs={{0,16},{1,17},{2,18},{3,19},{4,20},{5,21},{6,22},{7,23},{8,24},{9,... | collective-permute-start | bytes 393224 | tf_op jit(solution)/shard_map/ppermute | solution.py:345
  43.9 4.5 %collective-permute-start.5 = (f32[256,128]{1,0:T(8,128)S(1)}, f32[256,128]{1,0:T(8,128)S(1)}, u32[]{:S(2)}, u32[]{:S(2)}) collective-permute-start(f32[256,128]{1,0:T(8,128)S(1)} %update.2.own_ref), channel_id=1, source_target_pairs={{20,5},{21,6},{22,7},{23,3},{19,2},{18,1},{17,0},{16,32},{48,33},{... | collective-permute-start | bytes 393224 | tf_op jit(solution)/shard_map/ppermute | solution.py:338
  45.4 2.9 %collective-permute-start.6 = (f32[256,128]{1,0:T(8,128)S(1)}, f32[256,128]{1,0:T(8,128)S(1)}, u32[]{:S(2)}, u32[]{:S(2)}) collective-permute-start(f32[256,128]{1,0:T(8,128)S(1)} %update.2.own_ref), channel_id=1, source_target_pairs={{0,16},{1,17},{2,18},{3,19},{4,20},{5,21},{6,22},{7,23},{8,24},{9,... | collective-permute-start | bytes 393224 | tf_op jit(solution)/shard_map/ppermute | solution.py:339
  53.1 4.5 %collective-permute-start.7 = (f32[256,128]{1,0:T(8,128)S(1)}, f32[256,128]{1,0:T(8,128)S(1)}, u32[]{:S(2)}, u32[]{:S(2)}) collective-permute-start(f32[256,128]{1,0:T(8,128)S(1)} %get-tuple-element.25), channel_id=1, source_target_pairs={{20,5},{21,6},{22,7},{23,3},{19,2},{18,1},{17,0},{16,32},{48,33},{... | collective-permute-start | bytes 393224 | tf_op jit(solution)/shard_map/ppermute | solution.py:345
  54.7 2.9 %collective-permute-start.8 = (f32[256,128]{1,0:T(8,128)S(1)}, f32[256,128]{1,0:T(8,128)S(1)}, u32[]{:S(2)}, u32[]{:S(2)}) collective-permute-start(f32[256,128]{1,0:T(8,128)S(1)} %get-tuple-element.26), channel_id=1, source_target_pairs={{0,16},{1,17},{2,18},{3,19},{4,20},{5,21},{6,22},{7,23},{8,24},{9,... | collective-permute-start | bytes 393224 | tf_op jit(solution)/shard_map/ppermute | solution.py:345
  58.3 10.4 %all-to-all-start.1 = ((f32[16,16,128]{2,1,0:T(8,128)}), f32[16,16,128]{2,1,0:T(8,128)S(1)}, u32[]{:S(2)}, u32[]{:S(2)}) async-start(f32[16,16,128]{2,1,0:T(8,128)} %bitcast.8), calls=%async_computation.1 | async-start | bytes 262144 | tf_op jit(solution)/shard_map/all_to_all | solution.py:346
  68.7 3.5 %collective-permute-start.9 = (f32[8,16,128]{2,1,0:T(8,128)S(1)}, f32[8,16,128]{2,1,0:T(8,128)S(1)}, u32[]{:S(2)}, u32[]{:S(2)}) collective-permute-start(f32[8,16,128]{2,1,0:T(8,128)S(1)} %slice_select_fusion), channel_id=1, source_target_pairs={{0,16},{1,17},{2,18},{3,19},{4,20},{5,21},{6,22},{7,23},{8,24},{9,... | collective-permute-start | bytes 196616 | tf_op jit(solution)/shard_map/ppermute | solution.py:350

commit v3 on v2

--- a/solution.py
+++ b/solution.py
@@ -138,19 +138,21 @@
 
 
 def taps_kernel(cols_ref, rows_ref, band_ref, row_ref, back_ref):
+    def turned(base, count, width):
+        rows = jnp.broadcast_to(base, (count, base.shape[1]))
+        return split(pltpu.roll(rows, 0, 1, stride=1, stride_axis=0)[:, :width])
+
     for v in range(V):
         for d in range(2):
-            base = jnp.broadcast_to(cols_ref[2 * v + d : 2 * v + d + 1, :], (2 * T, 2 * T))
-            turned = pltpu.roll(base, 0, 1, stride=1, stride_axis=0)[:, :T]
-            hi, lo = split(turned)
-            band_ref[v, d, 0 : 2 * T, :] = hi
-            band_ref[v, d, 2 * T : 4 * T, :] = lo
-            band_ref[v, d, 4 * T : 6 * T, :] = hi
-        base = jnp.broadcast_to(rows_ref[2 * v : 2 * v + 1, :], (ROWS, T))
-        hi, lo = split(pltpu.roll(base, 0, 1, stride=1, stride_axis=0)[:, : 3 * ROWS])
-        row_ref[v] = jnp.concatenate([hi, hi, lo], axis=1)
-        base = jnp.broadcast_to(rows_ref[2 * v + 1 : 2 * v + 2, :], (3 * ROWS, T))
-        hi, lo = split(pltpu.roll(base, 0, 1, stride=1, stride_axis=0)[:, :ROWS])
+            hi, lo = turned(cols_ref[2 * v + d : 2 * v + d + 1, :], 2 * T, T)
+            band_ref[v, d, 0 : 2 * T, 0:T] = hi
+            band_ref[v, d, 0 : 2 * T, T : 2 * T] = lo
+            band_ref[v, d, 2 * T : 4 * T, 0:T] = hi
+            band_ref[v, d, 2 * T : 4 * T, T : 2 * T] = jnp.zeros_like(lo)
+        hi, lo = turned(rows_ref[2 * v : 2 * v + 1, :], ROWS, 3 * ROWS)
+        row_ref[v, 0:ROWS] = jnp.concatenate([hi, hi], axis=1)
+        row_ref[v, ROWS : 2 * ROWS] = jnp.concatenate([lo, jnp.zeros_like(lo)], axis=1)
+        hi, lo = turned(rows_ref[2 * v + 1 : 2 * v + 2, :], 3 * ROWS, ROWS)
         back_ref[v] = jnp.concatenate([hi, hi, lo], axis=1)
 
 
@@ -163,22 +165,21 @@
         jnp.where(lane < T // 2, turned[j], turned[j + 1]) for j in range(len(pieces) + 1)
     ]
     his, los = zip(*[split(m) for m in moved])
-    left = len(pieces)
-
-    def windows(parts):
-        return jnp.concatenate(
-            [jnp.concatenate([parts[c], parts[c + 1]], axis=1) for c in range(left)], axis=0
-        )
-
-    hi, lo = windows(his), windows(los)
-    return jnp.dot(
-        jnp.concatenate([hi, hi, lo], axis=1), band, preferred_element_type=F32
-    )
+    windows = [
+        jnp.concatenate([his[c], his[c + 1], los[c], los[c + 1]], axis=1)
+        for c in range(len(pieces))
+    ]
+    both = jnp.dot(jnp.concatenate(windows, axis=0), band, preferred_element_type=F32)
+    return both[:, :T] + both[:, T:]
+
+
+def column_tiles(ref, v):
+    return [ref[v, :, T * c : T * c + T] for c in range(GY)]
 
 
 def step_kernel(
     meta_ref, paired_ref, own_ref, swapped_ref, arrived_ref, band_ref, row_ref, back_ref,
-    pair_ref, mid_ref, swap_ref, est2, slope2, view_u, total2,
+    pair_ref, mid_ref, swap_ref, est2, slope2, view_u, total2, smooth, ratio, again,
 ):
     core, has_pair = here()
     first = core == 0
@@ -187,8 +188,15 @@
     def own_block(ref, half):
         return ref[0 : GY * ROWS, :].reshape(GY, ROWS, T)[:, 8 * half : 8 * half + 8, :]
 
+    def code_of(v, src, half, c):
+        return meta_ref[bases[src] + c, half * V + v].astype(F32)
+
+    def shift_of(v, src, half):
+        return meta_ref[bases[src], 8 + half * V + v]
+
     lane = lax.broadcasted_iota(jnp.int32, (GY, 8, T), 2)
     inner = jnp.where(lane < T - 1, 1.0 / 16.0, 0.0).astype(F32)
+    inner8 = inner[0]
     for half in range(2):
         paired = own_block(paired_ref, half) * has_pair
         swapped = own_block(swapped_ref, half)
@@ -201,48 +209,58 @@
             slope2[b, 0:GY] = d
             slope2[b, GY : 2 * GY] = d
     total2[...] = jnp.zeros(total2.shape, F32)
-    inner8 = inner[0]
-    for v in range(V):
+
+    def gather(v):
         for src in range(3):
             parts = []
             for half in range(2):
                 b = 2 * src + half
-                shift = meta_ref[bases[src], 8 + half * V + v]
+                shift = shift_of(v, src, half)
                 x = est2[b, pl.ds(shift, GY)]
                 d = slope2[b, pl.ds(shift, GY)]
-                parts.append([
-                    x[c] + meta_ref[bases[src] + c, half * V + v].astype(F32) * d[c]
-                    for c in range(GY)
-                ])
+                parts.append([x[c] + code_of(v, src, half, c) * d[c] for c in range(GY)])
             for c in range(GY):
                 hi, lo = split(jnp.concatenate([parts[0][c], parts[1][c]], axis=0))
                 cols = slice(T * c, T * c + T)
                 view_u[v, ROWS * src : ROWS * src + ROWS, cols] = hi
                 view_u[v, ROWS * (3 + src) : ROWS * (4 + src), cols] = lo
-                view_u[v, ROWS * (6 + src) : ROWS * (7 + src), cols] = hi
-        smooth = jnp.dot(row_ref[v], view_u[v], preferred_element_type=F32)
-        blurred = column_pass([smooth[:, T * c : T * c + T] for c in range(GY)], band_ref[v, 0])
-        ratio = [
-            arrived_ref[c, ROWS * (1 + v) : ROWS * (2 + v), :]
-            / blurred[ROWS * c : ROWS * c + ROWS, :]
-            for c in range(GY)
-        ]
-        again = column_pass(ratio, band_ref[v, 1])
-        his, los = zip(*[split(again[ROWS * c : ROWS * c + ROWS, :]) for c in range(GY)])
+
+    def rows_in(v):
+        both = jnp.dot(row_ref[v], view_u[v], preferred_element_type=F32)
+        smooth[v] = both[:ROWS] + both[ROWS:]
+
+    def cols_in(v):
+        blurred = column_pass(column_tiles(smooth, v), band_ref[v, 0])
+        for c in range(GY):
+            ratio[v, :, T * c : T * c + T] = (
+                arrived_ref[c, ROWS * (1 + v) : ROWS * (2 + v), :]
+                / blurred[ROWS * c : ROWS * c + ROWS, :]
+            )
+
+    def cols_back(v):
+        again[v] = column_pass(column_tiles(ratio, v), band_ref[v, 1])
+
+    def rows_back(v):
+        his, los = zip(*[split(again[v, ROWS * c : ROWS * c + ROWS, :]) for c in range(GY)])
         hi, lo = jnp.concatenate(his, axis=1), jnp.concatenate(los, axis=1)
         spread = jnp.dot(
             back_ref[v], jnp.concatenate([hi, lo, hi], axis=0), preferred_element_type=F32
         )
         for b in range(6):
             src, half = b // 2, b % 2
-            shift = meta_ref[bases[src], 8 + half * V + v]
             parts = []
             for c in range(GY):
                 r = spread[8 * b : 8 * b + 8, T * c : T * c + T]
                 g = r * inner8
                 g = pltpu.roll(g, 1, 1) - g
-                parts.append(r + meta_ref[bases[src] + c, half * V + v].astype(F32) * g)
-            total2[b, pl.ds(shift, GY)] += jnp.stack(parts)
+                parts.append(r + code_of(v, src, half, c) * g)
+            total2[b, pl.ds(shift_of(v, src, half), GY)] += jnp.stack(parts)
+
+    stages = (gather, rows_in, cols_in, cols_back, rows_back)
+    for turn in range(V + len(stages) - 1):
+        for i, stage in enumerate(stages):
+            if 0 <= turn - i < V:
+                stage(turn - i)
     for half in range(2):
         low, mid, high = [
             total2[2 * src + half, 0:GY] + total2[2 * src + half, GY : 2 * GY] for src in range(3)
@@ -253,9 +271,8 @@
                 ref[ROWS * c + 8 * half : ROWS * c + 8 * half + 8, :] = y[c]
 
 
-def place(base, width, taps, at):
-    left = at
-    return jnp.pad(taps, ((0, 0), (left, width - left - taps.shape[1])))
+def place(taps, at, width):
+    return jnp.pad(taps, ((0, 0), (at, width - at - taps.shape[1])))
 
 
 def body(estimate, views, psf_rows, psf_cols, shifts, codes):
@@ -275,22 +292,27 @@
         ],
         compiler_params=PARAMS,
         name="pack",
-    )(codes[:, :, 0], shifts, estimate, views)
+    )(
+        *[
+            pltpu.with_memory_space_constraint(a, pltpu.HBM)
+            for a in (codes[:, :, 0], shifts, estimate, views)
+        ]
+    )
     other = lax.ppermute(send, AXES, SWAP)
 
     rows_n = psf_rows / jnp.sum(psf_rows, axis=1, keepdims=True)
     cols_n = psf_cols / jnp.sum(psf_cols, axis=1, keepdims=True)
     col_base = jnp.stack(
-        [place(None, 2 * T, cols_n[:, ::-1], 177), place(None, 2 * T, cols_n, 177)], axis=1
+        [place(cols_n[:, ::-1], 177, 2 * T), place(cols_n, 177, 2 * T)], axis=1
     ).reshape(2 * V, 2 * T)
     row_base = jnp.stack(
-        [place(None, T, rows_n, 1), place(None, T, rows_n[:, ::-1], T - 31)], axis=1
+        [place(rows_n, 1, T), place(rows_n[:, ::-1], T - 31, T)], axis=1
     ).reshape(2 * V, T)
     band, row_mat, back_mat = pl.pallas_call(
         taps_kernel,
         out_shape=(
-            jax.ShapeDtypeStruct((V, 2, 6 * T, T), BF16),
-            jax.ShapeDtypeStruct((V, ROWS, 9 * ROWS), BF16),
+            jax.ShapeDtypeStruct((V, 2, 4 * T, 2 * T), BF16),
+            jax.ShapeDtypeStruct((V, 2 * ROWS, 6 * ROWS), BF16),
             jax.ShapeDtypeStruct((V, 3 * ROWS, 3 * ROWS), BF16),
         ),
         in_specs=[VMEM, VMEM],
@@ -327,8 +349,11 @@
         scratch_shapes=[
             pltpu.VMEM((6, 2 * GY, 8, T), F32),
             pltpu.VMEM((6, 2 * GY, 8, T), F32),
-            pltpu.VMEM((V, 9 * ROWS, GY * T), BF16),
+            pltpu.VMEM((V, 6 * ROWS, GY * T), BF16),
             pltpu.VMEM((6, 2 * GY, 8, T), F32),
+            pltpu.VMEM((V, ROWS, GY * T), F32),
+            pltpu.VMEM((V, ROWS, GY * T), F32),
+            pltpu.VMEM((V, GY * ROWS, T), F32),
         ],
         compiler_params=PARAMS,
         name="step",

time: 73.3 us -> 67.4 us (0.920)
  local copies, waits for them, and re-layouts: 3.61 us -> 0.39 us
  Pallas kernels: 13.6 us -> 11 us
    unnamed x12 -> x4, local copies, waits for them, and re-layouts: 3.22 us -> 0.01 us
    pallas_call x2, Pallas kernels: 9.57 us -> 6.55 us  [body(): step(meta, paired, own, swapped, arrived, band, row_mat, back_mat)]
where the time goes in v3:
time: 67.4 us; the launch traced here: 67.1 us
  waiting for transfers between devices  32 us (47%)
  starting transfers between devices  23.1 us (34%)
  Pallas kernels  11 us (16%)
    all_to_all x1, waiting for transfers between devices, body(): lax.all_to_all(joined, 'gy', split_axis=0, concat_axis=0, tiled=True)  12.2 us
    all_to_all x1, starting transfers between devices, body(): lax.all_to_all(joined, 'gy', split_axis=0, concat_axis=0, tiled=True)  7.86 us
    all_to_all x1, waiting for transfers between devices, body(): lax.all_to_all(own.reshape(GY, ROWS, T), 'gy', split_axis=0, concat_axis=...  6.8 us
    pallas_call x2, Pallas kernels, body(): step(meta, paired, own, swapped, arrived, band, row_mat, back_mat)  6.55 us
    ppermute x2, waiting for transfers between devices, body(): lax.ppermute(pair, AXES, PAIR)  5.85 us
    ppermute x2, waiting for transfers between devices, body(): paired = lax.ppermute(out, AXES, PAIR)  4.95 us
    ppermute x2, starting transfers between devices, body(): paired = lax.ppermute(out, AXES, PAIR)  4.45 us
    all_to_all x1, starting transfers between devices, body(): lax.all_to_all(own.reshape(GY, ROWS, T), 'gy', split_axis=0, concat_axis=...  3.51 us
  transfers between devices with their start and end apart: 12, of which 8 were waited for; matrix products, arithmetic and copies ran while one was open for 1% of the time, Pallas kernels for 1%

profile of v3, /device:TPU:1, one launch (start us, length us, event | category | flops | bytes accessed | tf_op | source)
XLA Modules:
  0.0 67.1 jit_solution(9569956191441172075)
XLA Ops:
  0.0 0.0 copy-start
  0.0 0.0 copy-start.1
  0.0 1.3 %pack.1 = (f32[8,88,128]{2,1,0:T(8,128)S(1)}, f32[8,88,128]{2,1,0:T(8,128)S(1)}) custom-call(s32[4,16]{1,0:T(4,128)} %bitcast.20, s32[4,16]{1,0:T(4,128)} %shifts_hbm.1, f32[2,128,128]{2,1,0:T(8,128)} %est_hbm.1, bf16[4,2,128,128]{3,2,1,0:T(8,128)(2,1)} %views_hbm.1), custom_call_target="tpu_custom_call" | custom-call | tf_op jit(solution)/shard_map/pack/pallas_call | solution.py:281
  1.3 1.5 %collective-permute-start = (f32[8,88,128]{2,1,0:T(8,128)S(1)}, f32[8,88,128]{2,1,0:T(8,128)S(1)}, u32[]{:S(2)}, u32[]{:S(2)}) collective-permute-start(f32[8,88,128]{2,1,0:T(8,128)S(1)} %get-tuple-element.17), channel_id=1, source_target_pairs={{0,16},{1,17},{2,18},{3,19},{4,20},{5,21},{6,22},{7,23},{8,24},{9,... | collective-permute-start | bytes 1081352 | tf_op jit(solution)/shard_map/ppermute | solution.py:301
  2.8 1.3 %collective-permute-done.other_ref = f32[8,88,128]{2,1,0:T(8,128)S(1)} collective-permute-done((f32[8,88,128]{2,1,0:T(8,128)S(1)}, f32[8,88,128]{2,1,0:T(8,128)S(1)}, u32[]{:S(2)}, u32[]{:S(2)}) %collective-permute-start) | collective-permute-done | bytes 360480 | tf_op jit(solution)/shard_map/ppermute | solution.py:301
  4.1 0.9 %join.1 = f32[16,88,128]{2,1,0:T(8,128)} custom-call(f32[8,88,128]{2,1,0:T(8,128)S(1)} %get-tuple-element.16.keep_ref, f32[8,88,128]{2,1,0:T(8,128)S(1)} %collective-permute-done.other_ref), custom_call_target="tpu_custom_call" | custom-call | tf_op jit(solution)/shard_map/join/pallas_call | solution.py:324
  5.0 7.9 %all-to-all-start = ((f32[16,88,128]{2,1,0:T(8,128)}), f32[16,88,128]{2,1,0:T(8,128)S(1)}, u32[]{:S(2)}, u32[]{:S(2)}) async-start(f32[16,88,128]{2,1,0:T(8,128)} %join.1), calls=%async_computation | async-start | bytes 1441792 | tf_op jit(solution)/shard_map/all_to_all | solution.py:333
  12.9 0.0 copy-done
  12.9 0.1 reduce_sum.18
  13.0 0.1 broadcast_divide_fusion.1
  13.1 0.1 rev.6
  13.2 0.0 copy-done.1
  13.2 0.1 reduce_sum.19
  13.3 0.1 broadcast_divide_fusion
  13.4 0.1 rev.7
  13.5 0.1 pad_bitcast_fusion
  13.6 12.2 %all-to-all-done.arrived_ref = f32[16,88,128]{2,1,0:T(8,128)S(1)} async-done(((f32[16,88,128]{2,1,0:T(8,128)}), f32[16,88,128]{2,1,0:T(8,128)S(1)}, u32[]{:S(2)}, u32[]{:S(2)}) %all-to-all-start) | async-done | bytes 720928 | tf_op jit(solution)/shard_map/all_to_all | solution.py:333
  25.8 2.9 %collective-permute-start.1 = (f32[272,128]{1,0:T(8,128)S(1)}, f32[272,128]{1,0:T(8,128)S(1)}, u32[]{:S(2)}, u32[]{:S(2)}) collective-permute-start(f32[272,128]{1,0:T(8,128)S(1)} %pad_maximum_fusion), channel_id=1, source_target_pairs={{20,5},{21,6},{22,7},{23,3},{19,2},{18,1},{17,0},{16,32},{48,33},{... | collective-permute-start | bytes 417800 | tf_op jit(solution)/shard_map/ppermute | solution.py:363
  28.7 0.0 collective-permute-start.2
  28.7 0.1 pad_bitcast_fusion.2
  28.8 0.9 %taps.1 = (bf16[4,2,512,256]{3,2,1,0:T(8,128)(2,1)S(1)}, bf16[4,32,96]{2,1,0:T(8,128)(2,1)S(1)}, bf16[4,48,48]{2,1,0:T(8,128)(2,1)S(1)}) custom-call(f32[8,256]{1,0:T(8,128)S(1)} %reshape.15.cols_ref, f32[8,128]{1,0:T(8,128)S(1)} %bitcast.17), custom_call_target="tpu_custom_call" | custom-call | tf_op jit(solution)/shard_map/taps/pallas_call | solution.py:311
  29.7 2.0 %collective-permute-done.1.paired_ref = f32[272,128]{1,0:T(8,128)S(1)} collective-permute-done((f32[272,128]{1,0:T(8,128)S(1)}, f32[272,128]{1,0:T(8,128)S(1)}, u32[]{:S(2)}, u32[]{:S(2)}) %collective-permute-start.1) | collective-permute-done | bytes 139296 | tf_op jit(solution)/shard_map/ppermute | solution.py:363
  31.7 0.0 collective-permute-done.2.swapped_ref
  31.7 3.3 %step.2 = (f32[256,128]{1,0:T(8,128)S(1)}, f32[256,128]{1,0:T(8,128)S(1)}, f32[256,128]{1,0:T(8,128)S(1)}) custom-call(s32[48,16]{1,0:T(8,128)S(1)} %maximum_convert_fusion.meta_ref, f32[272,128]{1,0:T(8,128)S(1)} %collective-permute-done.1.paired_ref, f32[256,128]{1,0:T(8,128)S(1)} %bitcast.15, f32[272,128]{1,0:T(8,128)S(1)} %collective-permute-done.2.swapped_ref, ...), custom_call_target="tpu_custom_call" | custom-call | tf_op jit(solution)/shard_map/step/pallas_call | solution.py:369
  35.0 1.5 %collective-permute-start.3 = (f32[256,128]{1,0:T(8,128)S(1)}, f32[256,128]{1,0:T(8,128)S(1)}, u32[]{:S(2)}, u32[]{:S(2)}) collective-permute-start(f32[256,128]{1,0:T(8,128)S(1)} %get-tuple-element.22), channel_id=1, source_target_pairs={{20,5},{21,6},{22,7},{23,3},{19,2},{18,1},{17,0},{16,32},{48,33},{... | collective-permute-start | bytes 393224 | tf_op jit(solution)/shard_map/ppermute | solution.py:370
  36.6 0.0 collective-permute-start.4
  36.6 2.9 %collective-permute-done.3.paired_ref = f32[256,128]{1,0:T(8,128)S(1)} collective-permute-done((f32[256,128]{1,0:T(8,128)S(1)}, f32[256,128]{1,0:T(8,128)S(1)}, u32[]{:S(2)}, u32[]{:S(2)}) %collective-permute-start.3) | collective-permute-done | bytes 131104 | tf_op jit(solution)/shard_map/ppermute | solution.py:370
  39.5 0.0 collective-permute-done.4.swapped_ref
  39.5 0.1 update.2.own_ref
  39.6 1.5 %collective-permute-start.5 = (f32[256,128]{1,0:T(8,128)S(1)}, f32[256,128]{1,0:T(8,128)S(1)}, u32[]{:S(2)}, u32[]{:S(2)}) collective-permute-start(f32[256,128]{1,0:T(8,128)S(1)} %update.2.own_ref), channel_id=1, source_target_pairs={{20,5},{21,6},{22,7},{23,3},{19,2},{18,1},{17,0},{16,32},{48,33},{... | collective-permute-start | bytes 393224 | tf_op jit(solution)/shard_map/ppermute | solution.py:363
  41.1 0.0 collective-permute-start.6
  41.1 2.9 %collective-permute-done.5.paired_ref = f32[256,128]{1,0:T(8,128)S(1)} collective-permute-done((f32[256,128]{1,0:T(8,128)S(1)}, f32[256,128]{1,0:T(8,128)S(1)}, u32[]{:S(2)}, u32[]{:S(2)}) %collective-permute-start.5) | collective-permute-done | bytes 131104 | tf_op jit(solution)/shard_map/ppermute | solution.py:363
  44.0 0.0 collective-permute-done.6.swapped_ref
  44.0 3.3 %step.3 = (f32[256,128]{1,0:T(8,128)S(1)}, f32[256,128]{1,0:T(8,128)S(1)}, f32[256,128]{1,0:T(8,128)S(1)}) custom-call(s32[48,16]{1,0:T(8,128)S(1)} %maximum_convert_fusion.meta_ref, f32[256,128]{1,0:T(8,128)S(1)} %collective-permute-done.5.paired_ref, f32[256,128]{1,0:T(8,128)S(1)} %update.2.own_ref, f32[256,128]{1,0:T(8,128)S(1)} %collective-permute-done.6.swapped_ref, ...), custom_call_target="tpu_custom_call" | custom-call | tf_op jit(solution)/shard_map/step/pallas_call | solution.py:369
  47.3 1.5 %collective-permute-start.7 = (f32[256,128]{1,0:T(8,128)S(1)}, f32[256,128]{1,0:T(8,128)S(1)}, u32[]{:S(2)}, u32[]{:S(2)}) collective-permute-start(f32[256,128]{1,0:T(8,128)S(1)} %get-tuple-element.25), channel_id=1, source_target_pairs={{20,5},{21,6},{22,7},{23,3},{19,2},{18,1},{17,0},{16,32},{48,33},{... | collective-permute-start | bytes 393224 | tf_op jit(solution)/shard_map/ppermute | solution.py:370
  48.9 0.0 collective-permute-start.8
  48.9 2.9 %collective-permute-done.7.paired_ref = f32[256,128]{1,0:T(8,128)S(1)} collective-permute-done((f32[256,128]{1,0:T(8,128)S(1)}, f32[256,128]{1,0:T(8,128)S(1)}, u32[]{:S(2)}, u32[]{:S(2)}) %collective-permute-start.7) | collective-permute-done | bytes 131104 | tf_op jit(solution)/shard_map/ppermute | solution.py:370
  51.8 0.0 collective-permute-done.8.swapped_ref
  51.8 0.7 %update.3 = f32[256,128]{1,0:T(8,128)} custom-call(f32[256,128]{1,0:T(8,128)S(1)} %update.2.own_ref, f32[256,128]{1,0:T(8,128)S(1)} %get-tuple-element.24.mid_ref, f32[256,128]{1,0:T(8,128)S(1)} %collective-permute-done.7.paired_ref, f32[256,128]{1,0:T(8,128)S(1)} %collective-permute-done.8.swapped_ref), custom_call_target="tpu_custom_call" | custom-call | tf_op jit(solution)/shard_map/update/pallas_call | solution.py:370
  52.5 3.5 %all-to-all-start.1 = ((f32[16,16,128]{2,1,0:T(8,128)}), f32[16,16,128]{2,1,0:T(8,128)S(1)}, u32[]{:S(2)}, u32[]{:S(2)}) async-start(f32[16,16,128]{2,1,0:T(8,128)} %bitcast.8), calls=%async_computation.1 | async-start | bytes 262144 | tf_op jit(solution)/shard_map/all_to_all | solution.py:371
  56.0 6.8 %all-to-all-done.1.home_ref = f32[16,16,128]{2,1,0:T(8,128)S(1)} async-done(((f32[16,16,128]{2,1,0:T(8,128)}), f32[16,16,128]{2,1,0:T(8,128)S(1)}, u32[]{:S(2)}, u32[]{:S(2)}) %all-to-all-start.1) | async-done | bytes 131104 | tf_op jit(solution)/shard_map/all_to_all | solution.py:371
  62.9 2.6 %collective-permute-start.9 = (f32[8,16,128]{2,1,0:T(8,128)S(1)}, f32[8,16,128]{2,1,0:T(8,128)S(1)}, u32[]{:S(2)}, u32[]{:S(2)}) collective-permute-start(f32[8,16,128]{2,1,0:T(8,128)S(1)} %slice_select_fusion), channel_id=1, source_target_pairs={{0,16},{1,17},{2,18},{3,19},{4,20},{5,21},{6,22},{7,23},{8,24},{9,... | collective-permute-start | bytes 196616 | tf_op jit(solution)/shard_map/ppermute | solution.py:375
  65.5 0.9 %collective-permute-done.9.got_ref = f32[8,16,128]{2,1,0:T(8,128)S(1)} collective-permute-done((f32[8,16,128]{2,1,0:T(8,128)S(1)}, f32[8,16,128]{2,1,0:T(8,128)S(1)}, u32[]{:S(2)}, u32[]{:S(2)}) %collective-permute-start.9) | collective-permute-done | bytes 65568 | tf_op jit(solution)/shard_map/ppermute | solution.py:375
  66.4 0.7 unpack.1
  (13 shorter events, 0.1 us)
Async XLA Ops:
  0.0 12.9 %copy-start = (f32[4,31]{1,0:T(4,128)S(1)}, f32[4,31]{1,0:T(4,128)}, u32[]{:S(2)}) copy-start(f32[4,31]{1,0:T(4,128)} %param.9) | copy-start | bytes 1492
  0.0 13.2 %copy-start.1 = (f32[4,31]{1,0:T(4,128)S(1)}, f32[4,31]{1,0:T(4,128)}, u32[]{:S(2)}) copy-start(f32[4,31]{1,0:T(4,128)} %param.8) | copy-start | bytes 1492
  1.3 2.8 %collective-permute-start = (f32[8,88,128]{2,1,0:T(8,128)S(1)}, f32[8,88,128]{2,1,0:T(8,128)S(1)}, u32[]{:S(2)}, u32[]{:S(2)}) collective-permute-start(f32[8,88,128]{2,1,0:T(8,128)S(1)} %get-tuple-element.17), channel_id=1, source_target_pairs={{0,16},{1,17},{2,18},{3,19},{4,20},{5,21},{6,22},{7,23},{8,24},{9,... | collective-permute-start | bytes 1081352 | tf_op jit(solution)/shard_map/ppermute | solution.py:301
  5.0 20.7 %all-to-all-start = ((f32[16,88,128]{2,1,0:T(8,128)}), f32[16,88,128]{2,1,0:T(8,128)S(1)}, u32[]{:S(2)}, u32[]{:S(2)}) async-start(f32[16,88,128]{2,1,0:T(8,128)} %join.1), calls=%async_computation | async-start | bytes 1441792 | tf_op jit(solution)/shard_map/all_to_all | solution.py:333
  25.8 5.9 %collective-permute-start.1 = (f32[272,128]{1,0:T(8,128)S(1)}, f32[272,128]{1,0:T(8,128)S(1)}, u32[]{:S(2)}, u32[]{:S(2)}) collective-permute-start(f32[272,128]{1,0:T(8,128)S(1)} %pad_maximum_fusion), channel_id=1, source_target_pairs={{20,5},{21,6},{22,7},{23,3},{19,2},{18,1},{17,0},{16,32},{48,33},{... | collective-permute-start | bytes 417800 | tf_op jit(solution)/shard_map/ppermute | solution.py:363
  28.7 3.0 %collective-permute-start.2 = (f32[272,128]{1,0:T(8,128)S(1)}, f32[272,128]{1,0:T(8,128)S(1)}, u32[]{:S(2)}, u32[]{:S(2)}) collective-permute-start(f32[272,128]{1,0:T(8,128)S(1)} %pad_maximum_fusion), channel_id=1, source_target_pairs={{0,16},{1,17},{2,18},{3,19},{4,20},{5,21},{6,22},{7,23},{8,24},{9,... | collective-permute-start | bytes 417800 | tf_op jit(solution)/shard_map/ppermute | solution.py:364
  35.0 4.5 %collective-permute-start.3 = (f32[256,128]{1,0:T(8,128)S(1)}, f32[256,128]{1,0:T(8,128)S(1)}, u32[]{:S(2)}, u32[]{:S(2)}) collective-permute-start(f32[256,128]{1,0:T(8,128)S(1)} %get-tuple-element.22), channel_id=1, source_target_pairs={{20,5},{21,6},{22,7},{23,3},{19,2},{18,1},{17,0},{16,32},{48,33},{... | collective-permute-start | bytes 393224 | tf_op jit(solution)/shard_map/ppermute | solution.py:370
  36.6 2.9 %collective-permute-start.4 = (f32[256,128]{1,0:T(8,128)S(1)}, f32[256,128]{1,0:T(8,128)S(1)}, u32[]{:S(2)}, u32[]{:S(2)}) collective-permute-start(f32[256,128]{1,0:T(8,128)S(1)} %get-tuple-element.23), channel_id=1, source_target_pairs={{0,16},{1,17},{2,18},{3,19},{4,20},{5,21},{6,22},{7,23},{8,24},{9,... | collective-permute-start | bytes 393224 | tf_op jit(solution)/shard_map/ppermute | solution.py:370
  39.6 4.5 %collective-permute-start.5 = (f32[256,128]{1,0:T(8,128)S(1)}, f32[256,128]{1,0:T(8,128)S(1)}, u32[]{:S(2)}, u32[]{:S(2)}) collective-permute-start(f32[256,128]{1,0:T(8,128)S(1)} %update.2.own_ref), channel_id=1, source_target_pairs={{20,5},{21,6},{22,7},{23,3},{19,2},{18,1},{17,0},{16,32},{48,33},{... | collective-permute-start | bytes 393224 | tf_op jit(solution)/shard_map/ppermute | solution.py:363
  41.1 2.9 %collective-permute-start.6 = (f32[256,128]{1,0:T(8,128)S(1)}, f32[256,128]{1,0:T(8,128)S(1)}, u32[]{:S(2)}, u32[]{:S(2)}) collective-permute-start(f32[256,128]{1,0:T(8,128)S(1)} %update.2.own_ref), channel_id=1, source_target_pairs={{0,16},{1,17},{2,18},{3,19},{4,20},{5,21},{6,22},{7,23},{8,24},{9,... | collective-permute-start | bytes 393224 | tf_op jit(solution)/shard_map/ppermute | solution.py:364
  47.3 4.5 %collective-permute-start.7 = (f32[256,128]{1,0:T(8,128)S(1)}, f32[256,128]{1,0:T(8,128)S(1)}, u32[]{:S(2)}, u32[]{:S(2)}) collective-permute-start(f32[256,128]{1,0:T(8,128)S(1)} %get-tuple-element.25), channel_id=1, source_target_pairs={{20,5},{21,6},{22,7},{23,3},{19,2},{18,1},{17,0},{16,32},{48,33},{... | collective-permute-start | bytes 393224 | tf_op jit(solution)/shard_map/ppermute | solution.py:370
  48.9 2.9 %collective-permute-start.8 = (f32[256,128]{1,0:T(8,128)S(1)}, f32[256,128]{1,0:T(8,128)S(1)}, u32[]{:S(2)}, u32[]{:S(2)}) collective-permute-start(f32[256,128]{1,0:T(8,128)S(1)} %get-tuple-element.26), channel_id=1, source_target_pairs={{0,16},{1,17},{2,18},{3,19},{4,20},{5,21},{6,22},{7,23},{8,24},{9,... | collective-permute-start | bytes 393224 | tf_op jit(solution)/shard_map/ppermute | solution.py:370
  52.5 10.4 %all-to-all-start.1 = ((f32[16,16,128]{2,1,0:T(8,128)}), f32[16,16,128]{2,1,0:T(8,128)S(1)}, u32[]{:S(2)}, u32[]{:S(2)}) async-start(f32[16,16,128]{2,1,0:T(8,128)} %bitcast.8), calls=%async_computation.1 | async-start | bytes 262144 | tf_op jit(solution)/shard_map/all_to_all | solution.py:371
  62.9 3.5 %collective-permute-start.9 = (f32[8,16,128]{2,1,0:T(8,128)S(1)}, f32[8,16,128]{2,1,0:T(8,128)S(1)}, u32[]{:S(2)}, u32[]{:S(2)}) collective-permute-start(f32[8,16,128]{2,1,0:T(8,128)S(1)} %slice_select_fusion), channel_id=1, source_target_pairs={{0,16},{1,17},{2,18},{3,19},{4,20},{5,21},{6,22},{7,23},{8,24},{9,... | collective-permute-start | bytes 196616 | tf_op jit(solution)/shard_map/ppermute | solution.py:375

commit v4 on v3

--- a/solution.py
+++ b/solution.py
@@ -19,6 +19,7 @@
 F32 = jnp.float32
 BF16 = jnp.bfloat16
 VMEM = pl.BlockSpec(memory_space=pltpu.VMEM)
+COST = pl.CostEstimate(flops=1_000_000_000, bytes_accessed=4_000_000, transcendentals=0)
 HBM = pl.BlockSpec(memory_space=pltpu.HBM)
 SMEM = pl.BlockSpec(memory_space=pltpu.SMEM)
 PARAMS = pltpu.CompilerParams(vmem_limit_bytes=48 * 1024 * 1024)
@@ -120,9 +121,13 @@
         copy.wait()
 
 
+def inside_kernel(paired_ref, out_ref):
+    _, has_pair = here()
+    out_ref[...] = paired_ref[...] * has_pair
+
+
 def update_kernel(own_ref, mid_ref, paired_ref, swapped_ref, out_ref):
-    _, has_pair = here()
-    total = mid_ref[...] + paired_ref[...] * has_pair + swapped_ref[...]
+    total = mid_ref[...] + paired_ref[...] + swapped_ref[...]
     out_ref[...] = own_ref[0 : GY * ROWS, :] * (total * 0.25)
 
 
@@ -137,7 +142,27 @@
             out_ref[plane, rows, :] = value
 
 
-def taps_kernel(cols_ref, rows_ref, band_ref, row_ref, back_ref):
+def put_split(ref, v, pieces, stacked=False):
+    axis = 0 if stacked else 1
+    hi = jnp.concatenate([p[0] for p in pieces], axis=axis)
+    lo = jnp.concatenate([p[1] for p in pieces], axis=axis)
+    ref[v] = jnp.concatenate(
+        [
+            jnp.concatenate([hi, hi], axis=1),
+            jnp.concatenate([lo, jnp.zeros_like(lo)], axis=1),
+        ],
+        axis=0,
+    )
+
+
+def taps_kernel(
+    cols_ref, rows_ref, band_ref, pair_in_ref, near_in_ref, pair_back_ref, near_back_ref
+):
+    core, _ = own_tile_inner()
+
+    def either(a, b):
+        return tuple(jnp.where(core == 0, x, y) for x, y in zip(a, b))
+
     def turned(base, count, width):
         rows = jnp.broadcast_to(base, (count, base.shape[1]))
         return split(pltpu.roll(rows, 0, 1, stride=1, stride_axis=0)[:, :width])
@@ -149,11 +174,16 @@
             band_ref[v, d, 0 : 2 * T, T : 2 * T] = lo
             band_ref[v, d, 2 * T : 4 * T, 0:T] = hi
             band_ref[v, d, 2 * T : 4 * T, T : 2 * T] = jnp.zeros_like(lo)
-        hi, lo = turned(rows_ref[2 * v : 2 * v + 1, :], ROWS, 3 * ROWS)
-        row_ref[v, 0:ROWS] = jnp.concatenate([hi, hi], axis=1)
-        row_ref[v, ROWS : 2 * ROWS] = jnp.concatenate([lo, jnp.zeros_like(lo)], axis=1)
-        hi, lo = turned(rows_ref[2 * v + 1 : 2 * v + 2, :], 3 * ROWS, ROWS)
-        back_ref[v] = jnp.concatenate([hi, hi, lo], axis=1)
+        before, own, after = [
+            turned(pltpu.roll(jnp.broadcast_to(rows_ref[2 * v : 2 * v + 1, :], (8, T)), (T - ROWS * i) % T, 1)[0:1], ROWS, ROWS) for i in range(3)
+        ]
+        put_split(pair_in_ref, v, [either(before, after)])
+        put_split(near_in_ref, v, [own, either(after, before)])
+        before, own, after = [
+            turned(pltpu.roll(jnp.broadcast_to(rows_ref[2 * v + 1 : 2 * v + 2, :], (8, T)), ROWS * i, 1)[0:1], ROWS, ROWS) for i in range(3)
+        ]
+        put_split(pair_back_ref, v, [either(before, after)], stacked=True)
+        put_split(near_back_ref, v, [own, either(after, before)], stacked=True)
 
 
 def column_pass(pieces, band):
@@ -177,57 +207,105 @@
     return [ref[v, :, T * c : T * c + T] for c in range(GY)]
 
 
-def step_kernel(
-    meta_ref, paired_ref, own_ref, swapped_ref, arrived_ref, band_ref, row_ref, back_ref,
-    pair_ref, mid_ref, swap_ref, est2, slope2, view_u, total2, smooth, ratio, again,
+def own_block(ref, half):
+    return ref[0 : GY * ROWS, :].reshape(GY, ROWS, T)[:, 8 * half : 8 * half + 8, :]
+
+
+def inner_lanes():
+    lane = lax.broadcasted_iota(jnp.int32, (8, T), 1)
+    return jnp.where(lane < T - 1, 1.0 / 16.0, 0.0).astype(F32)
+
+
+def put_twice(b, x, est2, slope2):
+    d = (pltpu.roll(x, T - 1, 2) - x) * inner_lanes()
+    for copy in range(2):
+        est2[b, GY * copy : GY * copy + GY] = x
+        slope2[b, GY * copy : GY * copy + GY] = d
+
+
+def code_of(meta_ref, v, b, c):
+    return meta_ref[GY * (b // 2) + c, b % 2 * V + v].astype(F32)
+
+
+def shift_of(meta_ref, v, b):
+    return meta_ref[GY * (b // 2), 8 + b % 2 * V + v]
+
+
+def gather(v, meta_ref, est2, slope2, view_u):
+    count = est2.shape[0] // 2
+    for src in range(count):
+        parts = []
+        for b in (2 * src, 2 * src + 1):
+            shift = shift_of(meta_ref, v, b)
+            x = est2[b, pl.ds(shift, GY)]
+            d = slope2[b, pl.ds(shift, GY)]
+            parts.append([x[c] + code_of(meta_ref, v, b, c) * d[c] for c in range(GY)])
+        for c in range(GY):
+            hi, lo = split(jnp.concatenate([parts[0][c], parts[1][c]], axis=0))
+            cols = slice(T * c, T * c + T)
+            view_u[v, ROWS * src : ROWS * src + ROWS, cols] = hi
+            view_u[v, ROWS * (count + src) : ROWS * (count + src + 1), cols] = lo
+
+
+def product(weights, values):
+    both = jnp.dot(weights, values, preferred_element_type=F32)
+    return both[: both.shape[0] // 2] + both[both.shape[0] // 2 :]
+
+
+def rows_back(v, meta_ref, back_ref, again, total2):
+    his, los = zip(*[split(again[v, ROWS * c : ROWS * c + ROWS, :]) for c in range(GY)])
+    values = jnp.concatenate(
+        [jnp.concatenate(his, axis=1), jnp.concatenate(los, axis=1)], axis=0
+    )
+    spread = product(back_ref[v], values)
+    inner = inner_lanes()
+    for b in range(total2.shape[0]):
+        parts = []
+        for c in range(GY):
+            r = spread[8 * b : 8 * b + 8, T * c : T * c + T]
+            g = r * inner
+            g = pltpu.roll(g, 1, 1) - g
+            parts.append(r + code_of(meta_ref, v, b, c) * g)
+        total2[b, pl.ds(shift_of(meta_ref, v, b), GY)] += jnp.stack(parts)
+
+
+def put_joined(ref, src, total2):
+    for half in range(2):
+        b = 2 * src + half
+        y = total2[b, 0:GY] + total2[b, GY : 2 * GY]
+        for c in range(GY):
+            ref[ROWS * c + 8 * half : ROWS * c + 8 * half + 8, :] = y[c]
+
+
+def in_turn(stages):
+    for turn in range(V + len(stages) - 1):
+        for i, stage in enumerate(stages):
+            if 0 <= turn - i < V:
+                stage(turn - i)
+
+
+def front_kernel(meta_ref, own_ref, swapped_ref, near_in_ref, smooth_ref, est2, slope2, view_u):
+    for src, ref in enumerate((own_ref, swapped_ref)):
+        for half in range(2):
+            put_twice(2 * src + half, own_block(ref, half), est2, slope2)
+
+    def rows_in(v):
+        smooth_ref[v] = product(near_in_ref[v], view_u[v])
+
+    in_turn((lambda v: gather(v, meta_ref, est2, slope2, view_u), rows_in))
+
+
+def core_kernel(
+    meta_ref, paired_ref, near_ref, arrived_ref, band_ref, pair_in_ref, pair_back_ref,
+    pair_ref, again_ref, est2, slope2, view_u, total2, smooth, ratio,
 ):
-    core, has_pair = here()
-    first = core == 0
-    bases = (jnp.where(first, 0, 2 * GY), GY, jnp.where(first, 2 * GY, 0))
-
-    def own_block(ref, half):
-        return ref[0 : GY * ROWS, :].reshape(GY, ROWS, T)[:, 8 * half : 8 * half + 8, :]
-
-    def code_of(v, src, half, c):
-        return meta_ref[bases[src] + c, half * V + v].astype(F32)
-
-    def shift_of(v, src, half):
-        return meta_ref[bases[src], 8 + half * V + v]
-
-    lane = lax.broadcasted_iota(jnp.int32, (GY, 8, T), 2)
-    inner = jnp.where(lane < T - 1, 1.0 / 16.0, 0.0).astype(F32)
-    inner8 = inner[0]
+    _, has_pair = here()
     for half in range(2):
-        paired = own_block(paired_ref, half) * has_pair
-        swapped = own_block(swapped_ref, half)
-        before, after = jnp.where(first, paired, swapped), jnp.where(first, swapped, paired)
-        for src, x in enumerate((before, own_block(own_ref, half), after)):
-            b = 2 * src + half
-            d = (pltpu.roll(x, T - 1, 2) - x) * inner
-            est2[b, 0:GY] = x
-            est2[b, GY : 2 * GY] = x
-            slope2[b, 0:GY] = d
-            slope2[b, GY : 2 * GY] = d
+        put_twice(half, own_block(paired_ref, half) * has_pair, est2, slope2)
     total2[...] = jnp.zeros(total2.shape, F32)
 
-    def gather(v):
-        for src in range(3):
-            parts = []
-            for half in range(2):
-                b = 2 * src + half
-                shift = shift_of(v, src, half)
-                x = est2[b, pl.ds(shift, GY)]
-                d = slope2[b, pl.ds(shift, GY)]
-                parts.append([x[c] + code_of(v, src, half, c) * d[c] for c in range(GY)])
-            for c in range(GY):
-                hi, lo = split(jnp.concatenate([parts[0][c], parts[1][c]], axis=0))
-                cols = slice(T * c, T * c + T)
-                view_u[v, ROWS * src : ROWS * src + ROWS, cols] = hi
-                view_u[v, ROWS * (3 + src) : ROWS * (4 + src), cols] = lo
-
     def rows_in(v):
-        both = jnp.dot(row_ref[v], view_u[v], preferred_element_type=F32)
-        smooth[v] = both[:ROWS] + both[ROWS:]
+        smooth[v] = near_ref[v] + product(pair_in_ref[v], view_u[v])
 
     def cols_in(v):
         blurred = column_pass(column_tiles(smooth, v), band_ref[v, 0])
@@ -238,37 +316,24 @@
             )
 
     def cols_back(v):
-        again[v] = column_pass(column_tiles(ratio, v), band_ref[v, 1])
-
-    def rows_back(v):
-        his, los = zip(*[split(again[v, ROWS * c : ROWS * c + ROWS, :]) for c in range(GY)])
-        hi, lo = jnp.concatenate(his, axis=1), jnp.concatenate(los, axis=1)
-        spread = jnp.dot(
-            back_ref[v], jnp.concatenate([hi, lo, hi], axis=0), preferred_element_type=F32
-        )
-        for b in range(6):
-            src, half = b // 2, b % 2
-            parts = []
-            for c in range(GY):
-                r = spread[8 * b : 8 * b + 8, T * c : T * c + T]
-                g = r * inner8
-                g = pltpu.roll(g, 1, 1) - g
-                parts.append(r + code_of(v, src, half, c) * g)
-            total2[b, pl.ds(shift_of(v, src, half), GY)] += jnp.stack(parts)
-
-    stages = (gather, rows_in, cols_in, cols_back, rows_back)
-    for turn in range(V + len(stages) - 1):
-        for i, stage in enumerate(stages):
-            if 0 <= turn - i < V:
-                stage(turn - i)
-    for half in range(2):
-        low, mid, high = [
-            total2[2 * src + half, 0:GY] + total2[2 * src + half, GY : 2 * GY] for src in range(3)
-        ]
-        pair, swap = jnp.where(first, low, high), jnp.where(first, high, low)
-        for ref, y in ((pair_ref, pair), (mid_ref, mid), (swap_ref, swap)):
-            for c in range(GY):
-                ref[ROWS * c + 8 * half : ROWS * c + 8 * half + 8, :] = y[c]
+        again_ref[v] = column_pass(column_tiles(ratio, v), band_ref[v, 1])
+
+    in_turn((
+        lambda v: gather(v, meta_ref, est2, slope2, view_u),
+        rows_in,
+        cols_in,
+        cols_back,
+        lambda v: rows_back(v, meta_ref, pair_back_ref, again_ref, total2),
+    ))
+    put_joined(pair_ref, 0, total2)
+
+
+def tail_kernel(meta_ref, again_ref, near_back_ref, mid_ref, swap_ref, total2):
+    total2[...] = jnp.zeros(total2.shape, F32)
+    for v in range(V):
+        rows_back(v, meta_ref, near_back_ref, again_ref, total2)
+    put_joined(mid_ref, 0, total2)
+    put_joined(swap_ref, 1, total2)
 
 
 def place(taps, at, width):
@@ -308,16 +373,19 @@
     row_base = jnp.stack(
         [place(rows_n, 1, T), place(rows_n[:, ::-1], T - 31, T)], axis=1
     ).reshape(2 * V, T)
-    band, row_mat, back_mat = pl.pallas_call(
+    band, pair_in, near_in, pair_back, near_back = pl.pallas_call(
         taps_kernel,
         out_shape=(
             jax.ShapeDtypeStruct((V, 2, 4 * T, 2 * T), BF16),
-            jax.ShapeDtypeStruct((V, 2 * ROWS, 6 * ROWS), BF16),
-            jax.ShapeDtypeStruct((V, 3 * ROWS, 3 * ROWS), BF16),
+            jax.ShapeDtypeStruct((V, 2 * ROWS, 2 * ROWS), BF16),
+            jax.ShapeDtypeStruct((V, 2 * ROWS, 4 * ROWS), BF16),
+            jax.ShapeDtypeStruct((V, 2 * ROWS, 2 * ROWS), BF16),
+            jax.ShapeDtypeStruct((V, 4 * ROWS, 2 * ROWS), BF16),
         ),
         in_specs=[VMEM, VMEM],
-        out_specs=(VMEM, VMEM, VMEM),
-        compiler_params=PARAMS,
+        out_specs=(VMEM,) * 5,
+        compiler_params=PARAMS,
+        cost_estimate=COST,
         name="taps",
     )(col_base, row_base)
 
@@ -332,7 +400,7 @@
     )(keep, other)
     arrived = lax.all_to_all(joined, "gy", split_axis=0, concat_axis=0, tiled=True)
     own = arrived[:, :ROWS, :].reshape(GY * ROWS, T)
-    own_meta = arrived[:, ROWS * (1 + V), :]
+    own_meta = arrived[:, ROWS * (1 + V), :] + 0.0 * band[0, 0, :GY, :T].astype(F32)
     update = pl.pallas_call(
         update_kernel,
         out_shape=jax.ShapeDtypeStruct((GY * ROWS, T), F32),
@@ -341,33 +409,70 @@
         compiler_params=PARAMS,
         name="update",
     )
-    step = pl.pallas_call(
-        step_kernel,
-        out_shape=(jax.ShapeDtypeStruct((GY * ROWS, T), F32),) * 3,
-        in_specs=[SMEM] + [VMEM] * 7,
-        out_specs=(VMEM,) * 3,
+    chunk = jax.ShapeDtypeStruct((GY * ROWS, T), F32)
+    inside = pl.pallas_call(
+        inside_kernel,
+        out_shape=chunk,
+        in_specs=[VMEM],
+        out_specs=VMEM,
+        compiler_params=PARAMS,
+        cost_estimate=COST,
+        name="inside",
+    )
+    doubled = [pltpu.VMEM((b, 2 * GY, 8, T), F32) for b in (2, 4)]
+    front = pl.pallas_call(
+        front_kernel,
+        out_shape=jax.ShapeDtypeStruct((V, ROWS, GY * T), F32),
+        in_specs=[SMEM] + [VMEM] * 3,
+        out_specs=VMEM,
+        scratch_shapes=[doubled[1], doubled[1], pltpu.VMEM((V, 4 * ROWS, GY * T), BF16)],
+        compiler_params=PARAMS,
+        cost_estimate=COST,
+        name="front",
+    )
+    middle = pl.pallas_call(
+        core_kernel,
+        out_shape=(chunk, jax.ShapeDtypeStruct((V, GY * ROWS, T), F32)),
+        in_specs=[SMEM] + [VMEM] * 6,
+        out_specs=(VMEM, VMEM),
         scratch_shapes=[
-            pltpu.VMEM((6, 2 * GY, 8, T), F32),
-            pltpu.VMEM((6, 2 * GY, 8, T), F32),
-            pltpu.VMEM((V, 6 * ROWS, GY * T), BF16),
-            pltpu.VMEM((6, 2 * GY, 8, T), F32),
+            doubled[0],
+            doubled[0],
+            pltpu.VMEM((V, 2 * ROWS, GY * T), BF16),
+            doubled[0],
             pltpu.VMEM((V, ROWS, GY * T), F32),
             pltpu.VMEM((V, ROWS, GY * T), F32),
-            pltpu.VMEM((V, GY * ROWS, T), F32),
         ],
         compiler_params=PARAMS,
-        name="step",
+        cost_estimate=COST,
+        name="middle",
+    )
+    tail = pl.pallas_call(
+        tail_kernel,
+        out_shape=(chunk, chunk),
+        in_specs=[SMEM] + [VMEM] * 2,
+        out_specs=(VMEM, VMEM),
+        scratch_shapes=[doubled[1]],
+        compiler_params=PARAMS,
+        cost_estimate=COST,
+        name="tail",
     )
     for sweep in range(ITERS):
         out = jnp.concatenate([own, own_meta], axis=0) if sweep == 0 else own
         paired = lax.ppermute(out, AXES, PAIR)
         swapped = lax.ppermute(out, AXES, SWAP)
         if sweep == 0:
-            meta = jnp.concatenate(
-                [paired[GY * ROWS :, :META], own_meta[:, :META], swapped[GY * ROWS :, :META]], axis=0
+            near_meta = jnp.concatenate(
+                [own_meta[:, :META], swapped[GY * ROWS :, :META]], axis=0
             ).astype(jnp.int32)
-        pair, mid, swap = step(meta, paired, own, swapped, arrived, band, row_mat, back_mat)
-        own = update(own, mid, lax.ppermute(pair, AXES, PAIR), lax.ppermute(swap, AXES, SWAP))
+        near = front(near_meta, own, swapped, near_in)
+        if sweep == 0:
+            pair_meta = (paired[GY * ROWS :, :META] + 0.0 * near[0, :, :META]).astype(jnp.int32)
+        pair, again = middle(pair_meta, paired, near, arrived, band, pair_in, pair_back)
+        mid, swap = tail(near_meta, again, near_back)
+        own = update(
+            own, mid, inside(lax.ppermute(pair, AXES, PAIR)), lax.ppermute(swap, AXES, SWAP)
+        )
     home = lax.all_to_all(
         own.reshape(GY, ROWS, T), "gy", split_axis=0, concat_axis=0, tiled=True
     )

time: 67.4 us -> 66.3 us (0.984)
  waiting for transfers between devices: 32 us -> 25.5 us
  Pallas kernels: 11 us -> 15.6 us
  other arithmetic: 0.43 us -> 1.81 us
  starting transfers between devices: 23.1 us -> 22.4 us
    pallas_call x4 -> x10, Pallas kernels: 7.29 us -> 11.4 us  [the longest x2 4.83 us: body(): middle(pair_meta, paired, near, arrived, band, pair_in, pair_back)]
    ppermute x2, waiting for transfers between devices: 5.85 us -> 3.17 us  [body(): lax.ppermute(pair, AXES, PAIR)]
    ppermute x2, starting transfers between devices: 4.45 us -> 2.65 us  [body(): paired = lax.ppermute(out, AXES, PAIR)]
    ppermute x2, waiting for transfers between devices: 4.95 us -> 3.22 us  [body(): paired = lax.ppermute(out, AXES, PAIR)]
    ppermute x2, starting transfers between devices: 0.01 us -> 1.63 us  [body(): swapped = lax.ppermute(out, AXES, SWAP)]
    ppermute x1, waiting for transfers between devices: 1.3 us -> 0.01 us  [body(): other = lax.ppermute(send, AXES, SWAP)]
    all_to_all x1, waiting for transfers between devices: 12.2 us -> 11.3 us  [body(): lax.all_to_all(joined, 'gy', split_axis=0, concat_axis=0, tiled=True)]
    reduce_sum x1, other arithmetic: 0.12 us -> 0.8 us  [body(): cols_n = psf_cols / jnp.sum(psf_cols, axis=1, keepdims=True)]
  transfers between devices with their start and end apart: 12 -> 12, of which waited for: 8 -> 7; matrix products, arithmetic and copies ran while one was open for 1% -> 3% of each run, Pallas kernels for 1% -> 11%
where the time goes in v4:
time: 66.3 us; the launch traced here: 65.9 us
  waiting for transfers between devices  25.5 us (38%)
  starting transfers between devices  22.4 us (34%)
  Pallas kernels  15.6 us (24%)
  other arithmetic  1.81 us (3%)
    all_to_all x1, waiting for transfers between devices, body(): lax.all_to_all(joined, 'gy', split_axis=0, concat_axis=0, tiled=True)  11.3 us
    all_to_all x1, starting transfers between devices, body(): lax.all_to_all(joined, 'gy', split_axis=0, concat_axis=0, tiled=True)  7.86 us
    all_to_all x1, waiting for transfers between devices, body(): lax.all_to_all(own.reshape(GY, ROWS, T), 'gy', split_axis=0, concat_axis=...  6.83 us
    pallas_call x2, Pallas kernels, body(): middle(pair_meta, paired, near, arrived, band, pair_in, pair_back)  4.83 us
    all_to_all x1, starting transfers between devices, body(): lax.all_to_all(own.reshape(GY, ROWS, T), 'gy', split_axis=0, concat_axis=...  3.65 us
    ppermute x2, waiting for transfers between devices, body(): paired = lax.ppermute(out, AXES, PAIR)  3.22 us
    ppermute x2, waiting for transfers between devices, body(): lax.ppermute(pair, AXES, PAIR)  3.17 us
    pallas_call x2, Pallas kernels, body(): near = front(near_meta, own, swapped, near_in)  3.01 us
  transfers between devices with their start and end apart: 12, of which 7 were waited for; matrix products, arithmetic and copies ran while one was open for 3% of the time, Pallas kernels for 11%

profile of v4, /device:TPU:1, one launch (start us, length us, event | category | flops | bytes accessed | tf_op | source)
XLA Modules:
  0.0 65.9 jit_solution(12140792353901581876)
XLA Ops:
  0.0 0.0 copy-start
  0.0 1.3 %pack.1 = (f32[8,88,128]{2,1,0:T(8,128)S(1)}, f32[8,88,128]{2,1,0:T(8,128)S(1)}) custom-call(s32[4,16]{1,0:T(4,128)} %bitcast.30, s32[4,16]{1,0:T(4,128)} %shifts_hbm.1, f32[2,128,128]{2,1,0:T(8,128)} %est_hbm.1, bf16[4,2,128,128]{3,2,1,0:T(8,128)(2,1)} %views_hbm.1), custom_call_target="tpu_custom_call" | custom-call | tf_op jit(solution)/shard_map/pack/pallas_call | solution.py:346
  1.3 1.5 %collective-permute-start = (f32[8,88,128]{2,1,0:T(8,128)S(1)}, f32[8,88,128]{2,1,0:T(8,128)S(1)}, u32[]{:S(2)}, u32[]{:S(2)}) collective-permute-start(f32[8,88,128]{2,1,0:T(8,128)S(1)} %get-tuple-element.21), channel_id=1, source_target_pairs={{0,16},{1,17},{2,18},{3,19},{4,20},{5,21},{6,22},{7,23},{8,24},{9,... | collective-permute-start | bytes 1081352 | tf_op jit(solution)/shard_map/ppermute | solution.py:366
  2.8 0.8 %reduce_sum.18 = f32[4]{0:T(128)S(1)} reduce(f32[4,31]{1,0:T(4,128)} %param.9, f32[]{:T(128)} %constant.33.clone.1), dimensions={1}, to_apply=%region_0.1 | reduce | flops 120 | bytes 516 | tf_op jit(solution)/shard_map/reduce_sum | solution.py:369
  3.6 0.8 %broadcast_divide_fusion.1 = f32[4,31]{1,0:T(4,128)S(1)} fusion(f32[4,31]{1,0:T(4,128)} %param.9, f32[4]{0:T(128)S(1)} %reduce_sum.18), kind=kLoop, calls=%fused_computation.15 | loop fusion | flops 124 | bytes 1008 | tf_op jit(solution)/shard_map/div | solution.py:369
  4.4 0.1 rev.6
  4.4 0.0 collective-permute-done.other_ref
  4.5 0.9 %join.1 = f32[16,88,128]{2,1,0:T(8,128)} custom-call(f32[8,88,128]{2,1,0:T(8,128)S(1)} %get-tuple-element.20.keep_ref, f32[8,88,128]{2,1,0:T(8,128)S(1)} %collective-permute-done.other_ref), custom_call_target="tpu_custom_call" | custom-call | tf_op jit(solution)/shard_map/join/pallas_call | solution.py:392
  5.4 7.9 %all-to-all-start = ((f32[16,88,128]{2,1,0:T(8,128)}), f32[16,88,128]{2,1,0:T(8,128)S(1)}, u32[]{:S(2)}, u32[]{:S(2)}) async-start(f32[16,88,128]{2,1,0:T(8,128)} %join.1), calls=%async_computation | async-start | bytes 1441792 | tf_op jit(solution)/shard_map/all_to_all | solution.py:401
  13.3 0.1 pad_bitcast_fusion
  13.4 0.0 copy-done
  13.4 0.1 reduce_sum.19
  13.5 0.1 broadcast_divide_fusion
  13.6 0.1 rev.7
  13.7 0.1 pad_bitcast_fusion.2
  13.8 1.4 %taps.1 = (bf16[4,2,512,256]{3,2,1,0:T(8,128)(2,1)S(1)}, bf16[4,32,32]{2,1,0:T(8,128)(2,1)S(1)}, bf16[4,32,64]{2,1,0:T(8,128)(2,1)S(1)}, bf16[4,32,32]{2,1,0:T(8,128)(2,1)S(1)}, bf16[4,64,32]{2,1,0:T(8,128)(2,1)S(1)}) custom-call(f32[8,256]{1,0:T(8,128)S(1)} %reshape.20.cols_ref, f32[8,128]{1,0:T(8,128)S(1)} %bitcast.27), custom_call_target="tpu_custom_call" | custom-call | flops 1000000000 | bytes 4000000 | tf_op jit(solution)/shard_map/taps/pallas_call | solution.py:376
  15.1 11.3 %all-to-all-done.arrived_ref = f32[16,88,128]{2,1,0:T(8,128)S(1)} async-done(((f32[16,88,128]{2,1,0:T(8,128)}), f32[16,88,128]{2,1,0:T(8,128)S(1)}, u32[]{:S(2)}, u32[]{:S(2)}) %all-to-all-start) | async-done | bytes 720928 | tf_op jit(solution)/shard_map/all_to_all | solution.py:401
  26.5 1.5 %collective-permute-start.1 = (f32[272,128]{1,0:T(8,128)S(1)}, f32[272,128]{1,0:T(8,128)S(1)}, u32[]{:S(2)}, u32[]{:S(2)}) collective-permute-start(f32[272,128]{1,0:T(8,128)S(1)} %pad_maximum_fusion), channel_id=1, source_target_pairs={{0,16},{1,17},{2,18},{3,19},{4,20},{5,21},{6,22},{7,23},{8,24},{9,... | collective-permute-start | bytes 417800 | tf_op jit(solution)/shard_map/ppermute | solution.py:463
  28.0 1.2 %collective-permute-start.2 = (f32[272,128]{1,0:T(8,128)S(1)}, f32[272,128]{1,0:T(8,128)S(1)}, u32[]{:S(2)}, u32[]{:S(2)}) collective-permute-start(f32[272,128]{1,0:T(8,128)S(1)} %pad_maximum_fusion), channel_id=1, source_target_pairs={{20,5},{21,6},{22,7},{23,3},{19,2},{18,1},{17,0},{16,32},{48,33},{... | collective-permute-start | bytes 417800 | tf_op jit(solution)/shard_map/ppermute | solution.py:462
  29.1 0.0 collective-permute-done.1.swapped_ref
  29.2 1.5 %front.2.near_ref = f32[4,16,2048]{2,1,0:T(8,128)S(1)} custom-call(s32[32,16]{1,0:T(8,128)S(1)} %maximum_convert_fusion.meta_ref, f32[256,128]{1,0:T(8,128)S(1)} %bitcast.25, f32[272,128]{1,0:T(8,128)S(1)} %collective-permute-done.1.swapped_ref, bf16[4,32,64]{2,1,0:T(8,128)(2,1)S(1)} %get-tuple-element.23.near_in_ref), custom_call_target="tpu_custom_call" | custom-call | flops 1000000000 | bytes 4000000 | tf_op jit(solution)/shard_map/front/pallas_call | solution.py:468
  30.7 1.8 %collective-permute-done.2.paired_ref = f32[272,128]{1,0:T(8,128)S(1)} collective-permute-done((f32[272,128]{1,0:T(8,128)S(1)}, f32[272,128]{1,0:T(8,128)S(1)}, u32[]{:S(2)}, u32[]{:S(2)}) %collective-permute-start.2) | collective-permute-done | bytes 139296 | tf_op jit(solution)/shard_map/ppermute | solution.py:462
  32.5 2.4 %middle.2 = (f32[256,128]{1,0:T(8,128)S(1)}, f32[4,256,128]{2,1,0:T(8,128)S(1)}) custom-call(s32[16,16]{1,0:T(8,128)S(1)} %fusion.2.meta_ref, f32[272,128]{1,0:T(8,128)S(1)} %collective-permute-done.2.paired_ref, f32[4,16,2048]{2,1,0:T(8,128)S(1)} %front.2.near_ref, f32[16,88,128]{2,1,0:T(8,128)S(1)} %all-to-all-done.arrived_ref, ...), custom_call_target="tpu_custom_call" | custom-call | flops 1000000000 | bytes 4000000 | tf_op jit(solution)/shard_map/middle/pallas_call | solution.py:471
  34.9 1.2 %collective-permute-start.3 = (f32[256,128]{1,0:T(8,128)S(1)}, f32[256,128]{1,0:T(8,128)S(1)}, u32[]{:S(2)}, u32[]{:S(2)}) collective-permute-start(f32[256,128]{1,0:T(8,128)S(1)} %get-tuple-element.29), channel_id=1, source_target_pairs={{20,5},{21,6},{22,7},{23,3},{19,2},{18,1},{17,0},{16,32},{48,33},{... | collective-permute-start | bytes 393224 | tf_op jit(solution)/shard_map/ppermute | solution.py:474
  36.1 1.4 %tail.2 = (f32[256,128]{1,0:T(8,128)S(1)}, f32[256,128]{1,0:T(8,128)S(1)}) custom-call(s32[32,16]{1,0:T(8,128)S(1)} %maximum_convert_fusion.meta_ref, f32[4,256,128]{2,1,0:T(8,128)S(1)} %get-tuple-element.26.again_ref, bf16[4,64,32]{2,1,0:T(8,128)(2,1)S(1)} %get-tuple-element.27.near_back_ref), custom_call_target="tpu_custom_call" | custom-call | flops 1000000000 | bytes 4000000 | tf_op jit(solution)/shard_map/tail/pallas_call | solution.py:472
  37.5 0.1 collective-permute-start.4
  37.6 1.7 %collective-permute-done.3.paired_ref = f32[256,128]{1,0:T(8,128)S(1)} collective-permute-done((f32[256,128]{1,0:T(8,128)S(1)}, f32[256,128]{1,0:T(8,128)S(1)}, u32[]{:S(2)}, u32[]{:S(2)}) %collective-permute-start.3) | collective-permute-done | bytes 131104 | tf_op jit(solution)/shard_map/ppermute | solution.py:474
  39.4 0.0 collective-permute-done.4.swapped_ref
  39.4 0.2 collective-permute-start.6
  39.6 1.5 %collective-permute-start.5 = (f32[256,128]{1,0:T(8,128)S(1)}, f32[256,128]{1,0:T(8,128)S(1)}, u32[]{:S(2)}, u32[]{:S(2)}) collective-permute-start(f32[256,128]{1,0:T(8,128)S(1)} %update.2.own_ref), channel_id=1, source_target_pairs={{20,5},{21,6},{22,7},{23,3},{19,2},{18,1},{17,0},{16,32},{48,33},{... | collective-permute-start | bytes 393224 | tf_op jit(solution)/shard_map/ppermute | solution.py:462
  41.1 0.0 collective-permute-done.6.swapped_ref
  41.1 1.5 %front.3.near_ref = f32[4,16,2048]{2,1,0:T(8,128)S(1)} custom-call(s32[32,16]{1,0:T(8,128)S(1)} %maximum_convert_fusion.meta_ref, f32[256,128]{1,0:T(8,128)S(1)} %update.2.own_ref, f32[256,128]{1,0:T(8,128)S(1)} %collective-permute-done.6.swapped_ref, bf16[4,32,64]{2,1,0:T(8,128)(2,1)S(1)} %get-tuple-element.23.near_in_ref), custom_call_target="tpu_custom_call" | custom-call | flops 1000000000 | bytes 4000000 | tf_op jit(solution)/shard_map/front/pallas_call | solution.py:468
  42.6 1.4 %collective-permute-done.5.paired_ref = f32[256,128]{1,0:T(8,128)S(1)} collective-permute-done((f32[256,128]{1,0:T(8,128)S(1)}, f32[256,128]{1,0:T(8,128)S(1)}, u32[]{:S(2)}, u32[]{:S(2)}) %collective-permute-start.5) | collective-permute-done | bytes 131104 | tf_op jit(solution)/shard_map/ppermute | solution.py:462
  44.0 2.4 %middle.3 = (f32[256,128]{1,0:T(8,128)S(1)}, f32[4,256,128]{2,1,0:T(8,128)S(1)}) custom-call(s32[16,16]{1,0:T(8,128)S(1)} %fusion.2.meta_ref, f32[256,128]{1,0:T(8,128)S(1)} %collective-permute-done.5.paired_ref, f32[4,16,2048]{2,1,0:T(8,128)S(1)} %front.3.near_ref, f32[16,88,128]{2,1,0:T(8,128)S(1)} %all-to-all-done.arrived_ref, ...), custom_call_target="tpu_custom_call" | custom-call | flops 1000000000 | bytes 4000000 | tf_op jit(solution)/shard_map/middle/pallas_call | solution.py:471
  46.4 1.5 %collective-permute-start.7 = (f32[256,128]{1,0:T(8,128)S(1)}, f32[256,128]{1,0:T(8,128)S(1)}, u32[]{:S(2)}, u32[]{:S(2)}) collective-permute-start(f32[256,128]{1,0:T(8,128)S(1)} %get-tuple-element.33), channel_id=1, source_target_pairs={{20,5},{21,6},{22,7},{23,3},{19,2},{18,1},{17,0},{16,32},{48,33},{... | collective-permute-start | bytes 393224 | tf_op jit(solution)/shard_map/ppermute | solution.py:474
  48.0 1.4 %tail.3 = (f32[256,128]{1,0:T(8,128)S(1)}, f32[256,128]{1,0:T(8,128)S(1)}) custom-call(s32[32,16]{1,0:T(8,128)S(1)} %maximum_convert_fusion.meta_ref, f32[4,256,128]{2,1,0:T(8,128)S(1)} %get-tuple-element.31.again_ref, bf16[4,64,32]{2,1,0:T(8,128)(2,1)S(1)} %get-tuple-element.27.near_back_ref), custom_call_target="tpu_custom_call" | custom-call | flops 1000000000 | bytes 4000000 | tf_op jit(solution)/shard_map/tail/pallas_call | solution.py:472
  49.4 0.1 collective-permute-start.8
  49.5 1.4 %collective-permute-done.7.paired_ref = f32[256,128]{1,0:T(8,128)S(1)} collective-permute-done((f32[256,128]{1,0:T(8,128)S(1)}, f32[256,128]{1,0:T(8,128)S(1)}, u32[]{:S(2)}, u32[]{:S(2)}) %collective-permute-start.7) | collective-permute-done | bytes 131104 | tf_op jit(solution)/shard_map/ppermute | solution.py:474
  50.9 0.0 collective-permute-done.8.swapped_ref
  50.9 0.7 %update.3 = f32[256,128]{1,0:T(8,128)} custom-call(f32[256,128]{1,0:T(8,128)S(1)} %update.2.own_ref, f32[256,128]{1,0:T(8,128)S(1)} %get-tuple-element.32.mid_ref, f32[256,128]{1,0:T(8,128)S(1)} %inside.3.paired_ref, f32[256,128]{1,0:T(8,128)S(1)} %collective-permute-done.8.swapped_ref), custom_call_target="tpu_custom_call" | custom-call | tf_op jit(solution)/shard_map/update/pallas_call | solution.py:473
  51.6 3.6 %all-to-all-start.1 = ((f32[16,16,128]{2,1,0:T(8,128)}), f32[16,16,128]{2,1,0:T(8,128)S(1)}, u32[]{:S(2)}, u32[]{:S(2)}) async-start(f32[16,16,128]{2,1,0:T(8,128)} %bitcast.10), calls=%async_computation.1 | async-start | bytes 262144 | tf_op jit(solution)/shard_map/all_to_all | solution.py:476
  55.3 6.8 %all-to-all-done.1.home_ref = f32[16,16,128]{2,1,0:T(8,128)S(1)} async-done(((f32[16,16,128]{2,1,0:T(8,128)}), f32[16,16,128]{2,1,0:T(8,128)S(1)}, u32[]{:S(2)}, u32[]{:S(2)}) %all-to-all-start.1) | async-done | bytes 131104 | tf_op jit(solution)/shard_map/all_to_all | solution.py:476
  62.2 2.2 %collective-permute-start.9 = (f32[8,16,128]{2,1,0:T(8,128)S(1)}, f32[8,16,128]{2,1,0:T(8,128)S(1)}, u32[]{:S(2)}, u32[]{:S(2)}) collective-permute-start(f32[8,16,128]{2,1,0:T(8,128)S(1)} %slice_select_fusion), channel_id=1, source_target_pairs={{0,16},{1,17},{2,18},{3,19},{4,20},{5,21},{6,22},{7,23},{8,24},{9,... | collective-permute-start | bytes 196616 | tf_op jit(solution)/shard_map/ppermute | solution.py:480
  64.4 0.9 %collective-permute-done.9.got_ref = f32[8,16,128]{2,1,0:T(8,128)S(1)} collective-permute-done((f32[8,16,128]{2,1,0:T(8,128)S(1)}, f32[8,16,128]{2,1,0:T(8,128)S(1)}, u32[]{:S(2)}, u32[]{:S(2)}) %collective-permute-start.9) | collective-permute-done | bytes 65568 | tf_op jit(solution)/shard_map/ppermute | solution.py:480
  65.3 0.7 %unpack.1 = f32[2,128,128]{2,1,0:T(8,128)} custom-call(f32[16,16,128]{2,1,0:T(8,128)S(1)} %all-to-all-done.1.home_ref, f32[8,16,128]{2,1,0:T(8,128)S(1)} %collective-permute-done.9.got_ref), custom_call_target="tpu_custom_call" | custom-call | tf_op jit(solution)/shard_map/unpack/pallas_call | solution.py:481
  (17 shorter events, 0.2 us)
Async XLA Ops:
  0.0 13.4 %copy-start = (f32[4,31]{1,0:T(4,128)S(1)}, f32[4,31]{1,0:T(4,128)}, u32[]{:S(2)}) copy-start(f32[4,31]{1,0:T(4,128)} %param.8) | copy-start | bytes 1492
  1.3 3.2 %collective-permute-start = (f32[8,88,128]{2,1,0:T(8,128)S(1)}, f32[8,88,128]{2,1,0:T(8,128)S(1)}, u32[]{:S(2)}, u32[]{:S(2)}) collective-permute-start(f32[8,88,128]{2,1,0:T(8,128)S(1)} %get-tuple-element.21), channel_id=1, source_target_pairs={{0,16},{1,17},{2,18},{3,19},{4,20},{5,21},{6,22},{7,23},{8,24},{9,... | collective-permute-start | bytes 1081352 | tf_op jit(solution)/shard_map/ppermute | solution.py:366
  5.4 21.1 %all-to-all-start = ((f32[16,88,128]{2,1,0:T(8,128)}), f32[16,88,128]{2,1,0:T(8,128)S(1)}, u32[]{:S(2)}, u32[]{:S(2)}) async-start(f32[16,88,128]{2,1,0:T(8,128)} %join.1), calls=%async_computation | async-start | bytes 1441792 | tf_op jit(solution)/shard_map/all_to_all | solution.py:401
  26.5 2.6 %collective-permute-start.1 = (f32[272,128]{1,0:T(8,128)S(1)}, f32[272,128]{1,0:T(8,128)S(1)}, u32[]{:S(2)}, u32[]{:S(2)}) collective-permute-start(f32[272,128]{1,0:T(8,128)S(1)} %pad_maximum_fusion), channel_id=1, source_target_pairs={{0,16},{1,17},{2,18},{3,19},{4,20},{5,21},{6,22},{7,23},{8,24},{9,... | collective-permute-start | bytes 417800 | tf_op jit(solution)/shard_map/ppermute | solution.py:463
  28.0 4.5 %collective-permute-start.2 = (f32[272,128]{1,0:T(8,128)S(1)}, f32[272,128]{1,0:T(8,128)S(1)}, u32[]{:S(2)}, u32[]{:S(2)}) collective-permute-start(f32[272,128]{1,0:T(8,128)S(1)} %pad_maximum_fusion), channel_id=1, source_target_pairs={{20,5},{21,6},{22,7},{23,3},{19,2},{18,1},{17,0},{16,32},{48,33},{... | collective-permute-start | bytes 417800 | tf_op jit(solution)/shard_map/ppermute | solution.py:462
  34.9 4.5 %collective-permute-start.3 = (f32[256,128]{1,0:T(8,128)S(1)}, f32[256,128]{1,0:T(8,128)S(1)}, u32[]{:S(2)}, u32[]{:S(2)}) collective-permute-start(f32[256,128]{1,0:T(8,128)S(1)} %get-tuple-element.29), channel_id=1, source_target_pairs={{20,5},{21,6},{22,7},{23,3},{19,2},{18,1},{17,0},{16,32},{48,33},{... | collective-permute-start | bytes 393224 | tf_op jit(solution)/shard_map/ppermute | solution.py:474
  37.5 1.9 %collective-permute-start.4 = (f32[256,128]{1,0:T(8,128)S(1)}, f32[256,128]{1,0:T(8,128)S(1)}, u32[]{:S(2)}, u32[]{:S(2)}) collective-permute-start(f32[256,128]{1,0:T(8,128)S(1)} %get-tuple-element.30), channel_id=1, source_target_pairs={{0,16},{1,17},{2,18},{3,19},{4,20},{5,21},{6,22},{7,23},{8,24},{9,... | collective-permute-start | bytes 393224 | tf_op jit(solution)/shard_map/ppermute | solution.py:474
  39.4 1.7 %collective-permute-start.6 = (f32[256,128]{1,0:T(8,128)S(1)}, f32[256,128]{1,0:T(8,128)S(1)}, u32[]{:S(2)}, u32[]{:S(2)}) collective-permute-start(f32[256,128]{1,0:T(8,128)S(1)} %update.2.own_ref), channel_id=1, source_target_pairs={{0,16},{1,17},{2,18},{3,19},{4,20},{5,21},{6,22},{7,23},{8,24},{9,... | collective-permute-start | bytes 393224 | tf_op jit(solution)/shard_map/ppermute | solution.py:463
  39.6 4.4 %collective-permute-start.5 = (f32[256,128]{1,0:T(8,128)S(1)}, f32[256,128]{1,0:T(8,128)S(1)}, u32[]{:S(2)}, u32[]{:S(2)}) collective-permute-start(f32[256,128]{1,0:T(8,128)S(1)} %update.2.own_ref), channel_id=1, source_target_pairs={{20,5},{21,6},{22,7},{23,3},{19,2},{18,1},{17,0},{16,32},{48,33},{... | collective-permute-start | bytes 393224 | tf_op jit(solution)/shard_map/ppermute | solution.py:462
  46.4 4.5 %collective-permute-start.7 = (f32[256,128]{1,0:T(8,128)S(1)}, f32[256,128]{1,0:T(8,128)S(1)}, u32[]{:S(2)}, u32[]{:S(2)}) collective-permute-start(f32[256,128]{1,0:T(8,128)S(1)} %get-tuple-element.33), channel_id=1, source_target_pairs={{20,5},{21,6},{22,7},{23,3},{19,2},{18,1},{17,0},{16,32},{48,33},{... | collective-permute-start | bytes 393224 | tf_op jit(solution)/shard_map/ppermute | solution.py:474
  49.4 1.6 %collective-permute-start.8 = (f32[256,128]{1,0:T(8,128)S(1)}, f32[256,128]{1,0:T(8,128)S(1)}, u32[]{:S(2)}, u32[]{:S(2)}) collective-permute-start(f32[256,128]{1,0:T(8,128)S(1)} %get-tuple-element.34), channel_id=1, source_target_pairs={{0,16},{1,17},{2,18},{3,19},{4,20},{5,21},{6,22},{7,23},{8,24},{9,... | collective-permute-start | bytes 393224 | tf_op jit(solution)/shard_map/ppermute | solution.py:474
  51.6 10.5 %all-to-all-start.1 = ((f32[16,16,128]{2,1,0:T(8,128)}), f32[16,16,128]{2,1,0:T(8,128)S(1)}, u32[]{:S(2)}, u32[]{:S(2)}) async-start(f32[16,16,128]{2,1,0:T(8,128)} %bitcast.10), calls=%async_computation.1 | async-start | bytes 262144 | tf_op jit(solution)/shard_map/all_to_all | solution.py:476
  62.2 3.1 %collective-permute-start.9 = (f32[8,16,128]{2,1,0:T(8,128)S(1)}, f32[8,16,128]{2,1,0:T(8,128)S(1)}, u32[]{:S(2)}, u32[]{:S(2)}) collective-permute-start(f32[8,16,128]{2,1,0:T(8,128)S(1)} %slice_select_fusion), channel_id=1, source_target_pairs={{0,16},{1,17},{2,18},{3,19},{4,20},{5,21},{6,22},{7,23},{8,24},{9,... | collective-permute-start | bytes 196616 | tf_op jit(solution)/shard_map/ppermute | solution.py:480

commit v5 on v4

--- a/solution.py
+++ b/solution.py
@@ -71,15 +71,13 @@
     return hi, (x - hi.astype(F32)).astype(BF16)
 
 
-def pack_kernel(
-    codes_hbm, shifts_hbm, est_hbm, views_hbm, keep_ref, send_ref, codes_ref, shifts_ref, est, views, sems
-):
+def pack(sub, out_ref, codes_hbm, shifts_hbm, est_hbm, views_hbm, codes_ref, shifts_ref, est, views, sems):
     core, _ = own_tile_inner()
     copies = [
         pltpu.make_async_copy(codes_hbm, codes_ref, sems.at[0]),
         pltpu.make_async_copy(shifts_hbm, shifts_ref, sems.at[1]),
-        pltpu.make_async_copy(est_hbm, est, sems.at[2]),
-        pltpu.make_async_copy(views_hbm, views, sems.at[3]),
+        pltpu.make_async_copy(est_hbm.at[:, :, sub], est, sems.at[2]),
+        pltpu.make_async_copy(views_hbm.at[:, :, :, sub], views, sems.at[3]),
     ]
     for copy in copies:
         copy.start()
@@ -87,38 +85,47 @@
         copy.wait()
     lane = lax.broadcasted_iota(jnp.int32, (8, T), 1)
     for slot in range(8):
-        plane, col = slot // 4, slot % 4
-        for ref, sub in ((keep_ref, core), (send_ref, 1 - core)):
-            chunk = 2 * part_of(col, core) + sub
-            rows = pl.ds(pl.multiple_of(chunk * ROWS, ROWS), ROWS)
-            meta = jnp.zeros((8, T), F32)
-            for half in range(2):
-                for v in range(V):
-                    code = codes_ref[v, 2 * chunk + half].astype(F32)
-                    shift = shifts_ref[v, 2 * chunk + half].astype(F32)
-                    meta = jnp.where(lane == half * V + v, code, meta)
-                    meta = jnp.where(lane == 8 + half * V + v, shift, meta)
-            ref[slot, 0:ROWS, :] = est[plane, rows, :]
+        plane, part = slot // 4, part_of(slot % 4, core)
+        block = 4 * part + 2 * sub
+        meta = jnp.zeros((8, T), F32)
+        for half in range(2):
             for v in range(V):
-                ref[slot, pl.ds(ROWS * (1 + v), ROWS), :] = views[v, plane, rows, :].astype(F32)
-            ref[slot, pl.ds(ROWS * (1 + V), 8), :] = meta
-
-
-def join_kernel(keep_ref, other_ref, out_hbm, sems):
-    _, inner = own_tile_inner()
-    copies = []
-    for i, (ref, near) in enumerate(((keep_ref, inner), (other_ref, jnp.logical_not(inner)))):
-        first, second = jnp.where(near, 4, 0), jnp.where(near, 8, 12)
-        copies.append(
-            pltpu.make_async_copy(ref.at[0:4], out_hbm.at[pl.ds(first, 4)], sems.at[2 * i])
-        )
-        copies.append(
-            pltpu.make_async_copy(ref.at[4:8], out_hbm.at[pl.ds(second, 4)], sems.at[2 * i + 1])
-        )
+                code = codes_ref[v, block + half].astype(F32)
+                shift = shifts_ref[v, block + half].astype(F32)
+                meta = jnp.where(lane == half * V + v, code, meta)
+                meta = jnp.where(lane == 8 + half * V + v, shift, meta)
+        out_ref[slot, 0:ROWS, :] = est[plane, part]
+        for v in range(V):
+            out_ref[slot, pl.ds(ROWS * (1 + v), ROWS), :] = views[v, plane, part].astype(F32)
+        out_ref[slot, pl.ds(ROWS * (1 + V), 8), :] = meta
+
+
+def place(ref, near, out_hbm, sems):
+    first, second = jnp.where(near, 4, 0), jnp.where(near, 8, 12)
+    copies = [
+        pltpu.make_async_copy(ref.at[0:4], out_hbm.at[pl.ds(first, 4)], sems.at[0]),
+        pltpu.make_async_copy(ref.at[4:8], out_hbm.at[pl.ds(second, 4)], sems.at[1]),
+    ]
     for copy in copies:
         copy.start()
     for copy in copies:
         copy.wait()
+
+
+def send_kernel(codes_hbm, shifts_hbm, est_hbm, views_hbm, send_ref, *scratch):
+    core, _ = own_tile_inner()
+    pack(1 - core, send_ref, codes_hbm, shifts_hbm, est_hbm, views_hbm, *scratch)
+
+
+def keep_kernel(codes_hbm, shifts_hbm, est_hbm, views_hbm, out_hbm, kept, place_sems, *scratch):
+    core, inner = own_tile_inner()
+    pack(core, kept, codes_hbm, shifts_hbm, est_hbm, views_hbm, *scratch)
+    place(kept, inner, out_hbm, place_sems)
+
+
+def join_kernel(kept_hbm, other_ref, out_hbm, sems):
+    _, inner = own_tile_inner()
+    place(other_ref, jnp.logical_not(inner), out_hbm, sems)
 
 
 def inside_kernel(paired_ref, out_ref):
@@ -155,10 +162,25 @@
     )
 
 
+def base_rows(psf_ref, width, at):
+    taps = psf_ref[...]
+    taps = taps / jnp.sum(taps, axis=1, keepdims=True)
+    lane = lax.broadcasted_iota(jnp.int32, (V, width), 1)
+    back, straight = jnp.zeros((V, width), F32), jnp.zeros((V, width), F32)
+    count = taps.shape[1]
+    for t in range(count):
+        tap = jnp.broadcast_to(taps[:, t : t + 1], (V, width))
+        back = jnp.where(lane == at[0] + count - 1 - t, tap, back)
+        straight = jnp.where(lane == at[1] + t, tap, straight)
+    return back, straight
+
+
 def taps_kernel(
-    cols_ref, rows_ref, band_ref, pair_in_ref, near_in_ref, pair_back_ref, near_back_ref
+    psf_rows_ref, psf_cols_ref, band_ref, pair_in_ref, near_in_ref, pair_back_ref, near_back_ref
 ):
     core, _ = own_tile_inner()
+    col_bases = base_rows(psf_cols_ref, 2 * T, (177, 177))
+    back_base, row_base = base_rows(psf_rows_ref, T, (T - 31, 1))
 
     def either(a, b):
         return tuple(jnp.where(core == 0, x, y) for x, y in zip(a, b))
@@ -169,18 +191,18 @@
 
     for v in range(V):
         for d in range(2):
-            hi, lo = turned(cols_ref[2 * v + d : 2 * v + d + 1, :], 2 * T, T)
+            hi, lo = turned(col_bases[d][v : v + 1], 2 * T, T)
             band_ref[v, d, 0 : 2 * T, 0:T] = hi
             band_ref[v, d, 0 : 2 * T, T : 2 * T] = lo
             band_ref[v, d, 2 * T : 4 * T, 0:T] = hi
             band_ref[v, d, 2 * T : 4 * T, T : 2 * T] = jnp.zeros_like(lo)
         before, own, after = [
-            turned(pltpu.roll(jnp.broadcast_to(rows_ref[2 * v : 2 * v + 1, :], (8, T)), (T - ROWS * i) % T, 1)[0:1], ROWS, ROWS) for i in range(3)
+            turned(pltpu.roll(jnp.broadcast_to(row_base[v : v + 1], (8, T)), (T - ROWS * i) % T, 1)[0:1], ROWS, ROWS) for i in range(3)
         ]
         put_split(pair_in_ref, v, [either(before, after)])
         put_split(near_in_ref, v, [own, either(after, before)])
         before, own, after = [
-            turned(pltpu.roll(jnp.broadcast_to(rows_ref[2 * v + 1 : 2 * v + 2, :], (8, T)), ROWS * i, 1)[0:1], ROWS, ROWS) for i in range(3)
+            turned(pltpu.roll(jnp.broadcast_to(back_base[v : v + 1], (8, T)), ROWS * i, 1)[0:1], ROWS, ROWS) for i in range(3)
         ]
         put_split(pair_back_ref, v, [either(before, after)], stacked=True)
         put_split(near_back_ref, v, [own, either(after, before)], stacked=True)
@@ -336,43 +358,58 @@
     put_joined(swap_ref, 1, total2)
 
 
-def place(taps, at, width):
-    return jnp.pad(taps, ((0, 0), (at, width - at - taps.shape[1])))
-
-
 def body(estimate, views, psf_rows, psf_cols, shifts, codes):
     _, inner = own_tile_inner()
+    taken = [
+        pltpu.with_memory_space_constraint(a, pltpu.HBM)
+        for a in (
+            codes[:, :, 0],
+            shifts,
+            estimate.reshape(Z, 4, 2, ROWS, T),
+            views.reshape(V, Z, 4, 2, ROWS, T),
+        )
+    ]
+    room = [
+        pltpu.SMEM((V, 2 * 8), jnp.int32),
+        pltpu.SMEM((V, 2 * 8), jnp.int32),
+        pltpu.VMEM((Z, 4, ROWS, T), F32),
+        pltpu.VMEM((V, Z, 4, ROWS, T), BF16),
+        pltpu.SemaphoreType.DMA((4,)),
+    ]
+    two_sems = pltpu.SemaphoreType.DMA((2,))
     unit = jax.ShapeDtypeStruct((8, UNIT, T), F32)
-    keep, send = pl.pallas_call(
-        pack_kernel,
-        out_shape=(unit, unit),
+    whole = jax.ShapeDtypeStruct((GY, UNIT, T), F32)
+    send = pl.pallas_call(
+        send_kernel,
+        out_shape=unit,
         in_specs=[HBM] * 4,
-        out_specs=(VMEM, VMEM),
-        scratch_shapes=[
-            pltpu.SMEM((V, 2 * 8), jnp.int32),
-            pltpu.SMEM((V, 2 * 8), jnp.int32),
-            pltpu.VMEM((Z, T, T), F32),
-            pltpu.VMEM((V, Z, T, T), BF16),
-            pltpu.SemaphoreType.DMA((4,)),
-        ],
-        compiler_params=PARAMS,
-        name="pack",
-    )(
-        *[
-            pltpu.with_memory_space_constraint(a, pltpu.HBM)
-            for a in (codes[:, :, 0], shifts, estimate, views)
-        ]
-    )
+        out_specs=VMEM,
+        scratch_shapes=room,
+        compiler_params=PARAMS,
+        name="send",
+    )(*taken)
     other = lax.ppermute(send, AXES, SWAP)
-
-    rows_n = psf_rows / jnp.sum(psf_rows, axis=1, keepdims=True)
-    cols_n = psf_cols / jnp.sum(psf_cols, axis=1, keepdims=True)
-    col_base = jnp.stack(
-        [place(cols_n[:, ::-1], 177, 2 * T), place(cols_n, 177, 2 * T)], axis=1
-    ).reshape(2 * V, 2 * T)
-    row_base = jnp.stack(
-        [place(rows_n, 1, T), place(rows_n[:, ::-1], T - 31, T)], axis=1
-    ).reshape(2 * V, T)
+    kept = pl.pallas_call(
+        keep_kernel,
+        out_shape=whole,
+        in_specs=[HBM] * 4,
+        out_specs=HBM,
+        scratch_shapes=[pltpu.VMEM((8, UNIT, T), F32), two_sems] + room,
+        compiler_params=PARAMS,
+        cost_estimate=COST,
+        name="keep",
+    )(*taken)
+    joined = pl.pallas_call(
+        join_kernel,
+        out_shape=whole,
+        in_specs=[HBM, VMEM],
+        out_specs=HBM,
+        scratch_shapes=[two_sems],
+        input_output_aliases={0: 0},
+        compiler_params=PARAMS,
+        name="join",
+    )(kept, other)
+
     band, pair_in, near_in, pair_back, near_back = pl.pallas_call(
         taps_kernel,
         out_shape=(
@@ -387,17 +424,8 @@
         compiler_params=PARAMS,
         cost_estimate=COST,
         name="taps",
-    )(col_base, row_base)
-
-    joined = pl.pallas_call(
-        join_kernel,
-        out_shape=jax.ShapeDtypeStruct((GY, UNIT, T), F32),
-        in_specs=[VMEM, VMEM],
-        out_specs=HBM,
-        scratch_shapes=[pltpu.SemaphoreType.DMA((4,))],
-        compiler_params=PARAMS,
-        name="join",
-    )(keep, other)
+    )(psf_rows, psf_cols)
+
     arrived = lax.all_to_all(joined, "gy", split_axis=0, concat_axis=0, tiled=True)
     own = arrived[:, :ROWS, :].reshape(GY * ROWS, T)
     own_meta = arrived[:, ROWS * (1 + V), :] + 0.0 * band[0, 0, :GY, :T].astype(F32)

time: 66.3 us -> 66.1 us (level)
  other arithmetic: 1.81 us -> 0.05 us
  Pallas kernels: 15.6 us -> 17 us
    pallas_call x2 -> x3, Pallas kernels: 2.22 us -> 3.71 us  [the longest x1 1.84 us: body(): pl.pallas_call(keep_kernel, out_shape=whole, in_specs=[HBM] * 4, out_spec...]
    reduce_sum x2 -> x0, other arithmetic: 0.92 us -> none  [the longest x1 0.8 us: body(): cols_n = psf_cols / jnp.sum(psf_cols, axis=1, keepdims=True)]
    div x2 -> x0, other arithmetic: 0.83 us -> none  [the longest x1 0.75 us: body(): cols_n = psf_cols / jnp.sum(psf_cols, axis=1, keepdims=True)]
  transfers between devices with their start and end apart: 12 -> 12, of which waited for: 7 -> 7; matrix products, arithmetic and copies ran while one was open for 3% -> 0% of each run, Pallas kernels for 11% -> 14%
where the time goes in v5:
time: 66.1 us; the launch traced here: 65.8 us
  waiting for transfers between devices  25.9 us (39%)
  starting transfers between devices  22.6 us (34%)
  Pallas kernels  17 us (26%)
    all_to_all x1, waiting for transfers between devices, body(): lax.all_to_all(joined, 'gy', split_axis=0, concat_axis=0, tiled=True)  11.9 us
    all_to_all x1, starting transfers between devices, body(): lax.all_to_all(joined, 'gy', split_axis=0, concat_axis=0, tiled=True)  7.86 us
    all_to_all x1, waiting for transfers between devices, body(): lax.all_to_all(own.reshape(GY, ROWS, T), 'gy', split_axis=0, concat_axis=...  6.83 us
    pallas_call x2, Pallas kernels, body(): middle(pair_meta, paired, near, arrived, band, pair_in, pair_back)  4.8 us
    all_to_all x1, starting transfers between devices, body(): lax.all_to_all(own.reshape(GY, ROWS, T), 'gy', split_axis=0, concat_axis=...  3.66 us
    ppermute x2, waiting for transfers between devices, body(): paired = lax.ppermute(out, AXES, PAIR)  3.15 us
    ppermute x2, waiting for transfers between devices, body(): lax.ppermute(pair, AXES, PAIR)  3.1 us
    pallas_call x2, Pallas kernels, body(): near = front(near_meta, own, swapped, near_in)  3.02 us
  transfers between devices with their start and end apart: 12, of which 7 were waited for; matrix products, arithmetic and copies ran while one was open for 0% of the time, Pallas kernels for 14%

profile of v5, /device:TPU:1, one launch (start us, length us, event | category | flops | bytes accessed | tf_op | source)
XLA Modules:
  0.0 65.8 jit_solution(16873873332166270673)
XLA Ops:
  0.0 1.1 %send.1 = f32[8,88,128]{2,1,0:T(8,128)S(1)} custom-call(s32[4,16]{1,0:T(4,128)} %bitcast.26, s32[4,16]{1,0:T(4,128)} %shifts_hbm.3, f32[2,4,2,16,128]{4,3,2,1,0:T(8,128)} %bitcast.22, bf16[4,2,4,2,16,128]{5,4,3,2,1,0:T(8,128)(2,1)} %bitcast.20), custom_call_target="tpu_custom_call" | custom-call | tf_op jit(solution)/shard_map/send/pallas_call | solution.py:382
  1.1 1.5 %collective-permute-start = (f32[8,88,128]{2,1,0:T(8,128)S(1)}, f32[8,88,128]{2,1,0:T(8,128)S(1)}, u32[]{:S(2)}, u32[]{:S(2)}) collective-permute-start(f32[8,88,128]{2,1,0:T(8,128)S(1)} %send.1), channel_id=1, source_target_pairs={{0,16},{1,17},{2,18},{3,19},{4,20},{5,21},{6,22},{7,23},{8,24},{9,... | collective-permute-start | bytes 1081352 | tf_op jit(solution)/shard_map/ppermute | solution.py:391
  2.6 1.8 %keep.1.kept_hbm = f32[16,88,128]{2,1,0:T(8,128)} custom-call(s32[4,16]{1,0:T(4,128)} %bitcast.27, s32[4,16]{1,0:T(4,128)} %shifts_hbm.3, f32[2,4,2,16,128]{4,3,2,1,0:T(8,128)} %bitcast.23, bf16[4,2,4,2,16,128]{5,4,3,2,1,0:T(8,128)(2,1)} %bitcast.21), custom_call_target="tpu_custom_call" | custom-call | flops 1000000000 | bytes 4000000 | tf_op jit(solution)/shard_map/keep/pallas_call | solution.py:392
  4.4 0.0 copy-start
  4.5 0.0 copy-start.1
  4.5 0.0 collective-permute-done.other_ref
  4.5 0.8 %join.1 = f32[16,88,128]{2,1,0:T(8,128)} custom-call(f32[16,88,128]{2,1,0:T(8,128)} %keep.1.kept_hbm, f32[8,88,128]{2,1,0:T(8,128)S(1)} %collective-permute-done.other_ref), custom_call_target="tpu_custom_call", output_to_operand_aliasing={{}: (0, {})} | custom-call | tf_op jit(solution)/shard_map/join/pallas_call | solution.py:402
  5.3 7.9 %all-to-all-start = ((f32[16,88,128]{2,1,0:T(8,128)}), f32[16,88,128]{2,1,0:T(8,128)S(1)}, u32[]{:S(2)}, u32[]{:S(2)}) async-start(f32[16,88,128]{2,1,0:T(8,128)} %join.1), calls=%async_computation | async-start | bytes 1441792 | tf_op jit(solution)/shard_map/all_to_all | solution.py:429
  13.1 0.0 copy-done
  13.2 0.0 copy-done.1
  13.2 1.2 %taps.1 = (bf16[4,2,512,256]{3,2,1,0:T(8,128)(2,1)S(1)}, bf16[4,32,32]{2,1,0:T(8,128)(2,1)S(1)}, bf16[4,32,64]{2,1,0:T(8,128)(2,1)S(1)}, bf16[4,32,32]{2,1,0:T(8,128)(2,1)S(1)}, bf16[4,64,32]{2,1,0:T(8,128)(2,1)S(1)}) custom-call(f32[4,31]{1,0:T(4,128)S(1)} %copy-done, f32[4,31]{1,0:T(4,128)S(1)} %copy-done.1), custom_call_target="tpu_custom_call" | custom-call | flops 1000000000 | bytes 4000000 | tf_op jit(solution)/shard_map/taps/pallas_call | solution.py:413
  14.4 11.9 %all-to-all-done.arrived_ref = f32[16,88,128]{2,1,0:T(8,128)S(1)} async-done(((f32[16,88,128]{2,1,0:T(8,128)}), f32[16,88,128]{2,1,0:T(8,128)S(1)}, u32[]{:S(2)}, u32[]{:S(2)}) %all-to-all-start) | async-done | bytes 720928 | tf_op jit(solution)/shard_map/all_to_all | solution.py:429
  26.4 1.5 %collective-permute-start.1 = (f32[272,128]{1,0:T(8,128)S(1)}, f32[272,128]{1,0:T(8,128)S(1)}, u32[]{:S(2)}, u32[]{:S(2)}) collective-permute-start(f32[272,128]{1,0:T(8,128)S(1)} %pad_maximum_fusion), channel_id=1, source_target_pairs={{0,16},{1,17},{2,18},{3,19},{4,20},{5,21},{6,22},{7,23},{8,24},{9,... | collective-permute-start | bytes 417800 | tf_op jit(solution)/shard_map/ppermute | solution.py:491
  27.9 1.2 %collective-permute-start.2 = (f32[272,128]{1,0:T(8,128)S(1)}, f32[272,128]{1,0:T(8,128)S(1)}, u32[]{:S(2)}, u32[]{:S(2)}) collective-permute-start(f32[272,128]{1,0:T(8,128)S(1)} %pad_maximum_fusion), channel_id=1, source_target_pairs={{20,5},{21,6},{22,7},{23,3},{19,2},{18,1},{17,0},{16,32},{48,33},{... | collective-permute-start | bytes 417800 | tf_op jit(solution)/shard_map/ppermute | solution.py:490
  29.1 0.0 collective-permute-done.1.swapped_ref
  29.1 1.5 %front.2.near_ref = f32[4,16,2048]{2,1,0:T(8,128)S(1)} custom-call(s32[32,16]{1,0:T(8,128)S(1)} %maximum_convert_fusion.meta_ref, f32[256,128]{1,0:T(8,128)S(1)} %bitcast.18, f32[272,128]{1,0:T(8,128)S(1)} %collective-permute-done.1.swapped_ref, bf16[4,32,64]{2,1,0:T(8,128)(2,1)S(1)} %get-tuple-element.19.near_in_ref), custom_call_target="tpu_custom_call" | custom-call | flops 1000000000 | bytes 4000000 | tf_op jit(solution)/shard_map/front/pallas_call | solution.py:496
  30.6 1.8 %collective-permute-done.2.paired_ref = f32[272,128]{1,0:T(8,128)S(1)} collective-permute-done((f32[272,128]{1,0:T(8,128)S(1)}, f32[272,128]{1,0:T(8,128)S(1)}, u32[]{:S(2)}, u32[]{:S(2)}) %collective-permute-start.2) | collective-permute-done | bytes 139296 | tf_op jit(solution)/shard_map/ppermute | solution.py:490
  32.4 2.4 %middle.2 = (f32[256,128]{1,0:T(8,128)S(1)}, f32[4,256,128]{2,1,0:T(8,128)S(1)}) custom-call(s32[16,16]{1,0:T(8,128)S(1)} %fusion.2.meta_ref, f32[272,128]{1,0:T(8,128)S(1)} %collective-permute-done.2.paired_ref, f32[4,16,2048]{2,1,0:T(8,128)S(1)} %front.2.near_ref, f32[16,88,128]{2,1,0:T(8,128)S(1)} %all-to-all-done.arrived_ref, ...), custom_call_target="tpu_custom_call" | custom-call | flops 1000000000 | bytes 4000000 | tf_op jit(solution)/shard_map/middle/pallas_call | solution.py:499
  34.8 1.3 %collective-permute-start.3 = (f32[256,128]{1,0:T(8,128)S(1)}, f32[256,128]{1,0:T(8,128)S(1)}, u32[]{:S(2)}, u32[]{:S(2)}) collective-permute-start(f32[256,128]{1,0:T(8,128)S(1)} %get-tuple-element.25), channel_id=1, source_target_pairs={{20,5},{21,6},{22,7},{23,3},{19,2},{18,1},{17,0},{16,32},{48,33},{... | collective-permute-start | bytes 393224 | tf_op jit(solution)/shard_map/ppermute | solution.py:502
  36.0 1.4 %tail.2 = (f32[256,128]{1,0:T(8,128)S(1)}, f32[256,128]{1,0:T(8,128)S(1)}) custom-call(s32[32,16]{1,0:T(8,128)S(1)} %maximum_convert_fusion.meta_ref, f32[4,256,128]{2,1,0:T(8,128)S(1)} %get-tuple-element.22.again_ref, bf16[4,64,32]{2,1,0:T(8,128)(2,1)S(1)} %get-tuple-element.23.near_back_ref), custom_call_target="tpu_custom_call" | custom-call | flops 1000000000 | bytes 4000000 | tf_op jit(solution)/shard_map/tail/pallas_call | solution.py:500
  37.5 0.1 collective-permute-start.4
  37.5 1.7 %collective-permute-done.3.paired_ref = f32[256,128]{1,0:T(8,128)S(1)} collective-permute-done((f32[256,128]{1,0:T(8,128)S(1)}, f32[256,128]{1,0:T(8,128)S(1)}, u32[]{:S(2)}, u32[]{:S(2)}) %collective-permute-start.3) | collective-permute-done | bytes 131104 | tf_op jit(solution)/shard_map/ppermute | solution.py:502
  39.3 0.0 collective-permute-done.4.swapped_ref
  39.3 0.2 collective-permute-start.6
  39.5 1.5 %collective-permute-start.5 = (f32[256,128]{1,0:T(8,128)S(1)}, f32[256,128]{1,0:T(8,128)S(1)}, u32[]{:S(2)}, u32[]{:S(2)}) collective-permute-start(f32[256,128]{1,0:T(8,128)S(1)} %update.2.own_ref), channel_id=1, source_target_pairs={{20,5},{21,6},{22,7},{23,3},{19,2},{18,1},{17,0},{16,32},{48,33},{... | collective-permute-start | bytes 393224 | tf_op jit(solution)/shard_map/ppermute | solution.py:490
  41.0 0.0 collective-permute-done.6.swapped_ref
  41.0 1.5 %front.3.near_ref = f32[4,16,2048]{2,1,0:T(8,128)S(1)} custom-call(s32[32,16]{1,0:T(8,128)S(1)} %maximum_convert_fusion.meta_ref, f32[256,128]{1,0:T(8,128)S(1)} %update.2.own_ref, f32[256,128]{1,0:T(8,128)S(1)} %collective-permute-done.6.swapped_ref, bf16[4,32,64]{2,1,0:T(8,128)(2,1)S(1)} %get-tuple-element.19.near_in_ref), custom_call_target="tpu_custom_call" | custom-call | flops 1000000000 | bytes 4000000 | tf_op jit(solution)/shard_map/front/pallas_call | solution.py:496
  42.5 1.4 %collective-permute-done.5.paired_ref = f32[256,128]{1,0:T(8,128)S(1)} collective-permute-done((f32[256,128]{1,0:T(8,128)S(1)}, f32[256,128]{1,0:T(8,128)S(1)}, u32[]{:S(2)}, u32[]{:S(2)}) %collective-permute-start.5) | collective-permute-done | bytes 131104 | tf_op jit(solution)/shard_map/ppermute | solution.py:490
  43.9 2.4 %middle.3 = (f32[256,128]{1,0:T(8,128)S(1)}, f32[4,256,128]{2,1,0:T(8,128)S(1)}) custom-call(s32[16,16]{1,0:T(8,128)S(1)} %fusion.2.meta_ref, f32[256,128]{1,0:T(8,128)S(1)} %collective-permute-done.5.paired_ref, f32[4,16,2048]{2,1,0:T(8,128)S(1)} %front.3.near_ref, f32[16,88,128]{2,1,0:T(8,128)S(1)} %all-to-all-done.arrived_ref, ...), custom_call_target="tpu_custom_call" | custom-call | flops 1000000000 | bytes 4000000 | tf_op jit(solution)/shard_map/middle/pallas_call | solution.py:499
  46.3 1.6 %collective-permute-start.7 = (f32[256,128]{1,0:T(8,128)S(1)}, f32[256,128]{1,0:T(8,128)S(1)}, u32[]{:S(2)}, u32[]{:S(2)}) collective-permute-start(f32[256,128]{1,0:T(8,128)S(1)} %get-tuple-element.29), channel_id=1, source_target_pairs={{20,5},{21,6},{22,7},{23,3},{19,2},{18,1},{17,0},{16,32},{48,33},{... | collective-permute-start | bytes 393224 | tf_op jit(solution)/shard_map/ppermute | solution.py:502
  47.9 1.4 %tail.3 = (f32[256,128]{1,0:T(8,128)S(1)}, f32[256,128]{1,0:T(8,128)S(1)}) custom-call(s32[32,16]{1,0:T(8,128)S(1)} %maximum_convert_fusion.meta_ref, f32[4,256,128]{2,1,0:T(8,128)S(1)} %get-tuple-element.27.again_ref, bf16[4,64,32]{2,1,0:T(8,128)(2,1)S(1)} %get-tuple-element.23.near_back_ref), custom_call_target="tpu_custom_call" | custom-call | flops 1000000000 | bytes 4000000 | tf_op jit(solution)/shard_map/tail/pallas_call | solution.py:500
  49.3 0.1 collective-permute-start.8
  49.4 1.4 %collective-permute-done.7.paired_ref = f32[256,128]{1,0:T(8,128)S(1)} collective-permute-done((f32[256,128]{1,0:T(8,128)S(1)}, f32[256,128]{1,0:T(8,128)S(1)}, u32[]{:S(2)}, u32[]{:S(2)}) %collective-permute-start.7) | collective-permute-done | bytes 131104 | tf_op jit(solution)/shard_map/ppermute | solution.py:502
  50.8 0.0 collective-permute-done.8.swapped_ref
  50.8 0.7 %update.3 = f32[256,128]{1,0:T(8,128)} custom-call(f32[256,128]{1,0:T(8,128)S(1)} %update.2.own_ref, f32[256,128]{1,0:T(8,128)S(1)} %get-tuple-element.28.mid_ref, f32[256,128]{1,0:T(8,128)S(1)} %inside.3.paired_ref, f32[256,128]{1,0:T(8,128)S(1)} %collective-permute-done.8.swapped_ref), custom_call_target="tpu_custom_call" | custom-call | tf_op jit(solution)/shard_map/update/pallas_call | solution.py:501
  51.5 3.7 %all-to-all-start.1 = ((f32[16,16,128]{2,1,0:T(8,128)}), f32[16,16,128]{2,1,0:T(8,128)S(1)}, u32[]{:S(2)}, u32[]{:S(2)}) async-start(f32[16,16,128]{2,1,0:T(8,128)} %bitcast.7), calls=%async_computation.1 | async-start | bytes 262144 | tf_op jit(solution)/shard_map/all_to_all | solution.py:504
  55.2 6.8 %all-to-all-done.1.home_ref = f32[16,16,128]{2,1,0:T(8,128)S(1)} async-done(((f32[16,16,128]{2,1,0:T(8,128)}), f32[16,16,128]{2,1,0:T(8,128)S(1)}, u32[]{:S(2)}, u32[]{:S(2)}) %all-to-all-start.1) | async-done | bytes 131104 | tf_op jit(solution)/shard_map/all_to_all | solution.py:504
  62.1 2.2 %collective-permute-start.9 = (f32[8,16,128]{2,1,0:T(8,128)S(1)}, f32[8,16,128]{2,1,0:T(8,128)S(1)}, u32[]{:S(2)}, u32[]{:S(2)}) collective-permute-start(f32[8,16,128]{2,1,0:T(8,128)S(1)} %slice_select_fusion), channel_id=1, source_target_pairs={{0,16},{1,17},{2,18},{3,19},{4,20},{5,21},{6,22},{7,23},{8,24},{9,... | collective-permute-start | bytes 196616 | tf_op jit(solution)/shard_map/ppermute | solution.py:508
  64.2 0.9 %collective-permute-done.9.got_ref = f32[8,16,128]{2,1,0:T(8,128)S(1)} collective-permute-done((f32[8,16,128]{2,1,0:T(8,128)S(1)}, f32[8,16,128]{2,1,0:T(8,128)S(1)}, u32[]{:S(2)}, u32[]{:S(2)}) %collective-permute-start.9) | collective-permute-done | bytes 65568 | tf_op jit(solution)/shard_map/ppermute | solution.py:508
  65.1 0.7 %unpack.1 = f32[2,128,128]{2,1,0:T(8,128)} custom-call(f32[16,16,128]{2,1,0:T(8,128)S(1)} %all-to-all-done.1.home_ref, f32[8,16,128]{2,1,0:T(8,128)S(1)} %collective-permute-done.9.got_ref), custom_call_target="tpu_custom_call" | custom-call | tf_op jit(solution)/shard_map/unpack/pallas_call | solution.py:509
  (12 shorter events, 0.1 us)
Async XLA Ops:
  1.1 3.4 %collective-permute-start = (f32[8,88,128]{2,1,0:T(8,128)S(1)}, f32[8,88,128]{2,1,0:T(8,128)S(1)}, u32[]{:S(2)}, u32[]{:S(2)}) collective-permute-start(f32[8,88,128]{2,1,0:T(8,128)S(1)} %send.1), channel_id=1, source_target_pairs={{0,16},{1,17},{2,18},{3,19},{4,20},{5,21},{6,22},{7,23},{8,24},{9,... | collective-permute-start | bytes 1081352 | tf_op jit(solution)/shard_map/ppermute | solution.py:391
  4.4 8.7 %copy-start = (f32[4,31]{1,0:T(4,128)S(1)}, f32[4,31]{1,0:T(4,128)}, u32[]{:S(2)}) copy-start(f32[4,31]{1,0:T(4,128)} %psf_rows_ref.1) | copy-start | bytes 1492
  4.5 8.7 %copy-start.1 = (f32[4,31]{1,0:T(4,128)S(1)}, f32[4,31]{1,0:T(4,128)}, u32[]{:S(2)}) copy-start(f32[4,31]{1,0:T(4,128)} %psf_cols_ref.1) | copy-start | bytes 1492
  5.3 21.0 %all-to-all-start = ((f32[16,88,128]{2,1,0:T(8,128)}), f32[16,88,128]{2,1,0:T(8,128)S(1)}, u32[]{:S(2)}, u32[]{:S(2)}) async-start(f32[16,88,128]{2,1,0:T(8,128)} %join.1), calls=%async_computation | async-start | bytes 1441792 | tf_op jit(solution)/shard_map/all_to_all | solution.py:429
  26.4 2.7 %collective-permute-start.1 = (f32[272,128]{1,0:T(8,128)S(1)}, f32[272,128]{1,0:T(8,128)S(1)}, u32[]{:S(2)}, u32[]{:S(2)}) collective-permute-start(f32[272,128]{1,0:T(8,128)S(1)} %pad_maximum_fusion), channel_id=1, source_target_pairs={{0,16},{1,17},{2,18},{3,19},{4,20},{5,21},{6,22},{7,23},{8,24},{9,... | collective-permute-start | bytes 417800 | tf_op jit(solution)/shard_map/ppermute | solution.py:491
  27.9 4.5 %collective-permute-start.2 = (f32[272,128]{1,0:T(8,128)S(1)}, f32[272,128]{1,0:T(8,128)S(1)}, u32[]{:S(2)}, u32[]{:S(2)}) collective-permute-start(f32[272,128]{1,0:T(8,128)S(1)} %pad_maximum_fusion), channel_id=1, source_target_pairs={{20,5},{21,6},{22,7},{23,3},{19,2},{18,1},{17,0},{16,32},{48,33},{... | collective-permute-start | bytes 417800 | tf_op jit(solution)/shard_map/ppermute | solution.py:490
  34.8 4.5 %collective-permute-start.3 = (f32[256,128]{1,0:T(8,128)S(1)}, f32[256,128]{1,0:T(8,128)S(1)}, u32[]{:S(2)}, u32[]{:S(2)}) collective-permute-start(f32[256,128]{1,0:T(8,128)S(1)} %get-tuple-element.25), channel_id=1, source_target_pairs={{20,5},{21,6},{22,7},{23,3},{19,2},{18,1},{17,0},{16,32},{48,33},{... | collective-permute-start | bytes 393224 | tf_op jit(solution)/shard_map/ppermute | solution.py:502
  37.5 1.8 %collective-permute-start.4 = (f32[256,128]{1,0:T(8,128)S(1)}, f32[256,128]{1,0:T(8,128)S(1)}, u32[]{:S(2)}, u32[]{:S(2)}) collective-permute-start(f32[256,128]{1,0:T(8,128)S(1)} %get-tuple-element.26), channel_id=1, source_target_pairs={{0,16},{1,17},{2,18},{3,19},{4,20},{5,21},{6,22},{7,23},{8,24},{9,... | collective-permute-start | bytes 393224 | tf_op jit(solution)/shard_map/ppermute | solution.py:502
  39.3 1.7 %collective-permute-start.6 = (f32[256,128]{1,0:T(8,128)S(1)}, f32[256,128]{1,0:T(8,128)S(1)}, u32[]{:S(2)}, u32[]{:S(2)}) collective-permute-start(f32[256,128]{1,0:T(8,128)S(1)} %update.2.own_ref), channel_id=1, source_target_pairs={{0,16},{1,17},{2,18},{3,19},{4,20},{5,21},{6,22},{7,23},{8,24},{9,... | collective-permute-start | bytes 393224 | tf_op jit(solution)/shard_map/ppermute | solution.py:491
  39.5 4.4 %collective-permute-start.5 = (f32[256,128]{1,0:T(8,128)S(1)}, f32[256,128]{1,0:T(8,128)S(1)}, u32[]{:S(2)}, u32[]{:S(2)}) collective-permute-start(f32[256,128]{1,0:T(8,128)S(1)} %update.2.own_ref), channel_id=1, source_target_pairs={{20,5},{21,6},{22,7},{23,3},{19,2},{18,1},{17,0},{16,32},{48,33},{... | collective-permute-start | bytes 393224 | tf_op jit(solution)/shard_map/ppermute | solution.py:490
  46.3 4.5 %collective-permute-start.7 = (f32[256,128]{1,0:T(8,128)S(1)}, f32[256,128]{1,0:T(8,128)S(1)}, u32[]{:S(2)}, u32[]{:S(2)}) collective-permute-start(f32[256,128]{1,0:T(8,128)S(1)} %get-tuple-element.29), channel_id=1, source_target_pairs={{20,5},{21,6},{22,7},{23,3},{19,2},{18,1},{17,0},{16,32},{48,33},{... | collective-permute-start | bytes 393224 | tf_op jit(solution)/shard_map/ppermute | solution.py:502
  49.3 1.5 %collective-permute-start.8 = (f32[256,128]{1,0:T(8,128)S(1)}, f32[256,128]{1,0:T(8,128)S(1)}, u32[]{:S(2)}, u32[]{:S(2)}) collective-permute-start(f32[256,128]{1,0:T(8,128)S(1)} %get-tuple-element.30), channel_id=1, source_target_pairs={{0,16},{1,17},{2,18},{3,19},{4,20},{5,21},{6,22},{7,23},{8,24},{9,... | collective-permute-start | bytes 393224 | tf_op jit(solution)/shard_map/ppermute | solution.py:502
  51.5 10.5 %all-to-all-start.1 = ((f32[16,16,128]{2,1,0:T(8,128)}), f32[16,16,128]{2,1,0:T(8,128)S(1)}, u32[]{:S(2)}, u32[]{:S(2)}) async-start(f32[16,16,128]{2,1,0:T(8,128)} %bitcast.7), calls=%async_computation.1 | async-start | bytes 262144 | tf_op jit(solution)/shard_map/all_to_all | solution.py:504
  62.1 3.1 %collective-permute-start.9 = (f32[8,16,128]{2,1,0:T(8,128)S(1)}, f32[8,16,128]{2,1,0:T(8,128)S(1)}, u32[]{:S(2)}, u32[]{:S(2)}) collective-permute-start(f32[8,16,128]{2,1,0:T(8,128)S(1)} %slice_select_fusion), channel_id=1, source_target_pairs={{0,16},{1,17},{2,18},{3,19},{4,20},{5,21},{6,22},{7,23},{8,24},{9,... | collective-permute-start | bytes 196616 | tf_op jit(solution)/shard_map/ppermute | solution.py:508

commit v6 on v5

--- a/solution.py
+++ b/solution.py
@@ -71,7 +71,7 @@
     return hi, (x - hi.astype(F32)).astype(BF16)
 
 
-def pack(sub, out_ref, codes_hbm, shifts_hbm, est_hbm, views_hbm, codes_ref, shifts_ref, est, views, sems):
+def pack(sub, slot_of, out_ref, codes_hbm, shifts_hbm, est_hbm, views_hbm, codes_ref, shifts_ref, est, views, sems):
     core, _ = own_tile_inner()
     copies = [
         pltpu.make_async_copy(codes_hbm, codes_ref, sems.at[0]),
@@ -85,7 +85,7 @@
         copy.wait()
     lane = lax.broadcasted_iota(jnp.int32, (8, T), 1)
     for slot in range(8):
-        plane, part = slot // 4, part_of(slot % 4, core)
+        plane, part, at = slot // 4, part_of(slot % 4, core), slot_of(slot)
         block = 4 * part + 2 * sub
         meta = jnp.zeros((8, T), F32)
         for half in range(2):
@@ -94,38 +94,41 @@
                 shift = shifts_ref[v, block + half].astype(F32)
                 meta = jnp.where(lane == half * V + v, code, meta)
                 meta = jnp.where(lane == 8 + half * V + v, shift, meta)
-        out_ref[slot, 0:ROWS, :] = est[plane, part]
+        out_ref[at, 0:ROWS, :] = est[plane, part]
         for v in range(V):
-            out_ref[slot, pl.ds(ROWS * (1 + v), ROWS), :] = views[v, plane, part].astype(F32)
-        out_ref[slot, pl.ds(ROWS * (1 + V), 8), :] = meta
-
-
-def place(ref, near, out_hbm, sems):
-    first, second = jnp.where(near, 4, 0), jnp.where(near, 8, 12)
-    copies = [
-        pltpu.make_async_copy(ref.at[0:4], out_hbm.at[pl.ds(first, 4)], sems.at[0]),
-        pltpu.make_async_copy(ref.at[4:8], out_hbm.at[pl.ds(second, 4)], sems.at[1]),
-    ]
-    for copy in copies:
-        copy.start()
-    for copy in copies:
-        copy.wait()
+            out_ref[at, pl.ds(ROWS * (1 + v), ROWS), :] = views[v, plane, part].astype(F32)
+        out_ref[at, pl.ds(ROWS * (1 + V), 8), :] = meta
+
+
+def halves(near):
+    return jnp.where(near, 4, 0), jnp.where(near, 8, 12)
 
 
 def send_kernel(codes_hbm, shifts_hbm, est_hbm, views_hbm, send_ref, *scratch):
     core, _ = own_tile_inner()
-    pack(1 - core, send_ref, codes_hbm, shifts_hbm, est_hbm, views_hbm, *scratch)
-
-
-def keep_kernel(codes_hbm, shifts_hbm, est_hbm, views_hbm, out_hbm, kept, place_sems, *scratch):
+    pack(1 - core, lambda slot: slot, send_ref, codes_hbm, shifts_hbm, est_hbm, views_hbm, *scratch)
+
+
+def keep_kernel(codes_hbm, shifts_hbm, est_hbm, views_hbm, out_ref, *scratch):
     core, inner = own_tile_inner()
-    pack(core, kept, codes_hbm, shifts_hbm, est_hbm, views_hbm, *scratch)
-    place(kept, inner, out_hbm, place_sems)
-
-
-def join_kernel(kept_hbm, other_ref, out_hbm, sems):
+    starts = halves(inner)
+    pack(
+        core, lambda slot: starts[slot // 4] + slot % 4, out_ref,
+        codes_hbm, shifts_hbm, est_hbm, views_hbm, *scratch,
+    )
+
+
+def join_kernel(kept_ref, other_ref, out_ref):
     _, inner = own_tile_inner()
-    place(other_ref, jnp.logical_not(inner), out_hbm, sems)
+    for i, start in enumerate(halves(jnp.logical_not(inner))):
+        out_ref[pl.ds(start, 4)] = other_ref[4 * i : 4 * i + 4]
+
+
+def lead_kernel(arrived_ref, out_ref):
+    for c in range(GY):
+        out_ref[ROWS * c : ROWS * c + ROWS, :] = arrived_ref[c, 0:ROWS, :]
+        meta = arrived_ref[c, ROWS * (1 + V) : ROWS * (1 + V) + 1, :]
+        out_ref[GY * ROWS + c : GY * ROWS + c + 1, :] = meta
 
 
 def inside_kernel(paired_ref, out_ref):
@@ -136,6 +139,12 @@
 def update_kernel(own_ref, mid_ref, paired_ref, swapped_ref, out_ref):
     total = mid_ref[...] + paired_ref[...] + swapped_ref[...]
     out_ref[...] = own_ref[0 : GY * ROWS, :] * (total * 0.25)
+
+
+def theirs_kernel(home_ref, out_ref):
+    _, inner = own_tile_inner()
+    out_ref[0:4] = home_ref[pl.ds(jnp.where(inner, 0, 4), 4)]
+    out_ref[4:8] = home_ref[pl.ds(jnp.where(inner, 12, 8), 4)]
 
 
 def unpack_kernel(home_ref, got_ref, out_ref):
@@ -356,6 +365,11 @@
         rows_back(v, meta_ref, near_back_ref, again_ref, total2)
     put_joined(mid_ref, 0, total2)
     put_joined(swap_ref, 1, total2)
+
+
+def all_to_all(blocks):
+    blocks = pltpu.with_memory_space_constraint(blocks, pltpu.VMEM)
+    return lax.all_to_all(blocks, "gy", split_axis=0, concat_axis=0, tiled=True)
 
 
 def body(estimate, views, psf_rows, psf_cols, shifts, codes):
@@ -376,7 +390,6 @@
         pltpu.VMEM((V, Z, 4, ROWS, T), BF16),
         pltpu.SemaphoreType.DMA((4,)),
     ]
-    two_sems = pltpu.SemaphoreType.DMA((2,))
     unit = jax.ShapeDtypeStruct((8, UNIT, T), F32)
     whole = jax.ShapeDtypeStruct((GY, UNIT, T), F32)
     send = pl.pallas_call(
@@ -393,8 +406,8 @@
         keep_kernel,
         out_shape=whole,
         in_specs=[HBM] * 4,
-        out_specs=HBM,
-        scratch_shapes=[pltpu.VMEM((8, UNIT, T), F32), two_sems] + room,
+        out_specs=VMEM,
+        scratch_shapes=room,
         compiler_params=PARAMS,
         cost_estimate=COST,
         name="keep",
@@ -402,9 +415,8 @@
     joined = pl.pallas_call(
         join_kernel,
         out_shape=whole,
-        in_specs=[HBM, VMEM],
-        out_specs=HBM,
-        scratch_shapes=[two_sems],
+        in_specs=[VMEM, VMEM],
+        out_specs=VMEM,
         input_output_aliases={0: 0},
         compiler_params=PARAMS,
         name="join",
@@ -422,13 +434,19 @@
         in_specs=[VMEM, VMEM],
         out_specs=(VMEM,) * 5,
         compiler_params=PARAMS,
-        cost_estimate=COST,
         name="taps",
     )(psf_rows, psf_cols)
 
-    arrived = lax.all_to_all(joined, "gy", split_axis=0, concat_axis=0, tiled=True)
-    own = arrived[:, :ROWS, :].reshape(GY * ROWS, T)
-    own_meta = arrived[:, ROWS * (1 + V), :] + 0.0 * band[0, 0, :GY, :T].astype(F32)
+    arrived = all_to_all(joined)
+    lead = pl.pallas_call(
+        lead_kernel,
+        out_shape=jax.ShapeDtypeStruct((GY * ROWS + GY, T), F32),
+        in_specs=[VMEM],
+        out_specs=VMEM,
+        compiler_params=PARAMS,
+        name="lead",
+    )(arrived)
+    own_meta = lead[GY * ROWS :, :META]
     update = pl.pallas_call(
         update_kernel,
         out_shape=jax.ShapeDtypeStruct((GY * ROWS, T), F32),
@@ -455,7 +473,6 @@
         out_specs=VMEM,
         scratch_shapes=[doubled[1], doubled[1], pltpu.VMEM((V, 4 * ROWS, GY * T), BF16)],
         compiler_params=PARAMS,
-        cost_estimate=COST,
         name="front",
     )
     middle = pl.pallas_call(
@@ -485,13 +502,13 @@
         cost_estimate=COST,
         name="tail",
     )
+    own = lead
     for sweep in range(ITERS):
-        out = jnp.concatenate([own, own_meta], axis=0) if sweep == 0 else own
-        paired = lax.ppermute(out, AXES, PAIR)
-        swapped = lax.ppermute(out, AXES, SWAP)
+        paired = lax.ppermute(own, AXES, PAIR)
+        swapped = lax.ppermute(own, AXES, SWAP)
         if sweep == 0:
             near_meta = jnp.concatenate(
-                [own_meta[:, :META], swapped[GY * ROWS :, :META]], axis=0
+                [own_meta, swapped[GY * ROWS :, :META]], axis=0
             ).astype(jnp.int32)
         near = front(near_meta, own, swapped, near_in)
         if sweep == 0:
@@ -501,10 +518,15 @@
         own = update(
             own, mid, inside(lax.ppermute(pair, AXES, PAIR)), lax.ppermute(swap, AXES, SWAP)
         )
-    home = lax.all_to_all(
-        own.reshape(GY, ROWS, T), "gy", split_axis=0, concat_axis=0, tiled=True
-    )
-    theirs = jnp.where(inner, jnp.concatenate([home[0:4], home[12:16]], axis=0), home[4:12])
+    home = all_to_all(own.reshape(GY, ROWS, T))
+    theirs = pl.pallas_call(
+        theirs_kernel,
+        out_shape=jax.ShapeDtypeStruct((8, ROWS, T), F32),
+        in_specs=[VMEM],
+        out_specs=VMEM,
+        compiler_params=PARAMS,
+        name="theirs",
+    )(home)
     got = lax.ppermute(theirs, AXES, SWAP)
     return pl.pallas_call(
         unpack_kernel,

time: 66.1 us -> 63.5 us (0.961)
  blocking collectives: 0 us -> 31.1 us
  waiting for transfers between devices: 25.9 us -> 6.15 us
  starting transfers between devices: 22.6 us -> 11 us
  Pallas kernels: 17 us -> 14.9 us
    all_to_all x0 -> x2, blocking collectives: none -> 31.1 us  [all_to_all(): return lax.all_to_all(blocks, 'gy', split_axis=0, concat_axis=0, tiled=True)]
    all_to_all x2 -> x0, waiting for transfers between devices: 18.8 us -> none  [the longest x1 11.9 us: body(): lax.all_to_all(joined, 'gy', split_axis=0, concat_axis=0, tiled=True)]
    all_to_all x2 -> x0, starting transfers between devices: 11.5 us -> none  [the longest x1 7.86 us: body(): lax.all_to_all(joined, 'gy', split_axis=0, concat_axis=0, tiled=True)]
    ppermute x4, waiting for transfers between devices: 3.16 us -> 1.92 us  [the longest x2 1.92 us: body(): paired = lax.ppermute(own, AXES, PAIR)]
    pallas_call x1, Pallas kernels: 1.84 us -> 1.09 us  [body(): pl.pallas_call(keep_kernel, out_shape=whole, in_specs=[HBM] * 4, out_spec...]
    pallas_call x1 -> x3, Pallas kernels: 0.78 us -> 0.06 us  [the longest x1 0.04 us: body(): pl.pallas_call(join_kernel, out_shape=whole, in_specs=[VMEM, VMEM], out_s...]
  transfers between devices with their start and end apart: 12 -> 10, of which waited for: 7 -> 6; matrix products, arithmetic and copies ran while one was open for 0% -> 0% of each run, Pallas kernels for 14% -> 13%
where the time goes in v6:
time: 63.5 us; the launch traced here: 63.3 us
  blocking collectives  31.1 us (49%)
  Pallas kernels  14.9 us (23%)
  starting transfers between devices  11 us (17%)
  waiting for transfers between devices  6.15 us (10%)
    all_to_all x2, blocking collectives, all_to_all(): return lax.all_to_all(blocks, 'gy', split_axis=0, concat_axis=0, tiled=True)  31.1 us
    pallas_call x2, Pallas kernels, body(): middle(pair_meta, paired, near, arrived, band, pair_in, pair_back)  4.82 us
    ppermute x2, waiting for transfers between devices, body(): lax.ppermute(pair, AXES, PAIR)  3.14 us
    pallas_call x2, Pallas kernels, body(): near = front(near_meta, own, swapped, near_in)  3.01 us
    ppermute x2, starting transfers between devices, body(): lax.ppermute(pair, AXES, PAIR)  2.82 us
    pallas_call x2, Pallas kernels, body(): mid, swap = tail(near_meta, again, near_back)  2.78 us
    ppermute x2, starting transfers between devices, body(): paired = lax.ppermute(own, AXES, PAIR)  2.7 us
    ppermute x1, starting transfers between devices, body(): got = lax.ppermute(theirs, AXES, SWAP)  2.08 us
  transfers between devices with their start and end apart: 10, of which 6 were waited for; matrix products, arithmetic and copies ran while one was open for 0% of the time, Pallas kernels for 13%

profile of v6, /device:TPU:1, one launch (start us, length us, event | category | flops | bytes accessed | tf_op | source)
XLA Modules:
  0.0 63.3 jit_solution(13084046962618852886)
XLA Ops:
  0.0 1.1 %send.1 = f32[8,88,128]{2,1,0:T(8,128)S(1)} custom-call(s32[4,16]{1,0:T(4,128)} %bitcast.15, s32[4,16]{1,0:T(4,128)} %shifts_hbm.3, f32[2,4,2,16,128]{4,3,2,1,0:T(8,128)} %bitcast.13, bf16[4,2,4,2,16,128]{5,4,3,2,1,0:T(8,128)(2,1)} %bitcast.11), custom_call_target="tpu_custom_call" | custom-call | tf_op jit(solution)/shard_map/send/pallas_call | solution.py:395
  1.1 1.5 %collective-permute-start = (f32[8,88,128]{2,1,0:T(8,128)S(1)}, f32[8,88,128]{2,1,0:T(8,128)S(1)}, u32[]{:S(2)}, u32[]{:S(2)}) collective-permute-start(f32[8,88,128]{2,1,0:T(8,128)S(1)} %send.1), channel_id=1, source_target_pairs={{0,16},{1,17},{2,18},{3,19},{4,20},{5,21},{6,22},{7,23},{8,24},{9,... | collective-permute-start | bytes 1081352 | tf_op jit(solution)/shard_map/ppermute | solution.py:404
  2.6 1.1 %keep.1.kept_ref = f32[16,88,128]{2,1,0:T(8,128)S(1)} custom-call(s32[4,16]{1,0:T(4,128)} %bitcast.16, s32[4,16]{1,0:T(4,128)} %shifts_hbm.3, f32[2,4,2,16,128]{4,3,2,1,0:T(8,128)} %bitcast.14, bf16[4,2,4,2,16,128]{5,4,3,2,1,0:T(8,128)(2,1)} %bitcast.12), custom_call_target="tpu_custom_call" | custom-call | flops 1000000000 | bytes 4000000 | tf_op jit(solution)/shard_map/keep/pallas_call | solution.py:405
  3.7 0.0 copy-start
  3.7 0.0 copy-start.1
  3.7 0.2 collective-permute-done.other_ref
  4.0 20.8 %all_to_all.10.arrived_ref = f32[16,88,128]{2,1,0:T(8,128)S(1)} all-to-all(f32[16,88,128]{2,1,0:T(8,128)S(1)} %join.1), channel_id=1, replica_groups=mesh['gx'=8,'gy'=16] {'gy'}, dimensions={0} | all-to-all | bytes 1441792 | tf_op jit(solution)/shard_map/all_to_all | solution.py:372
  24.7 1.6 %collective-permute-start.1 = (f32[272,128]{1,0:T(8,128)S(1)}, f32[272,128]{1,0:T(8,128)S(1)}, u32[]{:S(2)}, u32[]{:S(2)}) collective-permute-start(f32[272,128]{1,0:T(8,128)S(1)} %lead.1.own_ref), channel_id=1, source_target_pairs={{0,16},{1,17},{2,18},{3,19},{4,20},{5,21},{6,22},{7,23},{8,24},{9,... | collective-permute-start | bytes 417800 | tf_op jit(solution)/shard_map/ppermute | solution.py:508
  26.3 1.2 %collective-permute-start.2 = (f32[272,128]{1,0:T(8,128)S(1)}, f32[272,128]{1,0:T(8,128)S(1)}, u32[]{:S(2)}, u32[]{:S(2)}) collective-permute-start(f32[272,128]{1,0:T(8,128)S(1)} %lead.1.own_ref), channel_id=1, source_target_pairs={{20,5},{21,6},{22,7},{23,3},{19,2},{18,1},{17,0},{16,32},{48,33},{... | collective-permute-start | bytes 417800 | tf_op jit(solution)/shard_map/ppermute | solution.py:507
  27.5 0.0 copy-done
  27.5 0.0 copy-done.1
  27.5 1.2 %taps.1 = (bf16[4,2,512,256]{3,2,1,0:T(8,128)(2,1)S(1)}, bf16[4,32,32]{2,1,0:T(8,128)(2,1)S(1)}, bf16[4,32,64]{2,1,0:T(8,128)(2,1)S(1)}, bf16[4,32,32]{2,1,0:T(8,128)(2,1)S(1)}, bf16[4,64,32]{2,1,0:T(8,128)(2,1)S(1)}) custom-call(f32[4,31]{1,0:T(4,128)S(1)} %copy-done, f32[4,31]{1,0:T(4,128)S(1)} %copy-done.1), custom_call_target="tpu_custom_call" | custom-call | tf_op jit(solution)/shard_map/taps/pallas_call | solution.py:425
  28.7 0.0 collective-permute-done.1.swapped_ref
  28.8 1.5 %front.2.near_ref = f32[4,16,2048]{2,1,0:T(8,128)S(1)} custom-call(s32[32,16]{1,0:T(8,128)S(1)} %maximum_convert_fusion.meta_ref, f32[272,128]{1,0:T(8,128)S(1)} %lead.1.own_ref, f32[272,128]{1,0:T(8,128)S(1)} %collective-permute-done.1.swapped_ref, bf16[4,32,64]{2,1,0:T(8,128)(2,1)S(1)} %get-tuple-element.18.near_in_ref), custom_call_target="tpu_custom_call" | custom-call | tf_op jit(solution)/shard_map/front/pallas_call | solution.py:513
  30.3 0.5 collective-permute-done.2.paired_ref
  30.8 2.4 %middle.2 = (f32[256,128]{1,0:T(8,128)S(1)}, f32[4,256,128]{2,1,0:T(8,128)S(1)}) custom-call(s32[16,16]{1,0:T(8,128)S(1)} %fusion.2.meta_ref, f32[272,128]{1,0:T(8,128)S(1)} %collective-permute-done.2.paired_ref, f32[4,16,2048]{2,1,0:T(8,128)S(1)} %front.2.near_ref, f32[16,88,128]{2,1,0:T(8,128)S(1)} %all_to_all.10.arrived_ref, ...), custom_call_target="tpu_custom_call" | custom-call | flops 1000000000 | bytes 4000000 | tf_op jit(solution)/shard_map/middle/pallas_call | solution.py:516
  33.2 1.3 %collective-permute-start.3 = (f32[256,128]{1,0:T(8,128)S(1)}, f32[256,128]{1,0:T(8,128)S(1)}, u32[]{:S(2)}, u32[]{:S(2)}) collective-permute-start(f32[256,128]{1,0:T(8,128)S(1)} %get-tuple-element.25), channel_id=1, source_target_pairs={{20,5},{21,6},{22,7},{23,3},{19,2},{18,1},{17,0},{16,32},{48,33},{... | collective-permute-start | bytes 393224 | tf_op jit(solution)/shard_map/ppermute | solution.py:519
  34.5 1.4 %tail.2 = (f32[256,128]{1,0:T(8,128)S(1)}, f32[256,128]{1,0:T(8,128)S(1)}) custom-call(s32[32,16]{1,0:T(8,128)S(1)} %maximum_convert_fusion.meta_ref, f32[4,256,128]{2,1,0:T(8,128)S(1)} %get-tuple-element.22.again_ref, bf16[4,64,32]{2,1,0:T(8,128)(2,1)S(1)} %get-tuple-element.23.near_back_ref), custom_call_target="tpu_custom_call" | custom-call | flops 1000000000 | bytes 4000000 | tf_op jit(solution)/shard_map/tail/pallas_call | solution.py:517
  35.9 0.1 collective-permute-start.4
  36.0 1.7 %collective-permute-done.3.paired_ref = f32[256,128]{1,0:T(8,128)S(1)} collective-permute-done((f32[256,128]{1,0:T(8,128)S(1)}, f32[256,128]{1,0:T(8,128)S(1)}, u32[]{:S(2)}, u32[]{:S(2)}) %collective-permute-start.3) | collective-permute-done | bytes 131104 | tf_op jit(solution)/shard_map/ppermute | solution.py:519
  37.7 0.0 collective-permute-done.4.swapped_ref
  37.8 0.2 collective-permute-start.6
  37.9 1.5 %collective-permute-start.5 = (f32[256,128]{1,0:T(8,128)S(1)}, f32[256,128]{1,0:T(8,128)S(1)}, u32[]{:S(2)}, u32[]{:S(2)}) collective-permute-start(f32[256,128]{1,0:T(8,128)S(1)} %update.2.own_ref), channel_id=1, source_target_pairs={{20,5},{21,6},{22,7},{23,3},{19,2},{18,1},{17,0},{16,32},{48,33},{... | collective-permute-start | bytes 393224 | tf_op jit(solution)/shard_map/ppermute | solution.py:507
  39.4 0.0 collective-permute-done.6.swapped_ref
  39.4 1.5 %front.3.near_ref = f32[4,16,2048]{2,1,0:T(8,128)S(1)} custom-call(s32[32,16]{1,0:T(8,128)S(1)} %maximum_convert_fusion.meta_ref, f32[256,128]{1,0:T(8,128)S(1)} %update.2.own_ref, f32[256,128]{1,0:T(8,128)S(1)} %collective-permute-done.6.swapped_ref, bf16[4,32,64]{2,1,0:T(8,128)(2,1)S(1)} %get-tuple-element.18.near_in_ref), custom_call_target="tpu_custom_call" | custom-call | tf_op jit(solution)/shard_map/front/pallas_call | solution.py:513
  40.9 1.4 %collective-permute-done.5.paired_ref = f32[256,128]{1,0:T(8,128)S(1)} collective-permute-done((f32[256,128]{1,0:T(8,128)S(1)}, f32[256,128]{1,0:T(8,128)S(1)}, u32[]{:S(2)}, u32[]{:S(2)}) %collective-permute-start.5) | collective-permute-done | bytes 131104 | tf_op jit(solution)/shard_map/ppermute | solution.py:507
  42.3 2.4 %middle.3 = (f32[256,128]{1,0:T(8,128)S(1)}, f32[4,256,128]{2,1,0:T(8,128)S(1)}) custom-call(s32[16,16]{1,0:T(8,128)S(1)} %fusion.2.meta_ref, f32[256,128]{1,0:T(8,128)S(1)} %collective-permute-done.5.paired_ref, f32[4,16,2048]{2,1,0:T(8,128)S(1)} %front.3.near_ref, f32[16,88,128]{2,1,0:T(8,128)S(1)} %all_to_all.10.arrived_ref, ...), custom_call_target="tpu_custom_call" | custom-call | flops 1000000000 | bytes 4000000 | tf_op jit(solution)/shard_map/middle/pallas_call | solution.py:516
  44.8 1.6 %collective-permute-start.7 = (f32[256,128]{1,0:T(8,128)S(1)}, f32[256,128]{1,0:T(8,128)S(1)}, u32[]{:S(2)}, u32[]{:S(2)}) collective-permute-start(f32[256,128]{1,0:T(8,128)S(1)} %get-tuple-element.29), channel_id=1, source_target_pairs={{20,5},{21,6},{22,7},{23,3},{19,2},{18,1},{17,0},{16,32},{48,33},{... | collective-permute-start | bytes 393224 | tf_op jit(solution)/shard_map/ppermute | solution.py:519
  46.3 1.4 %tail.3 = (f32[256,128]{1,0:T(8,128)S(1)}, f32[256,128]{1,0:T(8,128)S(1)}) custom-call(s32[32,16]{1,0:T(8,128)S(1)} %maximum_convert_fusion.meta_ref, f32[4,256,128]{2,1,0:T(8,128)S(1)} %get-tuple-element.27.again_ref, bf16[4,64,32]{2,1,0:T(8,128)(2,1)S(1)} %get-tuple-element.23.near_back_ref), custom_call_target="tpu_custom_call" | custom-call | flops 1000000000 | bytes 4000000 | tf_op jit(solution)/shard_map/tail/pallas_call | solution.py:517
  47.7 0.1 collective-permute-start.8
  47.8 1.4 %collective-permute-done.7.paired_ref = f32[256,128]{1,0:T(8,128)S(1)} collective-permute-done((f32[256,128]{1,0:T(8,128)S(1)}, f32[256,128]{1,0:T(8,128)S(1)}, u32[]{:S(2)}, u32[]{:S(2)}) %collective-permute-start.7) | collective-permute-done | bytes 131104 | tf_op jit(solution)/shard_map/ppermute | solution.py:519
  49.3 0.0 collective-permute-done.8.swapped_ref
  49.3 10.3 %all_to_all.11.home_ref = f32[16,16,128]{2,1,0:T(8,128)S(1)} all-to-all(f32[16,16,128]{2,1,0:T(8,128)S(1)} %bitcast.10), channel_id=1, replica_groups=mesh['gx'=8,'gy'=16] {'gy'}, dimensions={0} | all-to-all | bytes 262144 | tf_op jit(solution)/shard_map/all_to_all | solution.py:372
  59.6 2.1 %collective-permute-start.9 = (f32[8,16,128]{2,1,0:T(8,128)S(1)}, f32[8,16,128]{2,1,0:T(8,128)S(1)}, u32[]{:S(2)}, u32[]{:S(2)}) collective-permute-start(f32[8,16,128]{2,1,0:T(8,128)S(1)} %theirs.1), channel_id=1, source_target_pairs={{0,16},{1,17},{2,18},{3,19},{4,20},{5,21},{6,22},{7,23},{8,24},{9,... | collective-permute-start | bytes 196616 | tf_op jit(solution)/shard_map/ppermute | solution.py:530
  61.7 0.9 %collective-permute-done.9.got_ref = f32[8,16,128]{2,1,0:T(8,128)S(1)} collective-permute-done((f32[8,16,128]{2,1,0:T(8,128)S(1)}, f32[8,16,128]{2,1,0:T(8,128)S(1)}, u32[]{:S(2)}, u32[]{:S(2)}) %collective-permute-start.9) | collective-permute-done | bytes 65568 | tf_op jit(solution)/shard_map/ppermute | solution.py:530
  62.6 0.7 %unpack.1 = f32[2,128,128]{2,1,0:T(8,128)} custom-call(f32[16,16,128]{2,1,0:T(8,128)S(1)} %all_to_all.11.home_ref, f32[8,16,128]{2,1,0:T(8,128)S(1)} %collective-permute-done.9.got_ref), custom_call_target="tpu_custom_call" | custom-call | tf_op jit(solution)/shard_map/unpack/pallas_call | solution.py:531
  (11 shorter events, 0.2 us)
Async XLA Ops:
  1.1 2.8 %collective-permute-start = (f32[8,88,128]{2,1,0:T(8,128)S(1)}, f32[8,88,128]{2,1,0:T(8,128)S(1)}, u32[]{:S(2)}, u32[]{:S(2)}) collective-permute-start(f32[8,88,128]{2,1,0:T(8,128)S(1)} %send.1), channel_id=1, source_target_pairs={{0,16},{1,17},{2,18},{3,19},{4,20},{5,21},{6,22},{7,23},{8,24},{9,... | collective-permute-start | bytes 1081352 | tf_op jit(solution)/shard_map/ppermute | solution.py:404
  3.7 23.8 %copy-start = (f32[4,31]{1,0:T(4,128)S(1)}, f32[4,31]{1,0:T(4,128)}, u32[]{:S(2)}) copy-start(f32[4,31]{1,0:T(4,128)} %psf_rows_ref.1) | copy-start | bytes 1492
  3.7 23.8 %copy-start.1 = (f32[4,31]{1,0:T(4,128)S(1)}, f32[4,31]{1,0:T(4,128)}, u32[]{:S(2)}) copy-start(f32[4,31]{1,0:T(4,128)} %psf_cols_ref.1) | copy-start | bytes 1492
  24.7 4.0 %collective-permute-start.1 = (f32[272,128]{1,0:T(8,128)S(1)}, f32[272,128]{1,0:T(8,128)S(1)}, u32[]{:S(2)}, u32[]{:S(2)}) collective-permute-start(f32[272,128]{1,0:T(8,128)S(1)} %lead.1.own_ref), channel_id=1, source_target_pairs={{0,16},{1,17},{2,18},{3,19},{4,20},{5,21},{6,22},{7,23},{8,24},{9,... | collective-permute-start | bytes 417800 | tf_op jit(solution)/shard_map/ppermute | solution.py:508
  26.3 4.5 %collective-permute-start.2 = (f32[272,128]{1,0:T(8,128)S(1)}, f32[272,128]{1,0:T(8,128)S(1)}, u32[]{:S(2)}, u32[]{:S(2)}) collective-permute-start(f32[272,128]{1,0:T(8,128)S(1)} %lead.1.own_ref), channel_id=1, source_target_pairs={{20,5},{21,6},{22,7},{23,3},{19,2},{18,1},{17,0},{16,32},{48,33},{... | collective-permute-start | bytes 417800 | tf_op jit(solution)/shard_map/ppermute | solution.py:507
  33.2 4.5 %collective-permute-start.3 = (f32[256,128]{1,0:T(8,128)S(1)}, f32[256,128]{1,0:T(8,128)S(1)}, u32[]{:S(2)}, u32[]{:S(2)}) collective-permute-start(f32[256,128]{1,0:T(8,128)S(1)} %get-tuple-element.25), channel_id=1, source_target_pairs={{20,5},{21,6},{22,7},{23,3},{19,2},{18,1},{17,0},{16,32},{48,33},{... | collective-permute-start | bytes 393224 | tf_op jit(solution)/shard_map/ppermute | solution.py:519
  35.9 1.8 %collective-permute-start.4 = (f32[256,128]{1,0:T(8,128)S(1)}, f32[256,128]{1,0:T(8,128)S(1)}, u32[]{:S(2)}, u32[]{:S(2)}) collective-permute-start(f32[256,128]{1,0:T(8,128)S(1)} %get-tuple-element.26), channel_id=1, source_target_pairs={{0,16},{1,17},{2,18},{3,19},{4,20},{5,21},{6,22},{7,23},{8,24},{9,... | collective-permute-start | bytes 393224 | tf_op jit(solution)/shard_map/ppermute | solution.py:519
  37.8 1.7 %collective-permute-start.6 = (f32[256,128]{1,0:T(8,128)S(1)}, f32[256,128]{1,0:T(8,128)S(1)}, u32[]{:S(2)}, u32[]{:S(2)}) collective-permute-start(f32[256,128]{1,0:T(8,128)S(1)} %update.2.own_ref), channel_id=1, source_target_pairs={{0,16},{1,17},{2,18},{3,19},{4,20},{5,21},{6,22},{7,23},{8,24},{9,... | collective-permute-start | bytes 393224 | tf_op jit(solution)/shard_map/ppermute | solution.py:508
  37.9 4.4 %collective-permute-start.5 = (f32[256,128]{1,0:T(8,128)S(1)}, f32[256,128]{1,0:T(8,128)S(1)}, u32[]{:S(2)}, u32[]{:S(2)}) collective-permute-start(f32[256,128]{1,0:T(8,128)S(1)} %update.2.own_ref), channel_id=1, source_target_pairs={{20,5},{21,6},{22,7},{23,3},{19,2},{18,1},{17,0},{16,32},{48,33},{... | collective-permute-start | bytes 393224 | tf_op jit(solution)/shard_map/ppermute | solution.py:507
  44.8 4.5 %collective-permute-start.7 = (f32[256,128]{1,0:T(8,128)S(1)}, f32[256,128]{1,0:T(8,128)S(1)}, u32[]{:S(2)}, u32[]{:S(2)}) collective-permute-start(f32[256,128]{1,0:T(8,128)S(1)} %get-tuple-element.29), channel_id=1, source_target_pairs={{20,5},{21,6},{22,7},{23,3},{19,2},{18,1},{17,0},{16,32},{48,33},{... | collective-permute-start | bytes 393224 | tf_op jit(solution)/shard_map/ppermute | solution.py:519
  47.7 1.5 %collective-permute-start.8 = (f32[256,128]{1,0:T(8,128)S(1)}, f32[256,128]{1,0:T(8,128)S(1)}, u32[]{:S(2)}, u32[]{:S(2)}) collective-permute-start(f32[256,128]{1,0:T(8,128)S(1)} %get-tuple-element.30), channel_id=1, source_target_pairs={{0,16},{1,17},{2,18},{3,19},{4,20},{5,21},{6,22},{7,23},{8,24},{9,... | collective-permute-start | bytes 393224 | tf_op jit(solution)/shard_map/ppermute | solution.py:519
  59.6 3.0 %collective-permute-start.9 = (f32[8,16,128]{2,1,0:T(8,128)S(1)}, f32[8,16,128]{2,1,0:T(8,128)S(1)}, u32[]{:S(2)}, u32[]{:S(2)}) collective-permute-start(f32[8,16,128]{2,1,0:T(8,128)S(1)} %theirs.1), channel_id=1, source_target_pairs={{0,16},{1,17},{2,18},{3,19},{4,20},{5,21},{6,22},{7,23},{8,24},{9,... | collective-permute-start | bytes 196616 | tf_op jit(solution)/shard_map/ppermute | solution.py:530

commit v7 on v6

--- a/solution.py
+++ b/solution.py
@@ -226,12 +226,15 @@
         jnp.where(lane < T // 2, turned[j], turned[j + 1]) for j in range(len(pieces) + 1)
     ]
     his, los = zip(*[split(m) for m in moved])
-    windows = [
-        jnp.concatenate([his[c], his[c + 1], los[c], los[c + 1]], axis=1)
-        for c in range(len(pieces))
-    ]
-    both = jnp.dot(jnp.concatenate(windows, axis=0), band, preferred_element_type=F32)
-    return both[:, :T] + both[:, T:]
+    done = []
+    for half in range(2):
+        windows = [
+            jnp.concatenate([his[c], his[c + 1], los[c], los[c + 1]], axis=1)
+            for c in range(half * len(pieces) // 2, (half + 1) * len(pieces) // 2)
+        ]
+        both = jnp.dot(jnp.concatenate(windows, axis=0), band, preferred_element_type=F32)
+        done.append(both[:, :T] + both[:, T:])
+    return jnp.concatenate(done, axis=0)
 
 
 def column_tiles(ref, v):
@@ -308,11 +311,10 @@
             ref[ROWS * c + 8 * half : ROWS * c + 8 * half + 8, :] = y[c]
 
 
-def in_turn(stages):
-    for turn in range(V + len(stages) - 1):
-        for i, stage in enumerate(stages):
-            if 0 <= turn - i < V:
-                stage(turn - i)
+def for_views(stages):
+    for stage in stages:
+        for v in range(V):
+            stage(v)
 
 
 def front_kernel(meta_ref, own_ref, swapped_ref, near_in_ref, smooth_ref, est2, slope2, view_u):
@@ -323,7 +325,7 @@
     def rows_in(v):
         smooth_ref[v] = product(near_in_ref[v], view_u[v])
 
-    in_turn((lambda v: gather(v, meta_ref, est2, slope2, view_u), rows_in))
+    for_views((lambda v: gather(v, meta_ref, est2, slope2, view_u), rows_in))
 
 
 def core_kernel(
@@ -349,7 +351,7 @@
     def cols_back(v):
         again_ref[v] = column_pass(column_tiles(ratio, v), band_ref[v, 1])
 
-    in_turn((
+    for_views((
         lambda v: gather(v, meta_ref, est2, slope2, view_u),
         rows_in,
         cols_in,

time: 63.5 us -> 62.8 us (0.989)
  Pallas kernels: 14.9 us -> 14.2 us
    pallas_call x2, Pallas kernels: 4.82 us -> 4.14 us  [body(): middle(pair_meta, paired, near, arrived, band, pair_in, pair_back)]
where the time goes in v7:
time: 62.8 us; the launch traced here: 62.6 us
  blocking collectives  31.1 us (50%)
  Pallas kernels  14.2 us (23%)
  starting transfers between devices  11 us (18%)
  waiting for transfers between devices  6.1 us (10%)
    all_to_all x2, blocking collectives, all_to_all(): return lax.all_to_all(blocks, 'gy', split_axis=0, concat_axis=0, tiled=True)  31.1 us
    pallas_call x2, Pallas kernels, body(): middle(pair_meta, paired, near, arrived, band, pair_in, pair_back)  4.14 us
    ppermute x2, waiting for transfers between devices, body(): lax.ppermute(pair, AXES, PAIR)  3.11 us
    pallas_call x2, Pallas kernels, body(): near = front(near_meta, own, swapped, near_in)  3.01 us
    ppermute x2, starting transfers between devices, body(): lax.ppermute(pair, AXES, PAIR)  2.84 us
    pallas_call x2, Pallas kernels, body(): mid, swap = tail(near_meta, again, near_back)  2.8 us
    ppermute x2, starting transfers between devices, body(): paired = lax.ppermute(own, AXES, PAIR)  2.7 us
    ppermute x1, starting transfers between devices, body(): got = lax.ppermute(theirs, AXES, SWAP)  2.08 us
  transfers between devices with their start and end apart: 10, of which 6 were waited for; matrix products, arithmetic and copies ran while one was open for 0% of the time, Pallas kernels for 13%

profile of v7, /device:TPU:1, one launch (start us, length us, event | category | flops | bytes accessed | tf_op | source)
XLA Modules:
  0.0 62.6 jit_solution(6491890892316957169)
XLA Ops:
  0.0 1.1 %send.1 = f32[8,88,128]{2,1,0:T(8,128)S(1)} custom-call(s32[4,16]{1,0:T(4,128)} %bitcast.15, s32[4,16]{1,0:T(4,128)} %shifts_hbm.3, f32[2,4,2,16,128]{4,3,2,1,0:T(8,128)} %bitcast.13, bf16[4,2,4,2,16,128]{5,4,3,2,1,0:T(8,128)(2,1)} %bitcast.11), custom_call_target="tpu_custom_call" | custom-call | tf_op jit(solution)/shard_map/send/pallas_call | solution.py:397
  1.1 1.5 %collective-permute-start = (f32[8,88,128]{2,1,0:T(8,128)S(1)}, f32[8,88,128]{2,1,0:T(8,128)S(1)}, u32[]{:S(2)}, u32[]{:S(2)}) collective-permute-start(f32[8,88,128]{2,1,0:T(8,128)S(1)} %send.1), channel_id=1, source_target_pairs={{0,16},{1,17},{2,18},{3,19},{4,20},{5,21},{6,22},{7,23},{8,24},{9,... | collective-permute-start | bytes 1081352 | tf_op jit(solution)/shard_map/ppermute | solution.py:406
  2.6 1.1 %keep.1.kept_ref = f32[16,88,128]{2,1,0:T(8,128)S(1)} custom-call(s32[4,16]{1,0:T(4,128)} %bitcast.16, s32[4,16]{1,0:T(4,128)} %shifts_hbm.3, f32[2,4,2,16,128]{4,3,2,1,0:T(8,128)} %bitcast.14, bf16[4,2,4,2,16,128]{5,4,3,2,1,0:T(8,128)(2,1)} %bitcast.12), custom_call_target="tpu_custom_call" | custom-call | flops 1000000000 | bytes 4000000 | tf_op jit(solution)/shard_map/keep/pallas_call | solution.py:407
  3.7 0.0 copy-start
  3.7 0.0 copy-start.1
  3.7 0.2 collective-permute-done.other_ref
  4.0 20.8 %all_to_all.10.arrived_ref = f32[16,88,128]{2,1,0:T(8,128)S(1)} all-to-all(f32[16,88,128]{2,1,0:T(8,128)S(1)} %join.1), channel_id=1, replica_groups=mesh['gx'=8,'gy'=16] {'gy'}, dimensions={0} | all-to-all | bytes 1441792 | tf_op jit(solution)/shard_map/all_to_all | solution.py:374
  24.7 1.6 %collective-permute-start.1 = (f32[272,128]{1,0:T(8,128)S(1)}, f32[272,128]{1,0:T(8,128)S(1)}, u32[]{:S(2)}, u32[]{:S(2)}) collective-permute-start(f32[272,128]{1,0:T(8,128)S(1)} %lead.1.own_ref), channel_id=1, source_target_pairs={{0,16},{1,17},{2,18},{3,19},{4,20},{5,21},{6,22},{7,23},{8,24},{9,... | collective-permute-start | bytes 417800 | tf_op jit(solution)/shard_map/ppermute | solution.py:510
  26.3 1.2 %collective-permute-start.2 = (f32[272,128]{1,0:T(8,128)S(1)}, f32[272,128]{1,0:T(8,128)S(1)}, u32[]{:S(2)}, u32[]{:S(2)}) collective-permute-start(f32[272,128]{1,0:T(8,128)S(1)} %lead.1.own_ref), channel_id=1, source_target_pairs={{20,5},{21,6},{22,7},{23,3},{19,2},{18,1},{17,0},{16,32},{48,33},{... | collective-permute-start | bytes 417800 | tf_op jit(solution)/shard_map/ppermute | solution.py:509
  27.5 0.0 copy-done
  27.5 0.0 copy-done.1
  27.5 1.2 %taps.1 = (bf16[4,2,512,256]{3,2,1,0:T(8,128)(2,1)S(1)}, bf16[4,32,32]{2,1,0:T(8,128)(2,1)S(1)}, bf16[4,32,64]{2,1,0:T(8,128)(2,1)S(1)}, bf16[4,32,32]{2,1,0:T(8,128)(2,1)S(1)}, bf16[4,64,32]{2,1,0:T(8,128)(2,1)S(1)}) custom-call(f32[4,31]{1,0:T(4,128)S(1)} %copy-done, f32[4,31]{1,0:T(4,128)S(1)} %copy-done.1), custom_call_target="tpu_custom_call" | custom-call | tf_op jit(solution)/shard_map/taps/pallas_call | solution.py:427
  28.7 0.0 collective-permute-done.1.swapped_ref
  28.8 1.5 %front.2.near_ref = f32[4,16,2048]{2,1,0:T(8,128)S(1)} custom-call(s32[32,16]{1,0:T(8,128)S(1)} %maximum_convert_fusion.meta_ref, f32[272,128]{1,0:T(8,128)S(1)} %lead.1.own_ref, f32[272,128]{1,0:T(8,128)S(1)} %collective-permute-done.1.swapped_ref, bf16[4,32,64]{2,1,0:T(8,128)(2,1)S(1)} %get-tuple-element.18.near_in_ref), custom_call_target="tpu_custom_call" | custom-call | tf_op jit(solution)/shard_map/front/pallas_call | solution.py:515
  30.3 0.5 collective-permute-done.2.paired_ref
  30.8 2.1 %middle.2 = (f32[256,128]{1,0:T(8,128)S(1)}, f32[4,256,128]{2,1,0:T(8,128)S(1)}) custom-call(s32[16,16]{1,0:T(8,128)S(1)} %fusion.2.meta_ref, f32[272,128]{1,0:T(8,128)S(1)} %collective-permute-done.2.paired_ref, f32[4,16,2048]{2,1,0:T(8,128)S(1)} %front.2.near_ref, f32[16,88,128]{2,1,0:T(8,128)S(1)} %all_to_all.10.arrived_ref, ...), custom_call_target="tpu_custom_call" | custom-call | flops 1000000000 | bytes 4000000 | tf_op jit(solution)/shard_map/middle/pallas_call | solution.py:518
  32.9 1.3 %collective-permute-start.3 = (f32[256,128]{1,0:T(8,128)S(1)}, f32[256,128]{1,0:T(8,128)S(1)}, u32[]{:S(2)}, u32[]{:S(2)}) collective-permute-start(f32[256,128]{1,0:T(8,128)S(1)} %get-tuple-element.25), channel_id=1, source_target_pairs={{20,5},{21,6},{22,7},{23,3},{19,2},{18,1},{17,0},{16,32},{48,33},{... | collective-permute-start | bytes 393224 | tf_op jit(solution)/shard_map/ppermute | solution.py:521
  34.1 1.4 %tail.2 = (f32[256,128]{1,0:T(8,128)S(1)}, f32[256,128]{1,0:T(8,128)S(1)}) custom-call(s32[32,16]{1,0:T(8,128)S(1)} %maximum_convert_fusion.meta_ref, f32[4,256,128]{2,1,0:T(8,128)S(1)} %get-tuple-element.22.again_ref, bf16[4,64,32]{2,1,0:T(8,128)(2,1)S(1)} %get-tuple-element.23.near_back_ref), custom_call_target="tpu_custom_call" | custom-call | flops 1000000000 | bytes 4000000 | tf_op jit(solution)/shard_map/tail/pallas_call | solution.py:519
  35.5 0.1 collective-permute-start.4
  35.6 1.7 %collective-permute-done.3.paired_ref = f32[256,128]{1,0:T(8,128)S(1)} collective-permute-done((f32[256,128]{1,0:T(8,128)S(1)}, f32[256,128]{1,0:T(8,128)S(1)}, u32[]{:S(2)}, u32[]{:S(2)}) %collective-permute-start.3) | collective-permute-done | bytes 131104 | tf_op jit(solution)/shard_map/ppermute | solution.py:521
  37.4 0.0 collective-permute-done.4.swapped_ref
  37.4 0.2 collective-permute-start.6
  37.6 1.5 %collective-permute-start.5 = (f32[256,128]{1,0:T(8,128)S(1)}, f32[256,128]{1,0:T(8,128)S(1)}, u32[]{:S(2)}, u32[]{:S(2)}) collective-permute-start(f32[256,128]{1,0:T(8,128)S(1)} %update.2.own_ref), channel_id=1, source_target_pairs={{20,5},{21,6},{22,7},{23,3},{19,2},{18,1},{17,0},{16,32},{48,33},{... | collective-permute-start | bytes 393224 | tf_op jit(solution)/shard_map/ppermute | solution.py:509
  39.1 0.0 collective-permute-done.6.swapped_ref
  39.1 1.5 %front.3.near_ref = f32[4,16,2048]{2,1,0:T(8,128)S(1)} custom-call(s32[32,16]{1,0:T(8,128)S(1)} %maximum_convert_fusion.meta_ref, f32[256,128]{1,0:T(8,128)S(1)} %update.2.own_ref, f32[256,128]{1,0:T(8,128)S(1)} %collective-permute-done.6.swapped_ref, bf16[4,32,64]{2,1,0:T(8,128)(2,1)S(1)} %get-tuple-element.18.near_in_ref), custom_call_target="tpu_custom_call" | custom-call | tf_op jit(solution)/shard_map/front/pallas_call | solution.py:515
  40.6 1.4 %collective-permute-done.5.paired_ref = f32[256,128]{1,0:T(8,128)S(1)} collective-permute-done((f32[256,128]{1,0:T(8,128)S(1)}, f32[256,128]{1,0:T(8,128)S(1)}, u32[]{:S(2)}, u32[]{:S(2)}) %collective-permute-start.5) | collective-permute-done | bytes 131104 | tf_op jit(solution)/shard_map/ppermute | solution.py:509
  42.0 2.1 %middle.3 = (f32[256,128]{1,0:T(8,128)S(1)}, f32[4,256,128]{2,1,0:T(8,128)S(1)}) custom-call(s32[16,16]{1,0:T(8,128)S(1)} %fusion.2.meta_ref, f32[256,128]{1,0:T(8,128)S(1)} %collective-permute-done.5.paired_ref, f32[4,16,2048]{2,1,0:T(8,128)S(1)} %front.3.near_ref, f32[16,88,128]{2,1,0:T(8,128)S(1)} %all_to_all.10.arrived_ref, ...), custom_call_target="tpu_custom_call" | custom-call | flops 1000000000 | bytes 4000000 | tf_op jit(solution)/shard_map/middle/pallas_call | solution.py:518
  44.1 1.6 %collective-permute-start.7 = (f32[256,128]{1,0:T(8,128)S(1)}, f32[256,128]{1,0:T(8,128)S(1)}, u32[]{:S(2)}, u32[]{:S(2)}) collective-permute-start(f32[256,128]{1,0:T(8,128)S(1)} %get-tuple-element.29), channel_id=1, source_target_pairs={{20,5},{21,6},{22,7},{23,3},{19,2},{18,1},{17,0},{16,32},{48,33},{... | collective-permute-start | bytes 393224 | tf_op jit(solution)/shard_map/ppermute | solution.py:521
  45.7 1.4 %tail.3 = (f32[256,128]{1,0:T(8,128)S(1)}, f32[256,128]{1,0:T(8,128)S(1)}) custom-call(s32[32,16]{1,0:T(8,128)S(1)} %maximum_convert_fusion.meta_ref, f32[4,256,128]{2,1,0:T(8,128)S(1)} %get-tuple-element.27.again_ref, bf16[4,64,32]{2,1,0:T(8,128)(2,1)S(1)} %get-tuple-element.23.near_back_ref), custom_call_target="tpu_custom_call" | custom-call | flops 1000000000 | bytes 4000000 | tf_op jit(solution)/shard_map/tail/pallas_call | solution.py:519
  47.1 0.1 collective-permute-start.8
  47.1 1.4 %collective-permute-done.7.paired_ref = f32[256,128]{1,0:T(8,128)S(1)} collective-permute-done((f32[256,128]{1,0:T(8,128)S(1)}, f32[256,128]{1,0:T(8,128)S(1)}, u32[]{:S(2)}, u32[]{:S(2)}) %collective-permute-start.7) | collective-permute-done | bytes 131104 | tf_op jit(solution)/shard_map/ppermute | solution.py:521
  48.6 0.0 collective-permute-done.8.swapped_ref
  48.6 10.3 %all_to_all.11.home_ref = f32[16,16,128]{2,1,0:T(8,128)S(1)} all-to-all(f32[16,16,128]{2,1,0:T(8,128)S(1)} %bitcast.10), channel_id=1, replica_groups=mesh['gx'=8,'gy'=16] {'gy'}, dimensions={0} | all-to-all | bytes 262144 | tf_op jit(solution)/shard_map/all_to_all | solution.py:374
  59.0 2.1 %collective-permute-start.9 = (f32[8,16,128]{2,1,0:T(8,128)S(1)}, f32[8,16,128]{2,1,0:T(8,128)S(1)}, u32[]{:S(2)}, u32[]{:S(2)}) collective-permute-start(f32[8,16,128]{2,1,0:T(8,128)S(1)} %theirs.1), channel_id=1, source_target_pairs={{0,16},{1,17},{2,18},{3,19},{4,20},{5,21},{6,22},{7,23},{8,24},{9,... | collective-permute-start | bytes 196616 | tf_op jit(solution)/shard_map/ppermute | solution.py:532
  61.1 0.9 %collective-permute-done.9.got_ref = f32[8,16,128]{2,1,0:T(8,128)S(1)} collective-permute-done((f32[8,16,128]{2,1,0:T(8,128)S(1)}, f32[8,16,128]{2,1,0:T(8,128)S(1)}, u32[]{:S(2)}, u32[]{:S(2)}) %collective-permute-start.9) | collective-permute-done | bytes 65568 | tf_op jit(solution)/shard_map/ppermute | solution.py:532
  62.0 0.7 %unpack.1 = f32[2,128,128]{2,1,0:T(8,128)} custom-call(f32[16,16,128]{2,1,0:T(8,128)S(1)} %all_to_all.11.home_ref, f32[8,16,128]{2,1,0:T(8,128)S(1)} %collective-permute-done.9.got_ref), custom_call_target="tpu_custom_call" | custom-call | tf_op jit(solution)/shard_map/unpack/pallas_call | solution.py:533
  (11 shorter events, 0.2 us)
Async XLA Ops:
  1.1 2.8 %collective-permute-start = (f32[8,88,128]{2,1,0:T(8,128)S(1)}, f32[8,88,128]{2,1,0:T(8,128)S(1)}, u32[]{:S(2)}, u32[]{:S(2)}) collective-permute-start(f32[8,88,128]{2,1,0:T(8,128)S(1)} %send.1), channel_id=1, source_target_pairs={{0,16},{1,17},{2,18},{3,19},{4,20},{5,21},{6,22},{7,23},{8,24},{9,... | collective-permute-start | bytes 1081352 | tf_op jit(solution)/shard_map/ppermute | solution.py:406
  3.7 23.8 %copy-start = (f32[4,31]{1,0:T(4,128)S(1)}, f32[4,31]{1,0:T(4,128)}, u32[]{:S(2)}) copy-start(f32[4,31]{1,0:T(4,128)} %psf_rows_ref.1) | copy-start | bytes 1492
  3.7 23.8 %copy-start.1 = (f32[4,31]{1,0:T(4,128)S(1)}, f32[4,31]{1,0:T(4,128)}, u32[]{:S(2)}) copy-start(f32[4,31]{1,0:T(4,128)} %psf_cols_ref.1) | copy-start | bytes 1492
  24.7 4.0 %collective-permute-start.1 = (f32[272,128]{1,0:T(8,128)S(1)}, f32[272,128]{1,0:T(8,128)S(1)}, u32[]{:S(2)}, u32[]{:S(2)}) collective-permute-start(f32[272,128]{1,0:T(8,128)S(1)} %lead.1.own_ref), channel_id=1, source_target_pairs={{0,16},{1,17},{2,18},{3,19},{4,20},{5,21},{6,22},{7,23},{8,24},{9,... | collective-permute-start | bytes 417800 | tf_op jit(solution)/shard_map/ppermute | solution.py:510
  26.3 4.5 %collective-permute-start.2 = (f32[272,128]{1,0:T(8,128)S(1)}, f32[272,128]{1,0:T(8,128)S(1)}, u32[]{:S(2)}, u32[]{:S(2)}) collective-permute-start(f32[272,128]{1,0:T(8,128)S(1)} %lead.1.own_ref), channel_id=1, source_target_pairs={{20,5},{21,6},{22,7},{23,3},{19,2},{18,1},{17,0},{16,32},{48,33},{... | collective-permute-start | bytes 417800 | tf_op jit(solution)/shard_map/ppermute | solution.py:509
  32.9 4.5 %collective-permute-start.3 = (f32[256,128]{1,0:T(8,128)S(1)}, f32[256,128]{1,0:T(8,128)S(1)}, u32[]{:S(2)}, u32[]{:S(2)}) collective-permute-start(f32[256,128]{1,0:T(8,128)S(1)} %get-tuple-element.25), channel_id=1, source_target_pairs={{20,5},{21,6},{22,7},{23,3},{19,2},{18,1},{17,0},{16,32},{48,33},{... | collective-permute-start | bytes 393224 | tf_op jit(solution)/shard_map/ppermute | solution.py:521
  35.5 1.8 %collective-permute-start.4 = (f32[256,128]{1,0:T(8,128)S(1)}, f32[256,128]{1,0:T(8,128)S(1)}, u32[]{:S(2)}, u32[]{:S(2)}) collective-permute-start(f32[256,128]{1,0:T(8,128)S(1)} %get-tuple-element.26), channel_id=1, source_target_pairs={{0,16},{1,17},{2,18},{3,19},{4,20},{5,21},{6,22},{7,23},{8,24},{9,... | collective-permute-start | bytes 393224 | tf_op jit(solution)/shard_map/ppermute | solution.py:521
  37.4 1.7 %collective-permute-start.6 = (f32[256,128]{1,0:T(8,128)S(1)}, f32[256,128]{1,0:T(8,128)S(1)}, u32[]{:S(2)}, u32[]{:S(2)}) collective-permute-start(f32[256,128]{1,0:T(8,128)S(1)} %update.2.own_ref), channel_id=1, source_target_pairs={{0,16},{1,17},{2,18},{3,19},{4,20},{5,21},{6,22},{7,23},{8,24},{9,... | collective-permute-start | bytes 393224 | tf_op jit(solution)/shard_map/ppermute | solution.py:510
  37.6 4.4 %collective-permute-start.5 = (f32[256,128]{1,0:T(8,128)S(1)}, f32[256,128]{1,0:T(8,128)S(1)}, u32[]{:S(2)}, u32[]{:S(2)}) collective-permute-start(f32[256,128]{1,0:T(8,128)S(1)} %update.2.own_ref), channel_id=1, source_target_pairs={{20,5},{21,6},{22,7},{23,3},{19,2},{18,1},{17,0},{16,32},{48,33},{... | collective-permute-start | bytes 393224 | tf_op jit(solution)/shard_map/ppermute | solution.py:509
  44.1 4.5 %collective-permute-start.7 = (f32[256,128]{1,0:T(8,128)S(1)}, f32[256,128]{1,0:T(8,128)S(1)}, u32[]{:S(2)}, u32[]{:S(2)}) collective-permute-start(f32[256,128]{1,0:T(8,128)S(1)} %get-tuple-element.29), channel_id=1, source_target_pairs={{20,5},{21,6},{22,7},{23,3},{19,2},{18,1},{17,0},{16,32},{48,33},{... | collective-permute-start | bytes 393224 | tf_op jit(solution)/shard_map/ppermute | solution.py:521
  47.1 1.5 %collective-permute-start.8 = (f32[256,128]{1,0:T(8,128)S(1)}, f32[256,128]{1,0:T(8,128)S(1)}, u32[]{:S(2)}, u32[]{:S(2)}) collective-permute-start(f32[256,128]{1,0:T(8,128)S(1)} %get-tuple-element.30), channel_id=1, source_target_pairs={{0,16},{1,17},{2,18},{3,19},{4,20},{5,21},{6,22},{7,23},{8,24},{9,... | collective-permute-start | bytes 393224 | tf_op jit(solution)/shard_map/ppermute | solution.py:521
  59.0 3.0 %collective-permute-start.9 = (f32[8,16,128]{2,1,0:T(8,128)S(1)}, f32[8,16,128]{2,1,0:T(8,128)S(1)}, u32[]{:S(2)}, u32[]{:S(2)}) collective-permute-start(f32[8,16,128]{2,1,0:T(8,128)S(1)} %theirs.1), channel_id=1, source_target_pairs={{0,16},{1,17},{2,18},{3,19},{4,20},{5,21},{6,22},{7,23},{8,24},{9,... | collective-permute-start | bytes 196616 | tf_op jit(solution)/shard_map/ppermute | solution.py:532

commit v8 on v7

--- a/solution.py
+++ b/solution.py
@@ -45,6 +45,9 @@
     ]
     + [(device_of(0, q), device_of(1, q)) for q in (0, CHUNKS - 1)]
 )
+
+
+CHIPS = [[(2 * x + c) * GY + g for c in range(2) for g in range(GY)] for x in range(GX // 2)]
 
 
 def own_tile_inner():
@@ -141,21 +144,23 @@
     out_ref[...] = own_ref[0 : GY * ROWS, :] * (total * 0.25)
 
 
-def theirs_kernel(home_ref, out_ref):
-    _, inner = own_tile_inner()
-    out_ref[0:4] = home_ref[pl.ds(jnp.where(inner, 0, 4), 4)]
-    out_ref[4:8] = home_ref[pl.ds(jnp.where(inner, 12, 8), 4)]
-
-
-def unpack_kernel(home_ref, got_ref, out_ref):
+def twice_kernel(own_ref, near_ref, paired_ref, swapped_ref, out_ref):
+    for copy in range(2):
+        update_kernel(
+            own_ref, near_ref, paired_ref, swapped_ref,
+            out_ref.at[GY * ROWS * copy : GY * ROWS * (copy + 1)],
+        )
+
+
+def unpack_kernel(home_ref, out_ref):
     core, inner = own_tile_inner()
     for slot in range(8):
         plane, col = slot // 4, slot % 4
-        start = 2 * part_of(col, core)
         source = jnp.where(inner, 4 + slot, 12 * plane + col)
-        for sub, value in ((core, home_ref[source]), (1 - core, got_ref[slot])):
-            rows = pl.ds(pl.multiple_of((start + sub) * ROWS, ROWS), ROWS)
-            out_ref[plane, rows, :] = value
+        for sub in range(2):
+            at = (2 * part_of(col, core) + sub) * ROWS
+            rows = pl.ds(pl.multiple_of(at, ROWS), ROWS)
+            out_ref[plane, rows, :] = home_ref[GY * sub + source]
 
 
 def put_split(ref, v, pieces, stacked=False):
@@ -449,14 +454,17 @@
         name="lead",
     )(arrived)
     own_meta = lead[GY * ROWS :, :META]
-    update = pl.pallas_call(
-        update_kernel,
-        out_shape=jax.ShapeDtypeStruct((GY * ROWS, T), F32),
-        in_specs=[VMEM] * 4,
-        out_specs=VMEM,
-        compiler_params=PARAMS,
-        name="update",
-    )
+    update, update_twice = [
+        pl.pallas_call(
+            kernel,
+            out_shape=jax.ShapeDtypeStruct((count * GY * ROWS, T), F32),
+            in_specs=[VMEM] * 4,
+            out_specs=VMEM,
+            compiler_params=PARAMS,
+            name=name,
+        )
+        for kernel, count, name in ((update_kernel, 1, "update"), (twice_kernel, 2, "last"))
+    ]
     chunk = jax.ShapeDtypeStruct((GY * ROWS, T), F32)
     inside = pl.pallas_call(
         inside_kernel,
@@ -517,27 +525,21 @@
             pair_meta = (paired[GY * ROWS :, :META] + 0.0 * near[0, :, :META]).astype(jnp.int32)
         pair, again = middle(pair_meta, paired, near, arrived, band, pair_in, pair_back)
         mid, swap = tail(near_meta, again, near_back)
-        own = update(
+        own = (update if sweep < ITERS - 1 else update_twice)(
             own, mid, inside(lax.ppermute(pair, AXES, PAIR)), lax.ppermute(swap, AXES, SWAP)
         )
-    home = all_to_all(own.reshape(GY, ROWS, T))
-    theirs = pl.pallas_call(
-        theirs_kernel,
-        out_shape=jax.ShapeDtypeStruct((8, ROWS, T), F32),
-        in_specs=[VMEM],
-        out_specs=VMEM,
-        compiler_params=PARAMS,
-        name="theirs",
-    )(home)
-    got = lax.ppermute(theirs, AXES, SWAP)
+    blocks = pltpu.with_memory_space_constraint(own.reshape(2 * GY, ROWS, T), pltpu.VMEM)
+    home = lax.all_to_all(
+        blocks, AXES, split_axis=0, concat_axis=0, tiled=True, axis_index_groups=CHIPS
+    )
     return pl.pallas_call(
         unpack_kernel,
         out_shape=jax.ShapeDtypeStruct((Z, T, T), F32),
-        in_specs=[VMEM, VMEM],
+        in_specs=[VMEM],
         out_specs=VMEM,
         compiler_params=PARAMS,
         name="unpack",
-    )(home, got)
+    )(home)
 
 
 def solution(mesh):

time: 62.8 us -> 62.3 us (level)
  blocking collectives: 31.1 us -> 33.5 us
  starting transfers between devices: 11 us -> 8.93 us
  waiting for transfers between devices: 6.1 us -> 5.21 us
    all_to_all x0 -> x1, blocking collectives: none -> 12.8 us  [body(): lax.all_to_all(blocks, AXES, split_axis=0, concat_axis=0, tiled=True, axi...]
    all_to_all x2 -> x1, blocking collectives: 31.1 us -> 20.8 us  [all_to_all(): return lax.all_to_all(blocks, 'gy', split_axis=0, concat_axis=0, tiled=True)]
    ppermute x1 -> x0, starting transfers between devices: 2.08 us -> none  [body(): got = lax.ppermute(theirs, AXES, SWAP)]
    ppermute x1 -> x0, waiting for transfers between devices: 0.9 us -> none  [body(): got = lax.ppermute(theirs, AXES, SWAP)]
  transfers between devices with their start and end apart: 10 -> 9, of which waited for: 6 -> 5; matrix products, arithmetic and copies ran while one was open for 0% -> 0% of each run, Pallas kernels for 13% -> 13%
where the time goes in v8:
time: 62.3 us; the launch traced here: 62.1 us
  blocking collectives  33.5 us (54%)
  Pallas kernels  14.2 us (23%)
  starting transfers between devices  8.93 us (14%)
  waiting for transfers between devices  5.21 us (8%)
    all_to_all x1, blocking collectives, all_to_all(): return lax.all_to_all(blocks, 'gy', split_axis=0, concat_axis=0, tiled=True)  20.8 us
    all_to_all x1, blocking collectives, body(): lax.all_to_all(blocks, AXES, split_axis=0, concat_axis=0, tiled=True, axi...  12.8 us
    pallas_call x2, Pallas kernels, body(): middle(pair_meta, paired, near, arrived, band, pair_in, pair_back)  4.15 us
    ppermute x2, waiting for transfers between devices, body(): lax.ppermute(pair, AXES, PAIR)  3.11 us
    pallas_call x2, Pallas kernels, body(): near = front(near_meta, own, swapped, near_in)  3.01 us
    ppermute x2, starting transfers between devices, body(): lax.ppermute(pair, AXES, PAIR)  2.83 us
    pallas_call x2, Pallas kernels, body(): mid, swap = tail(near_meta, again, near_back)  2.8 us
    ppermute x2, starting transfers between devices, body(): paired = lax.ppermute(own, AXES, PAIR)  2.7 us
  transfers between devices with their start and end apart: 9, of which 5 were waited for; matrix products, arithmetic and copies ran while one was open for 0% of the time, Pallas kernels for 13%

profile of v8, /device:TPU:1, one launch (start us, length us, event | category | flops | bytes accessed | tf_op | source)
XLA Modules:
  0.0 62.1 jit_solution(6026994461193626835)
XLA Ops:
  0.0 1.1 %send.1 = f32[8,88,128]{2,1,0:T(8,128)S(1)} custom-call(s32[4,16]{1,0:T(4,128)} %bitcast.15, s32[4,16]{1,0:T(4,128)} %shifts_hbm.3, f32[2,4,2,16,128]{4,3,2,1,0:T(8,128)} %bitcast.13, bf16[4,2,4,2,16,128]{5,4,3,2,1,0:T(8,128)(2,1)} %bitcast.11), custom_call_target="tpu_custom_call" | custom-call | tf_op jit(solution)/shard_map/send/pallas_call | solution.py:402
  1.1 1.5 %collective-permute-start = (f32[8,88,128]{2,1,0:T(8,128)S(1)}, f32[8,88,128]{2,1,0:T(8,128)S(1)}, u32[]{:S(2)}, u32[]{:S(2)}) collective-permute-start(f32[8,88,128]{2,1,0:T(8,128)S(1)} %send.1), channel_id=1, source_target_pairs={{0,16},{1,17},{2,18},{3,19},{4,20},{5,21},{6,22},{7,23},{8,24},{9,... | collective-permute-start | bytes 1081352 | tf_op jit(solution)/shard_map/ppermute | solution.py:411
  2.6 1.1 %keep.1.kept_ref = f32[16,88,128]{2,1,0:T(8,128)S(1)} custom-call(s32[4,16]{1,0:T(4,128)} %bitcast.16, s32[4,16]{1,0:T(4,128)} %shifts_hbm.3, f32[2,4,2,16,128]{4,3,2,1,0:T(8,128)} %bitcast.14, bf16[4,2,4,2,16,128]{5,4,3,2,1,0:T(8,128)(2,1)} %bitcast.12), custom_call_target="tpu_custom_call" | custom-call | flops 1000000000 | bytes 4000000 | tf_op jit(solution)/shard_map/keep/pallas_call | solution.py:412
  3.7 0.0 copy-start
  3.7 0.0 copy-start.1
  3.7 0.2 collective-permute-done.other_ref
  4.0 20.8 %all_to_all.10.arrived_ref = f32[16,88,128]{2,1,0:T(8,128)S(1)} all-to-all(f32[16,88,128]{2,1,0:T(8,128)S(1)} %join.1), channel_id=1, replica_groups=mesh['gx'=8,'gy'=16] {'gy'}, dimensions={0} | all-to-all | bytes 1441792 | tf_op jit(solution)/shard_map/all_to_all | solution.py:379
  24.7 1.6 %collective-permute-start.1 = (f32[272,128]{1,0:T(8,128)S(1)}, f32[272,128]{1,0:T(8,128)S(1)}, u32[]{:S(2)}, u32[]{:S(2)}) collective-permute-start(f32[272,128]{1,0:T(8,128)S(1)} %lead.1.own_ref), channel_id=1, source_target_pairs={{0,16},{1,17},{2,18},{3,19},{4,20},{5,21},{6,22},{7,23},{8,24},{9,... | collective-permute-start | bytes 417800 | tf_op jit(solution)/shard_map/ppermute | solution.py:518
  26.3 1.2 %collective-permute-start.2 = (f32[272,128]{1,0:T(8,128)S(1)}, f32[272,128]{1,0:T(8,128)S(1)}, u32[]{:S(2)}, u32[]{:S(2)}) collective-permute-start(f32[272,128]{1,0:T(8,128)S(1)} %lead.1.own_ref), channel_id=1, source_target_pairs={{20,5},{21,6},{22,7},{23,3},{19,2},{18,1},{17,0},{16,32},{48,33},{... | collective-permute-start | bytes 417800 | tf_op jit(solution)/shard_map/ppermute | solution.py:517
  27.5 0.0 copy-done
  27.5 0.0 copy-done.1
  27.5 1.2 %taps.1 = (bf16[4,2,512,256]{3,2,1,0:T(8,128)(2,1)S(1)}, bf16[4,32,32]{2,1,0:T(8,128)(2,1)S(1)}, bf16[4,32,64]{2,1,0:T(8,128)(2,1)S(1)}, bf16[4,32,32]{2,1,0:T(8,128)(2,1)S(1)}, bf16[4,64,32]{2,1,0:T(8,128)(2,1)S(1)}) custom-call(f32[4,31]{1,0:T(4,128)S(1)} %copy-done, f32[4,31]{1,0:T(4,128)S(1)} %copy-done.1), custom_call_target="tpu_custom_call" | custom-call | tf_op jit(solution)/shard_map/taps/pallas_call | solution.py:432
  28.7 0.0 collective-permute-done.1.swapped_ref
  28.8 1.5 %front.2.near_ref = f32[4,16,2048]{2,1,0:T(8,128)S(1)} custom-call(s32[32,16]{1,0:T(8,128)S(1)} %maximum_convert_fusion.meta_ref, f32[272,128]{1,0:T(8,128)S(1)} %lead.1.own_ref, f32[272,128]{1,0:T(8,128)S(1)} %collective-permute-done.1.swapped_ref, bf16[4,32,64]{2,1,0:T(8,128)(2,1)S(1)} %get-tuple-element.18.near_in_ref), custom_call_target="tpu_custom_call" | custom-call | tf_op jit(solution)/shard_map/front/pallas_call | solution.py:523
  30.3 0.5 collective-permute-done.2.paired_ref
  30.8 2.1 %middle.2 = (f32[256,128]{1,0:T(8,128)S(1)}, f32[4,256,128]{2,1,0:T(8,128)S(1)}) custom-call(s32[16,16]{1,0:T(8,128)S(1)} %fusion.2.meta_ref, f32[272,128]{1,0:T(8,128)S(1)} %collective-permute-done.2.paired_ref, f32[4,16,2048]{2,1,0:T(8,128)S(1)} %front.2.near_ref, f32[16,88,128]{2,1,0:T(8,128)S(1)} %all_to_all.10.arrived_ref, ...), custom_call_target="tpu_custom_call" | custom-call | flops 1000000000 | bytes 4000000 | tf_op jit(solution)/shard_map/middle/pallas_call | solution.py:526
  32.9 1.3 %collective-permute-start.3 = (f32[256,128]{1,0:T(8,128)S(1)}, f32[256,128]{1,0:T(8,128)S(1)}, u32[]{:S(2)}, u32[]{:S(2)}) collective-permute-start(f32[256,128]{1,0:T(8,128)S(1)} %get-tuple-element.25), channel_id=1, source_target_pairs={{20,5},{21,6},{22,7},{23,3},{19,2},{18,1},{17,0},{16,32},{48,33},{... | collective-permute-start | bytes 393224 | tf_op jit(solution)/shard_map/ppermute | solution.py:529
  34.1 1.4 %tail.2 = (f32[256,128]{1,0:T(8,128)S(1)}, f32[256,128]{1,0:T(8,128)S(1)}) custom-call(s32[32,16]{1,0:T(8,128)S(1)} %maximum_convert_fusion.meta_ref, f32[4,256,128]{2,1,0:T(8,128)S(1)} %get-tuple-element.22.again_ref, bf16[4,64,32]{2,1,0:T(8,128)(2,1)S(1)} %get-tuple-element.23.near_back_ref), custom_call_target="tpu_custom_call" | custom-call | flops 1000000000 | bytes 4000000 | tf_op jit(solution)/shard_map/tail/pallas_call | solution.py:527
  35.6 0.1 collective-permute-start.4
  35.6 1.7 %collective-permute-done.3.paired_ref = f32[256,128]{1,0:T(8,128)S(1)} collective-permute-done((f32[256,128]{1,0:T(8,128)S(1)}, f32[256,128]{1,0:T(8,128)S(1)}, u32[]{:S(2)}, u32[]{:S(2)}) %collective-permute-start.3) | collective-permute-done | bytes 131104 | tf_op jit(solution)/shard_map/ppermute | solution.py:529
  37.4 0.0 collective-permute-done.4.swapped_ref
  37.4 0.2 collective-permute-start.6
  37.6 1.5 %collective-permute-start.5 = (f32[256,128]{1,0:T(8,128)S(1)}, f32[256,128]{1,0:T(8,128)S(1)}, u32[]{:S(2)}, u32[]{:S(2)}) collective-permute-start(f32[256,128]{1,0:T(8,128)S(1)} %update.1.own_ref), channel_id=1, source_target_pairs={{20,5},{21,6},{22,7},{23,3},{19,2},{18,1},{17,0},{16,32},{48,33},{... | collective-permute-start | bytes 393224 | tf_op jit(solution)/shard_map/ppermute | solution.py:517
  39.1 0.0 collective-permute-done.6.swapped_ref
  39.1 1.5 %front.3.near_ref = f32[4,16,2048]{2,1,0:T(8,128)S(1)} custom-call(s32[32,16]{1,0:T(8,128)S(1)} %maximum_convert_fusion.meta_ref, f32[256,128]{1,0:T(8,128)S(1)} %update.1.own_ref, f32[256,128]{1,0:T(8,128)S(1)} %collective-permute-done.6.swapped_ref, bf16[4,32,64]{2,1,0:T(8,128)(2,1)S(1)} %get-tuple-element.18.near_in_ref), custom_call_target="tpu_custom_call" | custom-call | tf_op jit(solution)/shard_map/front/pallas_call | solution.py:523
  40.6 1.4 %collective-permute-done.5.paired_ref = f32[256,128]{1,0:T(8,128)S(1)} collective-permute-done((f32[256,128]{1,0:T(8,128)S(1)}, f32[256,128]{1,0:T(8,128)S(1)}, u32[]{:S(2)}, u32[]{:S(2)}) %collective-permute-start.5) | collective-permute-done | bytes 131104 | tf_op jit(solution)/shard_map/ppermute | solution.py:517
  42.0 2.1 %middle.3 = (f32[256,128]{1,0:T(8,128)S(1)}, f32[4,256,128]{2,1,0:T(8,128)S(1)}) custom-call(s32[16,16]{1,0:T(8,128)S(1)} %fusion.2.meta_ref, f32[256,128]{1,0:T(8,128)S(1)} %collective-permute-done.5.paired_ref, f32[4,16,2048]{2,1,0:T(8,128)S(1)} %front.3.near_ref, f32[16,88,128]{2,1,0:T(8,128)S(1)} %all_to_all.10.arrived_ref, ...), custom_call_target="tpu_custom_call" | custom-call | flops 1000000000 | bytes 4000000 | tf_op jit(solution)/shard_map/middle/pallas_call | solution.py:526
  44.1 1.6 %collective-permute-start.7 = (f32[256,128]{1,0:T(8,128)S(1)}, f32[256,128]{1,0:T(8,128)S(1)}, u32[]{:S(2)}, u32[]{:S(2)}) collective-permute-start(f32[256,128]{1,0:T(8,128)S(1)} %get-tuple-element.29), channel_id=1, source_target_pairs={{20,5},{21,6},{22,7},{23,3},{19,2},{18,1},{17,0},{16,32},{48,33},{... | collective-permute-start | bytes 393224 | tf_op jit(solution)/shard_map/ppermute | solution.py:529
  45.7 1.4 %tail.3 = (f32[256,128]{1,0:T(8,128)S(1)}, f32[256,128]{1,0:T(8,128)S(1)}) custom-call(s32[32,16]{1,0:T(8,128)S(1)} %maximum_convert_fusion.meta_ref, f32[4,256,128]{2,1,0:T(8,128)S(1)} %get-tuple-element.27.again_ref, bf16[4,64,32]{2,1,0:T(8,128)(2,1)S(1)} %get-tuple-element.23.near_back_ref), custom_call_target="tpu_custom_call" | custom-call | flops 1000000000 | bytes 4000000 | tf_op jit(solution)/shard_map/tail/pallas_call | solution.py:527
  47.1 0.1 collective-permute-start.8
  47.2 1.4 %collective-permute-done.7.paired_ref = f32[256,128]{1,0:T(8,128)S(1)} collective-permute-done((f32[256,128]{1,0:T(8,128)S(1)}, f32[256,128]{1,0:T(8,128)S(1)}, u32[]{:S(2)}, u32[]{:S(2)}) %collective-permute-start.7) | collective-permute-done | bytes 131104 | tf_op jit(solution)/shard_map/ppermute | solution.py:529
  48.6 0.0 collective-permute-done.8.swapped_ref
  48.6 12.8 %all_to_all.11.home_ref = f32[32,16,128]{2,1,0:T(8,128)S(1)} all-to-all(f32[32,16,128]{2,1,0:T(8,128)S(1)} %bitcast.10), channel_id=1, replica_groups={{0,1,2,3,4,5,6,7,8,9,10,11,12,13,14,15,16,17,18,19,20,21,22,23,24,25,26..., dimensions={0} | all-to-all | bytes 524288 | tf_op jit(solution)/shard_map/all_to_all | solution.py:532
  61.4 0.7 %unpack.1 = f32[2,128,128]{2,1,0:T(8,128)} custom-call(f32[32,16,128]{2,1,0:T(8,128)S(1)} %all_to_all.11.home_ref), custom_call_target="tpu_custom_call" | custom-call | tf_op jit(solution)/shard_map/unpack/pallas_call | solution.py:535
  (10 shorter events, 0.2 us)
Async XLA Ops:
  1.1 2.8 %collective-permute-start = (f32[8,88,128]{2,1,0:T(8,128)S(1)}, f32[8,88,128]{2,1,0:T(8,128)S(1)}, u32[]{:S(2)}, u32[]{:S(2)}) collective-permute-start(f32[8,88,128]{2,1,0:T(8,128)S(1)} %send.1), channel_id=1, source_target_pairs={{0,16},{1,17},{2,18},{3,19},{4,20},{5,21},{6,22},{7,23},{8,24},{9,... | collective-permute-start | bytes 1081352 | tf_op jit(solution)/shard_map/ppermute | solution.py:411
  3.7 23.8 %copy-start = (f32[4,31]{1,0:T(4,128)S(1)}, f32[4,31]{1,0:T(4,128)}, u32[]{:S(2)}) copy-start(f32[4,31]{1,0:T(4,128)} %psf_rows_ref.1) | copy-start | bytes 1492
  3.7 23.8 %copy-start.1 = (f32[4,31]{1,0:T(4,128)S(1)}, f32[4,31]{1,0:T(4,128)}, u32[]{:S(2)}) copy-start(f32[4,31]{1,0:T(4,128)} %psf_cols_ref.1) | copy-start | bytes 1492
  24.7 4.0 %collective-permute-start.1 = (f32[272,128]{1,0:T(8,128)S(1)}, f32[272,128]{1,0:T(8,128)S(1)}, u32[]{:S(2)}, u32[]{:S(2)}) collective-permute-start(f32[272,128]{1,0:T(8,128)S(1)} %lead.1.own_ref), channel_id=1, source_target_pairs={{0,16},{1,17},{2,18},{3,19},{4,20},{5,21},{6,22},{7,23},{8,24},{9,... | collective-permute-start | bytes 417800 | tf_op jit(solution)/shard_map/ppermute | solution.py:518
  26.3 4.5 %collective-permute-start.2 = (f32[272,128]{1,0:T(8,128)S(1)}, f32[272,128]{1,0:T(8,128)S(1)}, u32[]{:S(2)}, u32[]{:S(2)}) collective-permute-start(f32[272,128]{1,0:T(8,128)S(1)} %lead.1.own_ref), channel_id=1, source_target_pairs={{20,5},{21,6},{22,7},{23,3},{19,2},{18,1},{17,0},{16,32},{48,33},{... | collective-permute-start | bytes 417800 | tf_op jit(solution)/shard_map/ppermute | solution.py:517
  32.9 4.5 %collective-permute-start.3 = (f32[256,128]{1,0:T(8,128)S(1)}, f32[256,128]{1,0:T(8,128)S(1)}, u32[]{:S(2)}, u32[]{:S(2)}) collective-permute-start(f32[256,128]{1,0:T(8,128)S(1)} %get-tuple-element.25), channel_id=1, source_target_pairs={{20,5},{21,6},{22,7},{23,3},{19,2},{18,1},{17,0},{16,32},{48,33},{... | collective-permute-start | bytes 393224 | tf_op jit(solution)/shard_map/ppermute | solution.py:529
  35.6 1.8 %collective-permute-start.4 = (f32[256,128]{1,0:T(8,128)S(1)}, f32[256,128]{1,0:T(8,128)S(1)}, u32[]{:S(2)}, u32[]{:S(2)}) collective-permute-start(f32[256,128]{1,0:T(8,128)S(1)} %get-tuple-element.26), channel_id=1, source_target_pairs={{0,16},{1,17},{2,18},{3,19},{4,20},{5,21},{6,22},{7,23},{8,24},{9,... | collective-permute-start | bytes 393224 | tf_op jit(solution)/shard_map/ppermute | solution.py:529
  37.4 1.7 %collective-permute-start.6 = (f32[256,128]{1,0:T(8,128)S(1)}, f32[256,128]{1,0:T(8,128)S(1)}, u32[]{:S(2)}, u32[]{:S(2)}) collective-permute-start(f32[256,128]{1,0:T(8,128)S(1)} %update.1.own_ref), channel_id=1, source_target_pairs={{0,16},{1,17},{2,18},{3,19},{4,20},{5,21},{6,22},{7,23},{8,24},{9,... | collective-permute-start | bytes 393224 | tf_op jit(solution)/shard_map/ppermute | solution.py:518
  37.6 4.4 %collective-permute-start.5 = (f32[256,128]{1,0:T(8,128)S(1)}, f32[256,128]{1,0:T(8,128)S(1)}, u32[]{:S(2)}, u32[]{:S(2)}) collective-permute-start(f32[256,128]{1,0:T(8,128)S(1)} %update.1.own_ref), channel_id=1, source_target_pairs={{20,5},{21,6},{22,7},{23,3},{19,2},{18,1},{17,0},{16,32},{48,33},{... | collective-permute-start | bytes 393224 | tf_op jit(solution)/shard_map/ppermute | solution.py:517
  44.1 4.5 %collective-permute-start.7 = (f32[256,128]{1,0:T(8,128)S(1)}, f32[256,128]{1,0:T(8,128)S(1)}, u32[]{:S(2)}, u32[]{:S(2)}) collective-permute-start(f32[256,128]{1,0:T(8,128)S(1)} %get-tuple-element.29), channel_id=1, source_target_pairs={{20,5},{21,6},{22,7},{23,3},{19,2},{18,1},{17,0},{16,32},{48,33},{... | collective-permute-start | bytes 393224 | tf_op jit(solution)/shard_map/ppermute | solution.py:529
  47.1 1.5 %collective-permute-start.8 = (f32[256,128]{1,0:T(8,128)S(1)}, f32[256,128]{1,0:T(8,128)S(1)}, u32[]{:S(2)}, u32[]{:S(2)}) collective-permute-start(f32[256,128]{1,0:T(8,128)S(1)} %get-tuple-element.30), channel_id=1, source_target_pairs={{0,16},{1,17},{2,18},{3,19},{4,20},{5,21},{6,22},{7,23},{8,24},{9,... | collective-permute-start | bytes 393224 | tf_op jit(solution)/shard_map/ppermute | solution.py:529

commit v9 on v8

--- a/solution.py
+++ b/solution.py
@@ -76,13 +76,16 @@
 
 def pack(sub, slot_of, out_ref, codes_hbm, shifts_hbm, est_hbm, views_hbm, codes_ref, shifts_ref, est, views, sems):
     core, _ = own_tile_inner()
+    planes = [
+        pltpu.make_async_copy(views_hbm.at[:, p, :, sub], views.at[:, p], sems.at[3 + p])
+        for p in range(Z)
+    ]
     copies = [
         pltpu.make_async_copy(codes_hbm, codes_ref, sems.at[0]),
         pltpu.make_async_copy(shifts_hbm, shifts_ref, sems.at[1]),
         pltpu.make_async_copy(est_hbm.at[:, :, sub], est, sems.at[2]),
-        pltpu.make_async_copy(views_hbm.at[:, :, :, sub], views, sems.at[3]),
-    ]
-    for copy in copies:
+    ]
+    for copy in copies + planes:
         copy.start()
     for copy in copies:
         copy.wait()
@@ -98,9 +101,13 @@
                 meta = jnp.where(lane == half * V + v, code, meta)
                 meta = jnp.where(lane == 8 + half * V + v, shift, meta)
         out_ref[at, 0:ROWS, :] = est[plane, part]
+        out_ref[at, pl.ds(ROWS * (1 + V), 8), :] = meta
+    for slot in range(8):
+        plane, part, at = slot // 4, part_of(slot % 4, core), slot_of(slot)
+        if slot % 4 == 0:
+            planes[plane].wait()
         for v in range(V):
             out_ref[at, pl.ds(ROWS * (1 + v), ROWS), :] = views[v, plane, part].astype(F32)
-        out_ref[at, pl.ds(ROWS * (1 + V), 8), :] = meta
 
 
 def halves(near):
@@ -395,7 +402,7 @@
         pltpu.SMEM((V, 2 * 8), jnp.int32),
         pltpu.VMEM((Z, 4, ROWS, T), F32),
         pltpu.VMEM((V, Z, 4, ROWS, T), BF16),
-        pltpu.SemaphoreType.DMA((4,)),
+        pltpu.SemaphoreType.DMA((5,)),
     ]
     unit = jax.ShapeDtypeStruct((8, UNIT, T), F32)
     whole = jax.ShapeDtypeStruct((GY, UNIT, T), F32)

time: 62.3 us -> 62.3 us (level)
  no operation moved by 1% of the time
where the time goes in v9:
time: 62.3 us; the launch traced here: 62 us
  blocking collectives  33.5 us (54%)
  Pallas kernels  14.1 us (23%)
  starting transfers between devices  8.97 us (14%)
  waiting for transfers between devices  5.25 us (8%)
    all_to_all x1, blocking collectives, all_to_all(): return lax.all_to_all(blocks, 'gy', split_axis=0, concat_axis=0, tiled=True)  20.8 us
    all_to_all x1, blocking collectives, body(): lax.all_to_all(blocks, AXES, split_axis=0, concat_axis=0, tiled=True, axi...  12.8 us
    pallas_call x2, Pallas kernels, body(): middle(pair_meta, paired, near, arrived, band, pair_in, pair_back)  4.14 us
    ppermute x2, waiting for transfers between devices, body(): lax.ppermute(pair, AXES, PAIR)  3.1 us
    pallas_call x2, Pallas kernels, body(): near = front(near_meta, own, swapped, near_in)  3.02 us
    ppermute x2, starting transfers between devices, body(): lax.ppermute(pair, AXES, PAIR)  2.85 us
    pallas_call x2, Pallas kernels, body(): mid, swap = tail(near_meta, again, near_back)  2.8 us
    ppermute x2, starting transfers between devices, body(): paired = lax.ppermute(own, AXES, PAIR)  2.71 us
  transfers between devices with their start and end apart: 9, of which 5 were waited for; matrix products, arithmetic and copies ran while one was open for 0% of the time, Pallas kernels for 13%

profile of v9, /device:TPU:1, one launch (start us, length us, event | category | flops | bytes accessed | tf_op | source)
XLA Modules:
  0.0 62.0 jit_solution(14392157780021247271)
XLA Ops:
  0.0 1.0 %send.1 = f32[8,88,128]{2,1,0:T(8,128)S(1)} custom-call(s32[4,16]{1,0:T(4,128)} %bitcast.15, s32[4,16]{1,0:T(4,128)} %shifts_hbm.3, f32[2,4,2,16,128]{4,3,2,1,0:T(8,128)} %bitcast.13, bf16[4,2,4,2,16,128]{5,4,3,2,1,0:T(8,128)(2,1)} %bitcast.11), custom_call_target="tpu_custom_call" | custom-call | tf_op jit(solution)/shard_map/send/pallas_call | solution.py:409
  1.0 1.5 %collective-permute-start = (f32[8,88,128]{2,1,0:T(8,128)S(1)}, f32[8,88,128]{2,1,0:T(8,128)S(1)}, u32[]{:S(2)}, u32[]{:S(2)}) collective-permute-start(f32[8,88,128]{2,1,0:T(8,128)S(1)} %send.1), channel_id=1, source_target_pairs={{0,16},{1,17},{2,18},{3,19},{4,20},{5,21},{6,22},{7,23},{8,24},{9,... | collective-permute-start | bytes 1081352 | tf_op jit(solution)/shard_map/ppermute | solution.py:418
  2.5 1.0 %keep.1.kept_ref = f32[16,88,128]{2,1,0:T(8,128)S(1)} custom-call(s32[4,16]{1,0:T(4,128)} %bitcast.16, s32[4,16]{1,0:T(4,128)} %shifts_hbm.3, f32[2,4,2,16,128]{4,3,2,1,0:T(8,128)} %bitcast.14, bf16[4,2,4,2,16,128]{5,4,3,2,1,0:T(8,128)(2,1)} %bitcast.12), custom_call_target="tpu_custom_call" | custom-call | flops 1000000000 | bytes 4000000 | tf_op jit(solution)/shard_map/keep/pallas_call | solution.py:419
  3.6 0.0 copy-start
  3.6 0.0 copy-start.1
  3.6 0.3 collective-permute-done.other_ref
  3.9 20.8 %all_to_all.10.arrived_ref = f32[16,88,128]{2,1,0:T(8,128)S(1)} all-to-all(f32[16,88,128]{2,1,0:T(8,128)S(1)} %join.1), channel_id=1, replica_groups=mesh['gx'=8,'gy'=16] {'gy'}, dimensions={0} | all-to-all | bytes 1441792 | tf_op jit(solution)/shard_map/all_to_all | solution.py:386
  24.7 1.6 %collective-permute-start.1 = (f32[272,128]{1,0:T(8,128)S(1)}, f32[272,128]{1,0:T(8,128)S(1)}, u32[]{:S(2)}, u32[]{:S(2)}) collective-permute-start(f32[272,128]{1,0:T(8,128)S(1)} %lead.1.own_ref), channel_id=1, source_target_pairs={{0,16},{1,17},{2,18},{3,19},{4,20},{5,21},{6,22},{7,23},{8,24},{9,... | collective-permute-start | bytes 417800 | tf_op jit(solution)/shard_map/ppermute | solution.py:525
  26.2 1.2 %collective-permute-start.2 = (f32[272,128]{1,0:T(8,128)S(1)}, f32[272,128]{1,0:T(8,128)S(1)}, u32[]{:S(2)}, u32[]{:S(2)}) collective-permute-start(f32[272,128]{1,0:T(8,128)S(1)} %lead.1.own_ref), channel_id=1, source_target_pairs={{20,5},{21,6},{22,7},{23,3},{19,2},{18,1},{17,0},{16,32},{48,33},{... | collective-permute-start | bytes 417800 | tf_op jit(solution)/shard_map/ppermute | solution.py:524
  27.4 0.0 copy-done
  27.4 0.0 copy-done.1
  27.4 1.2 %taps.1 = (bf16[4,2,512,256]{3,2,1,0:T(8,128)(2,1)S(1)}, bf16[4,32,32]{2,1,0:T(8,128)(2,1)S(1)}, bf16[4,32,64]{2,1,0:T(8,128)(2,1)S(1)}, bf16[4,32,32]{2,1,0:T(8,128)(2,1)S(1)}, bf16[4,64,32]{2,1,0:T(8,128)(2,1)S(1)}) custom-call(f32[4,31]{1,0:T(4,128)S(1)} %copy-done, f32[4,31]{1,0:T(4,128)S(1)} %copy-done.1), custom_call_target="tpu_custom_call" | custom-call | tf_op jit(solution)/shard_map/taps/pallas_call | solution.py:439
  28.6 0.0 collective-permute-done.1.swapped_ref
  28.7 1.5 %front.2.near_ref = f32[4,16,2048]{2,1,0:T(8,128)S(1)} custom-call(s32[32,16]{1,0:T(8,128)S(1)} %maximum_convert_fusion.meta_ref, f32[272,128]{1,0:T(8,128)S(1)} %lead.1.own_ref, f32[272,128]{1,0:T(8,128)S(1)} %collective-permute-done.1.swapped_ref, bf16[4,32,64]{2,1,0:T(8,128)(2,1)S(1)} %get-tuple-element.18.near_in_ref), custom_call_target="tpu_custom_call" | custom-call | tf_op jit(solution)/shard_map/front/pallas_call | solution.py:530
  30.2 0.5 collective-permute-done.2.paired_ref
  30.7 2.1 %middle.2 = (f32[256,128]{1,0:T(8,128)S(1)}, f32[4,256,128]{2,1,0:T(8,128)S(1)}) custom-call(s32[16,16]{1,0:T(8,128)S(1)} %fusion.2.meta_ref, f32[272,128]{1,0:T(8,128)S(1)} %collective-permute-done.2.paired_ref, f32[4,16,2048]{2,1,0:T(8,128)S(1)} %front.2.near_ref, f32[16,88,128]{2,1,0:T(8,128)S(1)} %all_to_all.10.arrived_ref, ...), custom_call_target="tpu_custom_call" | custom-call | flops 1000000000 | bytes 4000000 | tf_op jit(solution)/shard_map/middle/pallas_call | solution.py:533
  32.8 1.3 %collective-permute-start.3 = (f32[256,128]{1,0:T(8,128)S(1)}, f32[256,128]{1,0:T(8,128)S(1)}, u32[]{:S(2)}, u32[]{:S(2)}) collective-permute-start(f32[256,128]{1,0:T(8,128)S(1)} %get-tuple-element.25), channel_id=1, source_target_pairs={{20,5},{21,6},{22,7},{23,3},{19,2},{18,1},{17,0},{16,32},{48,33},{... | collective-permute-start | bytes 393224 | tf_op jit(solution)/shard_map/ppermute | solution.py:536
  34.1 1.4 %tail.2 = (f32[256,128]{1,0:T(8,128)S(1)}, f32[256,128]{1,0:T(8,128)S(1)}) custom-call(s32[32,16]{1,0:T(8,128)S(1)} %maximum_convert_fusion.meta_ref, f32[4,256,128]{2,1,0:T(8,128)S(1)} %get-tuple-element.22.again_ref, bf16[4,64,32]{2,1,0:T(8,128)(2,1)S(1)} %get-tuple-element.23.near_back_ref), custom_call_target="tpu_custom_call" | custom-call | flops 1000000000 | bytes 4000000 | tf_op jit(solution)/shard_map/tail/pallas_call | solution.py:534
  35.5 0.1 collective-permute-start.4
  35.6 1.7 %collective-permute-done.3.paired_ref = f32[256,128]{1,0:T(8,128)S(1)} collective-permute-done((f32[256,128]{1,0:T(8,128)S(1)}, f32[256,128]{1,0:T(8,128)S(1)}, u32[]{:S(2)}, u32[]{:S(2)}) %collective-permute-start.3) | collective-permute-done | bytes 131104 | tf_op jit(solution)/shard_map/ppermute | solution.py:536
  37.3 0.0 collective-permute-done.4.swapped_ref
  37.3 0.2 collective-permute-start.6
  37.5 1.5 %collective-permute-start.5 = (f32[256,128]{1,0:T(8,128)S(1)}, f32[256,128]{1,0:T(8,128)S(1)}, u32[]{:S(2)}, u32[]{:S(2)}) collective-permute-start(f32[256,128]{1,0:T(8,128)S(1)} %update.1.own_ref), channel_id=1, source_target_pairs={{20,5},{21,6},{22,7},{23,3},{19,2},{18,1},{17,0},{16,32},{48,33},{... | collective-permute-start | bytes 393224 | tf_op jit(solution)/shard_map/ppermute | solution.py:524
  39.0 0.0 collective-permute-done.6.swapped_ref
  39.0 1.5 %front.3.near_ref = f32[4,16,2048]{2,1,0:T(8,128)S(1)} custom-call(s32[32,16]{1,0:T(8,128)S(1)} %maximum_convert_fusion.meta_ref, f32[256,128]{1,0:T(8,128)S(1)} %update.1.own_ref, f32[256,128]{1,0:T(8,128)S(1)} %collective-permute-done.6.swapped_ref, bf16[4,32,64]{2,1,0:T(8,128)(2,1)S(1)} %get-tuple-element.18.near_in_ref), custom_call_target="tpu_custom_call" | custom-call | tf_op jit(solution)/shard_map/front/pallas_call | solution.py:530
  40.5 1.4 %collective-permute-done.5.paired_ref = f32[256,128]{1,0:T(8,128)S(1)} collective-permute-done((f32[256,128]{1,0:T(8,128)S(1)}, f32[256,128]{1,0:T(8,128)S(1)}, u32[]{:S(2)}, u32[]{:S(2)}) %collective-permute-start.5) | collective-permute-done | bytes 131104 | tf_op jit(solution)/shard_map/ppermute | solution.py:524
  41.9 2.1 %middle.3 = (f32[256,128]{1,0:T(8,128)S(1)}, f32[4,256,128]{2,1,0:T(8,128)S(1)}) custom-call(s32[16,16]{1,0:T(8,128)S(1)} %fusion.2.meta_ref, f32[256,128]{1,0:T(8,128)S(1)} %collective-permute-done.5.paired_ref, f32[4,16,2048]{2,1,0:T(8,128)S(1)} %front.3.near_ref, f32[16,88,128]{2,1,0:T(8,128)S(1)} %all_to_all.10.arrived_ref, ...), custom_call_target="tpu_custom_call" | custom-call | flops 1000000000 | bytes 4000000 | tf_op jit(solution)/shard_map/middle/pallas_call | solution.py:533
  44.0 1.6 %collective-permute-start.7 = (f32[256,128]{1,0:T(8,128)S(1)}, f32[256,128]{1,0:T(8,128)S(1)}, u32[]{:S(2)}, u32[]{:S(2)}) collective-permute-start(f32[256,128]{1,0:T(8,128)S(1)} %get-tuple-element.29), channel_id=1, source_target_pairs={{20,5},{21,6},{22,7},{23,3},{19,2},{18,1},{17,0},{16,32},{48,33},{... | collective-permute-start | bytes 393224 | tf_op jit(solution)/shard_map/ppermute | solution.py:536
  45.6 1.4 %tail.3 = (f32[256,128]{1,0:T(8,128)S(1)}, f32[256,128]{1,0:T(8,128)S(1)}) custom-call(s32[32,16]{1,0:T(8,128)S(1)} %maximum_convert_fusion.meta_ref, f32[4,256,128]{2,1,0:T(8,128)S(1)} %get-tuple-element.27.again_ref, bf16[4,64,32]{2,1,0:T(8,128)(2,1)S(1)} %get-tuple-element.23.near_back_ref), custom_call_target="tpu_custom_call" | custom-call | flops 1000000000 | bytes 4000000 | tf_op jit(solution)/shard_map/tail/pallas_call | solution.py:534
  47.0 0.1 collective-permute-start.8
  47.1 1.4 %collective-permute-done.7.paired_ref = f32[256,128]{1,0:T(8,128)S(1)} collective-permute-done((f32[256,128]{1,0:T(8,128)S(1)}, f32[256,128]{1,0:T(8,128)S(1)}, u32[]{:S(2)}, u32[]{:S(2)}) %collective-permute-start.7) | collective-permute-done | bytes 131104 | tf_op jit(solution)/shard_map/ppermute | solution.py:536
  48.5 0.0 collective-permute-done.8.swapped_ref
  48.6 12.8 %all_to_all.11.home_ref = f32[32,16,128]{2,1,0:T(8,128)S(1)} all-to-all(f32[32,16,128]{2,1,0:T(8,128)S(1)} %bitcast.10), channel_id=1, replica_groups={{0,1,2,3,4,5,6,7,8,9,10,11,12,13,14,15,16,17,18,19,20,21,22,23,24,25,26..., dimensions={0} | all-to-all | bytes 524288 | tf_op jit(solution)/shard_map/all_to_all | solution.py:539
  61.3 0.7 %unpack.1 = f32[2,128,128]{2,1,0:T(8,128)} custom-call(f32[32,16,128]{2,1,0:T(8,128)S(1)} %all_to_all.11.home_ref), custom_call_target="tpu_custom_call" | custom-call | tf_op jit(solution)/shard_map/unpack/pallas_call | solution.py:542
  (10 shorter events, 0.2 us)
Async XLA Ops:
  1.0 2.8 %collective-permute-start = (f32[8,88,128]{2,1,0:T(8,128)S(1)}, f32[8,88,128]{2,1,0:T(8,128)S(1)}, u32[]{:S(2)}, u32[]{:S(2)}) collective-permute-start(f32[8,88,128]{2,1,0:T(8,128)S(1)} %send.1), channel_id=1, source_target_pairs={{0,16},{1,17},{2,18},{3,19},{4,20},{5,21},{6,22},{7,23},{8,24},{9,... | collective-permute-start | bytes 1081352 | tf_op jit(solution)/shard_map/ppermute | solution.py:418
  3.6 23.9 %copy-start = (f32[4,31]{1,0:T(4,128)S(1)}, f32[4,31]{1,0:T(4,128)}, u32[]{:S(2)}) copy-start(f32[4,31]{1,0:T(4,128)} %psf_rows_ref.1) | copy-start | bytes 1492
  3.6 23.9 %copy-start.1 = (f32[4,31]{1,0:T(4,128)S(1)}, f32[4,31]{1,0:T(4,128)}, u32[]{:S(2)}) copy-start(f32[4,31]{1,0:T(4,128)} %psf_cols_ref.1) | copy-start | bytes 1492
  24.7 4.0 %collective-permute-start.1 = (f32[272,128]{1,0:T(8,128)S(1)}, f32[272,128]{1,0:T(8,128)S(1)}, u32[]{:S(2)}, u32[]{:S(2)}) collective-permute-start(f32[272,128]{1,0:T(8,128)S(1)} %lead.1.own_ref), channel_id=1, source_target_pairs={{0,16},{1,17},{2,18},{3,19},{4,20},{5,21},{6,22},{7,23},{8,24},{9,... | collective-permute-start | bytes 417800 | tf_op jit(solution)/shard_map/ppermute | solution.py:525
  26.2 4.5 %collective-permute-start.2 = (f32[272,128]{1,0:T(8,128)S(1)}, f32[272,128]{1,0:T(8,128)S(1)}, u32[]{:S(2)}, u32[]{:S(2)}) collective-permute-start(f32[272,128]{1,0:T(8,128)S(1)} %lead.1.own_ref), channel_id=1, source_target_pairs={{20,5},{21,6},{22,7},{23,3},{19,2},{18,1},{17,0},{16,32},{48,33},{... | collective-permute-start | bytes 417800 | tf_op jit(solution)/shard_map/ppermute | solution.py:524
  32.8 4.5 %collective-permute-start.3 = (f32[256,128]{1,0:T(8,128)S(1)}, f32[256,128]{1,0:T(8,128)S(1)}, u32[]{:S(2)}, u32[]{:S(2)}) collective-permute-start(f32[256,128]{1,0:T(8,128)S(1)} %get-tuple-element.25), channel_id=1, source_target_pairs={{20,5},{21,6},{22,7},{23,3},{19,2},{18,1},{17,0},{16,32},{48,33},{... | collective-permute-start | bytes 393224 | tf_op jit(solution)/shard_map/ppermute | solution.py:536
  35.5 1.8 %collective-permute-start.4 = (f32[256,128]{1,0:T(8,128)S(1)}, f32[256,128]{1,0:T(8,128)S(1)}, u32[]{:S(2)}, u32[]{:S(2)}) collective-permute-start(f32[256,128]{1,0:T(8,128)S(1)} %get-tuple-element.26), channel_id=1, source_target_pairs={{0,16},{1,17},{2,18},{3,19},{4,20},{5,21},{6,22},{7,23},{8,24},{9,... | collective-permute-start | bytes 393224 | tf_op jit(solution)/shard_map/ppermute | solution.py:536
  37.3 1.7 %collective-permute-start.6 = (f32[256,128]{1,0:T(8,128)S(1)}, f32[256,128]{1,0:T(8,128)S(1)}, u32[]{:S(2)}, u32[]{:S(2)}) collective-permute-start(f32[256,128]{1,0:T(8,128)S(1)} %update.1.own_ref), channel_id=1, source_target_pairs={{0,16},{1,17},{2,18},{3,19},{4,20},{5,21},{6,22},{7,23},{8,24},{9,... | collective-permute-start | bytes 393224 | tf_op jit(solution)/shard_map/ppermute | solution.py:525
  37.5 4.4 %collective-permute-start.5 = (f32[256,128]{1,0:T(8,128)S(1)}, f32[256,128]{1,0:T(8,128)S(1)}, u32[]{:S(2)}, u32[]{:S(2)}) collective-permute-start(f32[256,128]{1,0:T(8,128)S(1)} %update.1.own_ref), channel_id=1, source_target_pairs={{20,5},{21,6},{22,7},{23,3},{19,2},{18,1},{17,0},{16,32},{48,33},{... | collective-permute-start | bytes 393224 | tf_op jit(solution)/shard_map/ppermute | solution.py:524
  44.0 4.5 %collective-permute-start.7 = (f32[256,128]{1,0:T(8,128)S(1)}, f32[256,128]{1,0:T(8,128)S(1)}, u32[]{:S(2)}, u32[]{:S(2)}) collective-permute-start(f32[256,128]{1,0:T(8,128)S(1)} %get-tuple-element.29), channel_id=1, source_target_pairs={{20,5},{21,6},{22,7},{23,3},{19,2},{18,1},{17,0},{16,32},{48,33},{... | collective-permute-start | bytes 393224 | tf_op jit(solution)/shard_map/ppermute | solution.py:536
  47.0 1.5 %collective-permute-start.8 = (f32[256,128]{1,0:T(8,128)S(1)}, f32[256,128]{1,0:T(8,128)S(1)}, u32[]{:S(2)}, u32[]{:S(2)}) collective-permute-start(f32[256,128]{1,0:T(8,128)S(1)} %get-tuple-element.30), channel_id=1, source_target_pairs={{0,16},{1,17},{2,18},{3,19},{4,20},{5,21},{6,22},{7,23},{8,24},{9,... | collective-permute-start | bytes 393224 | tf_op jit(solution)/shard_map/ppermute | solution.py:536

commit v10 on v8

--- a/solution.py
+++ b/solution.py
@@ -144,12 +144,11 @@
     out_ref[...] = own_ref[0 : GY * ROWS, :] * (total * 0.25)
 
 
-def twice_kernel(own_ref, near_ref, paired_ref, swapped_ref, out_ref):
+def twice_kernel(own_ref, mid_ref, paired_ref, swapped_ref, out_ref):
+    total = mid_ref[...] + paired_ref[...] + swapped_ref[...]
+    updated = own_ref[0 : GY * ROWS, :] * (total * 0.25)
     for copy in range(2):
-        update_kernel(
-            own_ref, near_ref, paired_ref, swapped_ref,
-            out_ref.at[GY * ROWS * copy : GY * ROWS * (copy + 1)],
-        )
+        out_ref[GY * ROWS * copy : GY * ROWS * (copy + 1), :] = updated
 
 
 def unpack_kernel(home_ref, out_ref):

time: 62.3 us -> 62.3 us (level)
  no operation moved by 1% of the time
where the time goes in v10:
time: 62.3 us; the launch traced here: 62.1 us
  blocking collectives  33.5 us (54%)
  Pallas kernels  14.2 us (23%)
  starting transfers between devices  8.95 us (14%)
  waiting for transfers between devices  5.2 us (8%)
    all_to_all x1, blocking collectives, all_to_all(): return lax.all_to_all(blocks, 'gy', split_axis=0, concat_axis=0, tiled=True)  20.8 us
    all_to_all x1, blocking collectives, body(): lax.all_to_all(blocks, AXES, split_axis=0, concat_axis=0, tiled=True, axi...  12.8 us
    pallas_call x2, Pallas kernels, body(): middle(pair_meta, paired, near, arrived, band, pair_in, pair_back)  4.15 us
    ppermute x2, waiting for transfers between devices, body(): lax.ppermute(pair, AXES, PAIR)  3.11 us
    pallas_call x2, Pallas kernels, body(): near = front(near_meta, own, swapped, near_in)  3.01 us
    ppermute x2, starting transfers between devices, body(): lax.ppermute(pair, AXES, PAIR)  2.84 us
    pallas_call x2, Pallas kernels, body(): mid, swap = tail(near_meta, again, near_back)  2.8 us
    ppermute x2, starting transfers between devices, body(): paired = lax.ppermute(own, AXES, PAIR)  2.7 us
  transfers between devices with their start and end apart: 9, of which 5 were waited for; matrix products, arithmetic and copies ran while one was open for 0% of the time, Pallas kernels for 13%

profile of v10, /device:TPU:1, one launch (start us, length us, event | category | flops | bytes accessed | tf_op | source)
XLA Modules:
  0.0 62.1 jit_solution(13602450731003741217)
XLA Ops:
  0.0 1.1 %send.1 = f32[8,88,128]{2,1,0:T(8,128)S(1)} custom-call(s32[4,16]{1,0:T(4,128)} %bitcast.15, s32[4,16]{1,0:T(4,128)} %shifts_hbm.3, f32[2,4,2,16,128]{4,3,2,1,0:T(8,128)} %bitcast.13, bf16[4,2,4,2,16,128]{5,4,3,2,1,0:T(8,128)(2,1)} %bitcast.11), custom_call_target="tpu_custom_call" | custom-call | tf_op jit(solution)/shard_map/send/pallas_call | solution.py:401
  1.1 1.5 %collective-permute-start = (f32[8,88,128]{2,1,0:T(8,128)S(1)}, f32[8,88,128]{2,1,0:T(8,128)S(1)}, u32[]{:S(2)}, u32[]{:S(2)}) collective-permute-start(f32[8,88,128]{2,1,0:T(8,128)S(1)} %send.1), channel_id=1, source_target_pairs={{0,16},{1,17},{2,18},{3,19},{4,20},{5,21},{6,22},{7,23},{8,24},{9,... | collective-permute-start | bytes 1081352 | tf_op jit(solution)/shard_map/ppermute | solution.py:410
  2.6 1.1 %keep.1.kept_ref = f32[16,88,128]{2,1,0:T(8,128)S(1)} custom-call(s32[4,16]{1,0:T(4,128)} %bitcast.16, s32[4,16]{1,0:T(4,128)} %shifts_hbm.3, f32[2,4,2,16,128]{4,3,2,1,0:T(8,128)} %bitcast.14, bf16[4,2,4,2,16,128]{5,4,3,2,1,0:T(8,128)(2,1)} %bitcast.12), custom_call_target="tpu_custom_call" | custom-call | flops 1000000000 | bytes 4000000 | tf_op jit(solution)/shard_map/keep/pallas_call | solution.py:411
  3.7 0.0 copy-start
  3.7 0.0 copy-start.1
  3.7 0.2 collective-permute-done.other_ref
  4.0 20.8 %all_to_all.10.arrived_ref = f32[16,88,128]{2,1,0:T(8,128)S(1)} all-to-all(f32[16,88,128]{2,1,0:T(8,128)S(1)} %join.1), channel_id=1, replica_groups=mesh['gx'=8,'gy'=16] {'gy'}, dimensions={0} | all-to-all | bytes 1441792 | tf_op jit(solution)/shard_map/all_to_all | solution.py:378
  24.7 1.6 %collective-permute-start.1 = (f32[272,128]{1,0:T(8,128)S(1)}, f32[272,128]{1,0:T(8,128)S(1)}, u32[]{:S(2)}, u32[]{:S(2)}) collective-permute-start(f32[272,128]{1,0:T(8,128)S(1)} %lead.1.own_ref), channel_id=1, source_target_pairs={{0,16},{1,17},{2,18},{3,19},{4,20},{5,21},{6,22},{7,23},{8,24},{9,... | collective-permute-start | bytes 417800 | tf_op jit(solution)/shard_map/ppermute | solution.py:517
  26.3 1.2 %collective-permute-start.2 = (f32[272,128]{1,0:T(8,128)S(1)}, f32[272,128]{1,0:T(8,128)S(1)}, u32[]{:S(2)}, u32[]{:S(2)}) collective-permute-start(f32[272,128]{1,0:T(8,128)S(1)} %lead.1.own_ref), channel_id=1, source_target_pairs={{20,5},{21,6},{22,7},{23,3},{19,2},{18,1},{17,0},{16,32},{48,33},{... | collective-permute-start | bytes 417800 | tf_op jit(solution)/shard_map/ppermute | solution.py:516
  27.5 0.0 copy-done
  27.5 0.0 copy-done.1
  27.5 1.2 %taps.1 = (bf16[4,2,512,256]{3,2,1,0:T(8,128)(2,1)S(1)}, bf16[4,32,32]{2,1,0:T(8,128)(2,1)S(1)}, bf16[4,32,64]{2,1,0:T(8,128)(2,1)S(1)}, bf16[4,32,32]{2,1,0:T(8,128)(2,1)S(1)}, bf16[4,64,32]{2,1,0:T(8,128)(2,1)S(1)}) custom-call(f32[4,31]{1,0:T(4,128)S(1)} %copy-done, f32[4,31]{1,0:T(4,128)S(1)} %copy-done.1), custom_call_target="tpu_custom_call" | custom-call | tf_op jit(solution)/shard_map/taps/pallas_call | solution.py:431
  28.7 0.0 collective-permute-done.1.swapped_ref
  28.8 1.5 %front.2.near_ref = f32[4,16,2048]{2,1,0:T(8,128)S(1)} custom-call(s32[32,16]{1,0:T(8,128)S(1)} %maximum_convert_fusion.meta_ref, f32[272,128]{1,0:T(8,128)S(1)} %lead.1.own_ref, f32[272,128]{1,0:T(8,128)S(1)} %collective-permute-done.1.swapped_ref, bf16[4,32,64]{2,1,0:T(8,128)(2,1)S(1)} %get-tuple-element.18.near_in_ref), custom_call_target="tpu_custom_call" | custom-call | tf_op jit(solution)/shard_map/front/pallas_call | solution.py:522
  30.3 0.5 collective-permute-done.2.paired_ref
  30.8 2.1 %middle.2 = (f32[256,128]{1,0:T(8,128)S(1)}, f32[4,256,128]{2,1,0:T(8,128)S(1)}) custom-call(s32[16,16]{1,0:T(8,128)S(1)} %fusion.2.meta_ref, f32[272,128]{1,0:T(8,128)S(1)} %collective-permute-done.2.paired_ref, f32[4,16,2048]{2,1,0:T(8,128)S(1)} %front.2.near_ref, f32[16,88,128]{2,1,0:T(8,128)S(1)} %all_to_all.10.arrived_ref, ...), custom_call_target="tpu_custom_call" | custom-call | flops 1000000000 | bytes 4000000 | tf_op jit(solution)/shard_map/middle/pallas_call | solution.py:525
  32.9 1.3 %collective-permute-start.3 = (f32[256,128]{1,0:T(8,128)S(1)}, f32[256,128]{1,0:T(8,128)S(1)}, u32[]{:S(2)}, u32[]{:S(2)}) collective-permute-start(f32[256,128]{1,0:T(8,128)S(1)} %get-tuple-element.25), channel_id=1, source_target_pairs={{20,5},{21,6},{22,7},{23,3},{19,2},{18,1},{17,0},{16,32},{48,33},{... | collective-permute-start | bytes 393224 | tf_op jit(solution)/shard_map/ppermute | solution.py:528
  34.1 1.4 %tail.2 = (f32[256,128]{1,0:T(8,128)S(1)}, f32[256,128]{1,0:T(8,128)S(1)}) custom-call(s32[32,16]{1,0:T(8,128)S(1)} %maximum_convert_fusion.meta_ref, f32[4,256,128]{2,1,0:T(8,128)S(1)} %get-tuple-element.22.again_ref, bf16[4,64,32]{2,1,0:T(8,128)(2,1)S(1)} %get-tuple-element.23.near_back_ref), custom_call_target="tpu_custom_call" | custom-call | flops 1000000000 | bytes 4000000 | tf_op jit(solution)/shard_map/tail/pallas_call | solution.py:526
  35.5 0.1 collective-permute-start.4
  35.6 1.7 %collective-permute-done.3.paired_ref = f32[256,128]{1,0:T(8,128)S(1)} collective-permute-done((f32[256,128]{1,0:T(8,128)S(1)}, f32[256,128]{1,0:T(8,128)S(1)}, u32[]{:S(2)}, u32[]{:S(2)}) %collective-permute-start.3) | collective-permute-done | bytes 131104 | tf_op jit(solution)/shard_map/ppermute | solution.py:528
  37.4 0.0 collective-permute-done.4.swapped_ref
  37.4 0.2 collective-permute-start.6
  37.6 1.5 %collective-permute-start.5 = (f32[256,128]{1,0:T(8,128)S(1)}, f32[256,128]{1,0:T(8,128)S(1)}, u32[]{:S(2)}, u32[]{:S(2)}) collective-permute-start(f32[256,128]{1,0:T(8,128)S(1)} %update.1.own_ref), channel_id=1, source_target_pairs={{20,5},{21,6},{22,7},{23,3},{19,2},{18,1},{17,0},{16,32},{48,33},{... | collective-permute-start | bytes 393224 | tf_op jit(solution)/shard_map/ppermute | solution.py:516
  39.1 0.0 collective-permute-done.6.swapped_ref
  39.1 1.5 %front.3.near_ref = f32[4,16,2048]{2,1,0:T(8,128)S(1)} custom-call(s32[32,16]{1,0:T(8,128)S(1)} %maximum_convert_fusion.meta_ref, f32[256,128]{1,0:T(8,128)S(1)} %update.1.own_ref, f32[256,128]{1,0:T(8,128)S(1)} %collective-permute-done.6.swapped_ref, bf16[4,32,64]{2,1,0:T(8,128)(2,1)S(1)} %get-tuple-element.18.near_in_ref), custom_call_target="tpu_custom_call" | custom-call | tf_op jit(solution)/shard_map/front/pallas_call | solution.py:522
  40.6 1.4 %collective-permute-done.5.paired_ref = f32[256,128]{1,0:T(8,128)S(1)} collective-permute-done((f32[256,128]{1,0:T(8,128)S(1)}, f32[256,128]{1,0:T(8,128)S(1)}, u32[]{:S(2)}, u32[]{:S(2)}) %collective-permute-start.5) | collective-permute-done | bytes 131104 | tf_op jit(solution)/shard_map/ppermute | solution.py:516
  42.0 2.1 %middle.3 = (f32[256,128]{1,0:T(8,128)S(1)}, f32[4,256,128]{2,1,0:T(8,128)S(1)}) custom-call(s32[16,16]{1,0:T(8,128)S(1)} %fusion.2.meta_ref, f32[256,128]{1,0:T(8,128)S(1)} %collective-permute-done.5.paired_ref, f32[4,16,2048]{2,1,0:T(8,128)S(1)} %front.3.near_ref, f32[16,88,128]{2,1,0:T(8,128)S(1)} %all_to_all.10.arrived_ref, ...), custom_call_target="tpu_custom_call" | custom-call | flops 1000000000 | bytes 4000000 | tf_op jit(solution)/shard_map/middle/pallas_call | solution.py:525
  44.1 1.6 %collective-permute-start.7 = (f32[256,128]{1,0:T(8,128)S(1)}, f32[256,128]{1,0:T(8,128)S(1)}, u32[]{:S(2)}, u32[]{:S(2)}) collective-permute-start(f32[256,128]{1,0:T(8,128)S(1)} %get-tuple-element.29), channel_id=1, source_target_pairs={{20,5},{21,6},{22,7},{23,3},{19,2},{18,1},{17,0},{16,32},{48,33},{... | collective-permute-start | bytes 393224 | tf_op jit(solution)/shard_map/ppermute | solution.py:528
  45.7 1.4 %tail.3 = (f32[256,128]{1,0:T(8,128)S(1)}, f32[256,128]{1,0:T(8,128)S(1)}) custom-call(s32[32,16]{1,0:T(8,128)S(1)} %maximum_convert_fusion.meta_ref, f32[4,256,128]{2,1,0:T(8,128)S(1)} %get-tuple-element.27.again_ref, bf16[4,64,32]{2,1,0:T(8,128)(2,1)S(1)} %get-tuple-element.23.near_back_ref), custom_call_target="tpu_custom_call" | custom-call | flops 1000000000 | bytes 4000000 | tf_op jit(solution)/shard_map/tail/pallas_call | solution.py:526
  47.1 0.1 collective-permute-start.8
  47.2 1.4 %collective-permute-done.7.paired_ref = f32[256,128]{1,0:T(8,128)S(1)} collective-permute-done((f32[256,128]{1,0:T(8,128)S(1)}, f32[256,128]{1,0:T(8,128)S(1)}, u32[]{:S(2)}, u32[]{:S(2)}) %collective-permute-start.7) | collective-permute-done | bytes 131104 | tf_op jit(solution)/shard_map/ppermute | solution.py:528
  48.6 0.0 collective-permute-done.8.swapped_ref
  48.6 12.8 %all_to_all.11.home_ref = f32[32,16,128]{2,1,0:T(8,128)S(1)} all-to-all(f32[32,16,128]{2,1,0:T(8,128)S(1)} %bitcast.10), channel_id=1, replica_groups={{0,1,2,3,4,5,6,7,8,9,10,11,12,13,14,15,16,17,18,19,20,21,22,23,24,25,26..., dimensions={0} | all-to-all | bytes 524288 | tf_op jit(solution)/shard_map/all_to_all | solution.py:531
  61.4 0.7 %unpack.1 = f32[2,128,128]{2,1,0:T(8,128)} custom-call(f32[32,16,128]{2,1,0:T(8,128)S(1)} %all_to_all.11.home_ref), custom_call_target="tpu_custom_call" | custom-call | tf_op jit(solution)/shard_map/unpack/pallas_call | solution.py:534
  (10 shorter events, 0.2 us)
Async XLA Ops:
  1.1 2.8 %collective-permute-start = (f32[8,88,128]{2,1,0:T(8,128)S(1)}, f32[8,88,128]{2,1,0:T(8,128)S(1)}, u32[]{:S(2)}, u32[]{:S(2)}) collective-permute-start(f32[8,88,128]{2,1,0:T(8,128)S(1)} %send.1), channel_id=1, source_target_pairs={{0,16},{1,17},{2,18},{3,19},{4,20},{5,21},{6,22},{7,23},{8,24},{9,... | collective-permute-start | bytes 1081352 | tf_op jit(solution)/shard_map/ppermute | solution.py:410
  3.7 23.8 %copy-start = (f32[4,31]{1,0:T(4,128)S(1)}, f32[4,31]{1,0:T(4,128)}, u32[]{:S(2)}) copy-start(f32[4,31]{1,0:T(4,128)} %psf_rows_ref.1) | copy-start | bytes 1492
  3.7 23.8 %copy-start.1 = (f32[4,31]{1,0:T(4,128)S(1)}, f32[4,31]{1,0:T(4,128)}, u32[]{:S(2)}) copy-start(f32[4,31]{1,0:T(4,128)} %psf_cols_ref.1) | copy-start | bytes 1492
  24.7 4.0 %collective-permute-start.1 = (f32[272,128]{1,0:T(8,128)S(1)}, f32[272,128]{1,0:T(8,128)S(1)}, u32[]{:S(2)}, u32[]{:S(2)}) collective-permute-start(f32[272,128]{1,0:T(8,128)S(1)} %lead.1.own_ref), channel_id=1, source_target_pairs={{0,16},{1,17},{2,18},{3,19},{4,20},{5,21},{6,22},{7,23},{8,24},{9,... | collective-permute-start | bytes 417800 | tf_op jit(solution)/shard_map/ppermute | solution.py:517
  26.3 4.5 %collective-permute-start.2 = (f32[272,128]{1,0:T(8,128)S(1)}, f32[272,128]{1,0:T(8,128)S(1)}, u32[]{:S(2)}, u32[]{:S(2)}) collective-permute-start(f32[272,128]{1,0:T(8,128)S(1)} %lead.1.own_ref), channel_id=1, source_target_pairs={{20,5},{21,6},{22,7},{23,3},{19,2},{18,1},{17,0},{16,32},{48,33},{... | collective-permute-start | bytes 417800 | tf_op jit(solution)/shard_map/ppermute | solution.py:516
  32.9 4.5 %collective-permute-start.3 = (f32[256,128]{1,0:T(8,128)S(1)}, f32[256,128]{1,0:T(8,128)S(1)}, u32[]{:S(2)}, u32[]{:S(2)}) collective-permute-start(f32[256,128]{1,0:T(8,128)S(1)} %get-tuple-element.25), channel_id=1, source_target_pairs={{20,5},{21,6},{22,7},{23,3},{19,2},{18,1},{17,0},{16,32},{48,33},{... | collective-permute-start | bytes 393224 | tf_op jit(solution)/shard_map/ppermute | solution.py:528
  35.5 1.8 %collective-permute-start.4 = (f32[256,128]{1,0:T(8,128)S(1)}, f32[256,128]{1,0:T(8,128)S(1)}, u32[]{:S(2)}, u32[]{:S(2)}) collective-permute-start(f32[256,128]{1,0:T(8,128)S(1)} %get-tuple-element.26), channel_id=1, source_target_pairs={{0,16},{1,17},{2,18},{3,19},{4,20},{5,21},{6,22},{7,23},{8,24},{9,... | collective-permute-start | bytes 393224 | tf_op jit(solution)/shard_map/ppermute | solution.py:528
  37.4 1.7 %collective-permute-start.6 = (f32[256,128]{1,0:T(8,128)S(1)}, f32[256,128]{1,0:T(8,128)S(1)}, u32[]{:S(2)}, u32[]{:S(2)}) collective-permute-start(f32[256,128]{1,0:T(8,128)S(1)} %update.1.own_ref), channel_id=1, source_target_pairs={{0,16},{1,17},{2,18},{3,19},{4,20},{5,21},{6,22},{7,23},{8,24},{9,... | collective-permute-start | bytes 393224 | tf_op jit(solution)/shard_map/ppermute | solution.py:517
  37.6 4.4 %collective-permute-start.5 = (f32[256,128]{1,0:T(8,128)S(1)}, f32[256,128]{1,0:T(8,128)S(1)}, u32[]{:S(2)}, u32[]{:S(2)}) collective-permute-start(f32[256,128]{1,0:T(8,128)S(1)} %update.1.own_ref), channel_id=1, source_target_pairs={{20,5},{21,6},{22,7},{23,3},{19,2},{18,1},{17,0},{16,32},{48,33},{... | collective-permute-start | bytes 393224 | tf_op jit(solution)/shard_map/ppermute | solution.py:516
  44.1 4.5 %collective-permute-start.7 = (f32[256,128]{1,0:T(8,128)S(1)}, f32[256,128]{1,0:T(8,128)S(1)}, u32[]{:S(2)}, u32[]{:S(2)}) collective-permute-start(f32[256,128]{1,0:T(8,128)S(1)} %get-tuple-element.29), channel_id=1, source_target_pairs={{20,5},{21,6},{22,7},{23,3},{19,2},{18,1},{17,0},{16,32},{48,33},{... | collective-permute-start | bytes 393224 | tf_op jit(solution)/shard_map/ppermute | solution.py:528
  47.1 1.5 %collective-permute-start.8 = (f32[256,128]{1,0:T(8,128)S(1)}, f32[256,128]{1,0:T(8,128)S(1)}, u32[]{:S(2)}, u32[]{:S(2)}) collective-permute-start(f32[256,128]{1,0:T(8,128)S(1)} %get-tuple-element.30), channel_id=1, source_target_pairs={{0,16},{1,17},{2,18},{3,19},{4,20},{5,21},{6,22},{7,23},{8,24},{9,... | collective-permute-start | bytes 393224 | tf_op jit(solution)/shard_map/ppermute | solution.py:528
